TPU v7x, 32 devices: a whole 2x2x4 slice. The times are simulated.
32 devices in a mesh: section: 2 (over core), dp: 8 (over z, y), tensor: 2 (over x).
Axes of the slice: x: 2, y: 2, z: 4, core: 2. Of those that a mesh axis runs over, the one named last changes fastest.
Arguments:
- layer_inputs: bfloat16 [2, 16, 512, 1024], P('section', 'dp', None, 'tensor'), may hold values from -6 to 6
- output_cotangents: bfloat16 [2, 16, 512, 1024], P('section', 'dp', None, 'tensor'), may hold values from -6 to 6
- segment_ids: int32 [2, 16, 512], P(None, 'dp'), may hold values from 0 to 3, never falling along the last dimension, each value on 1 to 256 neighbouring positions
- attention_in: bfloat16 [2, 1024, 3, 1024], P('section', None, None, 'tensor'), may hold values from -0.1875 to 0.1875
- attention_out: bfloat16 [2, 1024, 1024], P('section', 'tensor'), may hold values from -1.5 to 1.5
- cross_weights: bfloat16 [2, 1024, 2, 1024], P('section', None, None, 'tensor'), may hold values from -0.875 to 0.875
- expand_weights: bfloat16 [2, 1024, 4096], P('section', None, 'tensor'), may hold values from -0.1875 to 0.1875
- contract_weights: bfloat16 [2, 4096, 1024], P('section', 'tensor'), may hold values from -0.125 to 0.125
- norm_gains: float32 [2, 3, 1024], P('section', None, 'tensor'), may hold values from 0.25 to 1.75
- bias_tables: float32 [2, 32, 16], P('section', None, 'tensor'), may hold values from -1.5 to 1.5
Outputs:
- layer_outputs: float32 [2, 16, 512, 1024], P('section', 'dp', None, 'tensor')
- input_gradient: float32 [2, 16, 512, 1024], P('section', 'dp', None, 'tensor')
- attention_in_gradient: float32 [2, 1024, 3, 1024], P('section', None, None, 'tensor')
- attention_out_gradient: float32 [2, 1024, 1024], P('section', 'tensor')
- cross_gradient: float32 [2, 1024, 2, 1024], P('section', None, None, 'tensor')
- expand_gradient: float32 [2, 1024, 4096], P('section', None, 'tensor')
- contract_gradient: float32 [2, 4096, 1024], P('section', 'tensor')
- gains_gradient: float32 [2, 3, 1024], P('section', None, 'tensor')
- bias_gradient: float32 [2, 32, 16], P('section', None, 'tensor')
Inputs may be any that keep to these rules, and one draw needn't show every extreme that they name: `segment_ids`: in each row the numbers never fall and every number of 0 to 3 occurs.
All inputs are finite; a program needn't handle non-finite values.
Results may differ from a plain program's by a relative error of at most 0.025.
Values may be sent and summed in bfloat16 or wider, within the bound.
No kernel may reach another device: no remote copies, remote signals or barrier semaphores. Data moves between devices by JAX's collectives and lax.ppermute only.
A program may use at most 256 MiB of HBM per device.

v0:
```python
import jax
import jax.numpy as jnp
import numpy as np
from jax import lax
from jax.sharding import PartitionSpec as P

D = 1024
HEAD = 64
BUCKETS = 32
MAXDIST = 128


epsilon = 1e-06
masked_score = -1e30
highest = lax.Precision.HIGHEST


def shifted(block, axis, distance):
    devices = range(lax.axis_size(axis))
    route = [(i - distance, i) for i in devices if i - distance in devices]
    return lax.ppermute(block, axis, route)


def bucket_matrix(length, causal):
    count = BUCKETS if causal else BUCKETS // 2
    exact = count // 2
    distance = np.arange(length)
    spread = exact + (
        np.log(np.maximum(distance, 1) / exact) / np.log(MAXDIST / exact) * (count - exact)
    ).astype(np.int64)
    levels = np.where(distance < exact, distance, np.minimum(spread, count - 1))
    breaks = [
        int(np.argmax(levels >= level))
        for level in range(1, count)
        if bool((levels >= level).any())
    ]
    offset = (
        jnp.arange(length, dtype=jnp.int32)[None, :] - jnp.arange(length, dtype=jnp.int32)[:, None]
    )
    if causal:
        reach = jnp.maximum(-offset, 0)
        bucket = jnp.zeros((length, length), jnp.int32)
    else:
        reach = jnp.abs(offset)
        bucket = jnp.where(offset > 0, count, 0).astype(jnp.int32)
    for edge in breaks:
        bucket = bucket + (reach >= edge).astype(jnp.int32)
    return bucket


def onehot_table(length, causal):
    bucket = bucket_matrix(length, causal)
    labels = jnp.arange(BUCKETS, dtype=jnp.int32)
    return (bucket[:, :, None] == labels).astype(jnp.float32).reshape(length * length, BUCKETS)


def smooth(values):
    return jax.nn.gelu(values, approximate=True)


def feature_sum(partial_value):
    return lax.psum_scatter(
        partial_value.astype(jnp.bfloat16), "tensor", scatter_dimension=1, tiled=True
    ).astype(jnp.float32)


def feature_gather(local):
    return lax.all_gather(local, "tensor", axis=1, tiled=True)


def token_totals(values):
    return lax.psum(values, "tensor")


def norm_forward(hidden, gain):
    inverse = lax.rsqrt(token_totals(jnp.sum(hidden * hidden, axis=1)) / D + epsilon)
    scaled = (hidden * inverse[:, None] * gain).astype(jnp.bfloat16)
    return (feature_gather(scaled), inverse)


def norm_backward(hidden, gain, inverse, partial_value):
    upstream = feature_sum(partial_value)
    gain_grad = jnp.sum(upstream * hidden * inverse[:, None], axis=0)
    scaled = upstream * gain
    inner = token_totals(jnp.sum(scaled * hidden, axis=1))
    result = inverse[:, None] * scaled - hidden * (inverse * inverse * inverse * inner / D)[:, None]
    return (result, gain_grad)


def score_block(query, keys, bias, allowed):
    scores = (
        jnp.einsum("qhe,khe->hqk", query, keys, preferred_element_type=jnp.float32) * HEAD ** (-0.5)
        + bias
    )
    return jnp.where(allowed[None], scores, masked_score)


def attend_rows(query, keys, values, bias, allowed):

    def one_row(item):
        row_query, row_keys, row_values, row_allowed = item
        scores = score_block(row_query, row_keys, bias, row_allowed)
        peak = jnp.max(scores, axis=2, keepdims=True)
        exponent = jnp.exp(scores - peak)
        total = jnp.sum(exponent, axis=2, keepdims=True)
        weights = (exponent / total).astype(jnp.bfloat16)
        mixed = jnp.einsum("hqk,khe->qhe", weights, row_values, preferred_element_type=jnp.float32)
        return (mixed.astype(jnp.bfloat16), peak[:, :, 0] + jnp.log(total[:, :, 0]))

    return lax.map(one_row, (query, keys, values, allowed))


def attend_back(query, keys, values, bias, allowed, logsum, upstream, with_bias):
    scale = HEAD ** (-0.5)

    def one_row(carry, item):
        row_query, row_keys, row_values, row_allowed, row_logsum, row_up = item
        scores = score_block(row_query, row_keys, bias, row_allowed)
        weights = jnp.exp(scores - row_logsum[:, :, None])
        dots = jnp.einsum("qhe,khe->hqk", row_up, row_values, preferred_element_type=jnp.float32)
        inner = jnp.sum(weights * dots, axis=2, keepdims=True)
        score_grad = (weights * (dots - inner)).astype(jnp.bfloat16)
        query_grad = (
            jnp.einsum("hqk,khe->qhe", score_grad, row_keys, preferred_element_type=jnp.float32)
            * scale
        )
        key_grad = (
            jnp.einsum("hqk,qhe->khe", score_grad, row_query, preferred_element_type=jnp.float32)
            * scale
        )
        value_grad = jnp.einsum(
            "hqk,qhe->khe", weights.astype(jnp.bfloat16), row_up, preferred_element_type=jnp.float32
        )
        if with_bias:
            carry = carry + score_grad.astype(jnp.float32)
        return (carry, (query_grad, key_grad, value_grad))

    if with_bias:
        start = jnp.zeros((query.shape[2], query.shape[1], keys.shape[1]), jnp.float32)
    else:
        start = jnp.zeros((1,), jnp.float32)
    bias_grad, (query_grad, key_grad, value_grad) = lax.scan(
        one_row, start, (query, keys, values, allowed, logsum, upstream)
    )
    return (query_grad, key_grad, value_grad, bias_grad)


def self_forward(hidden, gain, mixing, projecting, bias, allowed):
    rows, length = allowed.shape[:2]
    heads = projecting.shape[0] // HEAD
    normed, inverse = norm_forward(hidden, gain)
    projected = jnp.dot(normed, mixing, preferred_element_type=jnp.float32).astype(jnp.bfloat16)
    projected = projected.reshape(rows, length, 3, heads, HEAD)
    mixed, logsum = attend_rows(
        projected[:, :, 0], projected[:, :, 1], projected[:, :, 2], bias, allowed
    )
    flat = mixed.reshape(rows * length, heads * HEAD)
    result = hidden + feature_sum(jnp.dot(flat, projecting, preferred_element_type=jnp.float32))
    return (result, (normed, inverse, projected, logsum, flat))


def self_backward(hidden, gain, mixing, projecting, bias, allowed, kept, grad):
    normed, inverse, projected, logsum, flat = kept
    rows, length = allowed.shape[:2]
    heads = projecting.shape[0] // HEAD
    full = feature_gather(grad.astype(jnp.bfloat16))
    projecting_grad = jnp.einsum("tc,td->cd", flat, full, preferred_element_type=jnp.float32)
    flat_grad = jnp.einsum("td,cd->tc", full, projecting, preferred_element_type=jnp.float32)
    flat_grad = flat_grad.astype(jnp.bfloat16).reshape(rows, length, heads, HEAD)
    query_grad, key_grad, value_grad, bias_grad = attend_back(
        projected[:, :, 0],
        projected[:, :, 1],
        projected[:, :, 2],
        bias,
        allowed,
        logsum,
        flat_grad,
        True,
    )
    joined = (
        jnp.stack([query_grad, key_grad, value_grad], axis=2)
        .astype(jnp.bfloat16)
        .reshape(rows * length, -1)
    )
    mixing_grad = jnp.einsum("td,tc->dc", normed, joined, preferred_element_type=jnp.float32)
    partial_value = jnp.einsum("tc,dc->td", joined, mixing, preferred_element_type=jnp.float32)
    result, gain_grad = norm_backward(hidden, gain, inverse, partial_value)
    return (result + grad, mixing_grad, projecting_grad, gain_grad, bias_grad)


def dense_forward(hidden, gain, expanding, contracting):
    normed, inverse = norm_forward(hidden, gain)
    before = jnp.dot(normed, expanding, preferred_element_type=jnp.float32)
    activated = smooth(before).astype(jnp.bfloat16)
    result = hidden + feature_sum(
        jnp.dot(activated, contracting, preferred_element_type=jnp.float32)
    )
    return (result, (normed, inverse, before, activated))


def dense_backward(hidden, gain, expanding, contracting, kept, grad):
    normed, inverse, before, activated = kept
    full = feature_gather(grad.astype(jnp.bfloat16))
    contract_grad = jnp.einsum("tf,td->fd", activated, full, preferred_element_type=jnp.float32)
    upward = jnp.einsum("td,fd->tf", full, contracting, preferred_element_type=jnp.float32)
    again, smooth_back = jax.vjp(smooth, before)
    before_grad = smooth_back(upward)[0].astype(jnp.bfloat16)
    expand_grad = jnp.einsum("td,tf->df", normed, before_grad, preferred_element_type=jnp.float32)
    partial_value = jnp.einsum(
        "tf,df->td", before_grad, expanding, preferred_element_type=jnp.float32
    )
    result, gain_grad = norm_backward(hidden, gain, inverse, partial_value)
    return (result + grad, expand_grad, contract_grad, gain_grad)


def layer_bias(table, length, causal):
    onehot = onehot_table(length, causal)
    bias = jnp.dot(onehot, table, precision=highest, preferred_element_type=jnp.float32)
    return (onehot, bias.reshape(length, length, -1).transpose(2, 0, 1))


def encoder_pass(hidden, segments, weights, bias):
    mixing, projecting, crossing, expanding, contracting, gains = weights
    allowed = segments[:, :, None] == segments[:, None, :]
    after_attention, attention_kept = self_forward(
        hidden, gains[0], mixing, projecting, bias, allowed
    )
    layer_out, dense_kept = dense_forward(after_attention, gains[1], expanding, contracting)
    normed_out, inverse = norm_forward(layer_out, gains[2])
    return (layer_out, normed_out, (allowed, after_attention, attention_kept, dense_kept, inverse))


def encoder_backward(hidden, segments, weights, onehot, bias, memory_grad, outer_grad):
    mixing, projecting, crossing, expanding, contracting, gains = weights
    layer_out, normed_out, kept = encoder_pass(hidden, segments, weights, bias)
    allowed, after_attention, attention_kept, dense_kept, inverse = kept
    cross_flat = crossing.reshape(crossing.shape[0], -1)
    cross_grad = jnp.einsum(
        "td,tc->dc", normed_out, memory_grad, preferred_element_type=jnp.float32
    )
    partial_value = jnp.einsum(
        "tc,dc->td", memory_grad, cross_flat, preferred_element_type=jnp.float32
    )
    result, gain_out = norm_backward(layer_out, gains[2], inverse, partial_value)
    grad_out = result + outer_grad
    grad_mid, expand_grad, contract_grad, gain_dense = dense_backward(
        after_attention, gains[1], expanding, contracting, dense_kept, grad_out
    )
    grad_in, mixing_grad, projecting_grad, gain_self, bias_grad = self_backward(
        hidden, gains[0], mixing, projecting, bias, allowed, attention_kept, grad_mid
    )
    heads = bias_grad.shape[0]
    table_grad = jnp.einsum(
        "pb,ph->bh", onehot, bias_grad.transpose(1, 2, 0).reshape(-1, heads), precision=highest
    )
    parts = (
        mixing_grad.reshape(mixing.shape[0], 3, -1),
        projecting_grad,
        cross_grad.reshape(crossing.shape),
        expand_grad,
        contract_grad,
        jnp.stack([gain_self, gain_dense, gain_out]),
        table_grad,
    )
    return (grad_in, parts)


def decoder_step(hidden, own_ids, memory_ids, weights, onehot, bias, memory, outer_grad):
    mixing, projecting, crossing, expanding, contracting, gains = weights
    rows, length = own_ids.shape
    heads = projecting.shape[0] // HEAD
    order = jnp.arange(length, dtype=jnp.int32)
    allowed = (own_ids[:, :, None] == own_ids[:, None, :]) & (order[None, :] <= order[:, None])[
        None
    ]
    after_self, self_kept = self_forward(hidden, gains[0], mixing, projecting, bias, allowed)
    normed, inverse = norm_forward(after_self, gains[1])
    query = jnp.dot(normed, crossing[:, 0, :], preferred_element_type=jnp.float32).astype(
        jnp.bfloat16
    )
    query = query.reshape(rows, length, heads, HEAD)
    stored = memory.reshape(rows, length, 2, heads, HEAD)
    cross_allowed = own_ids[:, :, None] == memory_ids[:, None, :]
    mixed, logsum = attend_rows(query, stored[:, :, 0], stored[:, :, 1], 0.0, cross_allowed)
    mixed_flat = mixed.reshape(rows * length, heads * HEAD)
    cross_term = jnp.einsum(
        "tc,dc->td", mixed_flat, crossing[:, 1, :], preferred_element_type=jnp.float32
    )
    after_cross = after_self + feature_sum(cross_term)
    layer_out, dense_kept = dense_forward(after_cross, gains[2], expanding, contracting)
    grad_cross, expand_grad, contract_grad, gain_dense = dense_backward(
        after_cross, gains[2], expanding, contracting, dense_kept, outer_grad
    )
    full = feature_gather(grad_cross.astype(jnp.bfloat16))
    cross_out_grad = jnp.einsum("td,tc->dc", full, mixed_flat, preferred_element_type=jnp.float32)
    mixed_grad = jnp.einsum(
        "td,dc->tc", full, crossing[:, 1, :], preferred_element_type=jnp.float32
    )
    mixed_grad = mixed_grad.astype(jnp.bfloat16).reshape(rows, length, heads, HEAD)
    query_grad, key_grad, value_grad, unused = attend_back(
        query, stored[:, :, 0], stored[:, :, 1], 0.0, cross_allowed, logsum, mixed_grad, False
    )
    query_low = query_grad.astype(jnp.bfloat16).reshape(rows * length, -1)
    cross_in_grad = jnp.einsum("td,tc->dc", normed, query_low, preferred_element_type=jnp.float32)
    partial_value = jnp.einsum(
        "tc,dc->td", query_low, crossing[:, 0, :], preferred_element_type=jnp.float32
    )
    result, gain_cross = norm_backward(after_self, gains[1], inverse, partial_value)
    grad_self = result + grad_cross
    grad_in, mixing_grad, projecting_grad, gain_self, bias_grad = self_backward(
        hidden, gains[0], mixing, projecting, bias, allowed, self_kept, grad_self
    )
    memory_grad = (
        jnp.stack([key_grad, value_grad], axis=2).astype(jnp.bfloat16).reshape(rows * length, -1)
    )
    table_grad = jnp.einsum(
        "pb,ph->bh", onehot, bias_grad.transpose(1, 2, 0).reshape(-1, heads), precision=highest
    )
    parts = (
        mixing_grad.reshape(mixing.shape[0], 3, -1),
        projecting_grad,
        jnp.stack([cross_in_grad, cross_out_grad], axis=1),
        expand_grad,
        contract_grad,
        jnp.stack([gain_self, gain_cross, gain_dense]),
        table_grad,
    )
    return (layer_out, grad_in, parts, memory_grad)


def body(
    layer_inputs,
    output_cotangents,
    segment_ids,
    attention_in,
    attention_out,
    cross_weights,
    expand_weights,
    contract_weights,
    norm_gains,
    bias_tables,
):
    section_rows = layer_inputs.shape[1]
    length = layer_inputs.shape[2]
    local_width = layer_inputs.shape[3]
    units = 1
    unit_rows = section_rows // units
    unit_tokens = unit_rows * length
    weights = (
        attention_in[0].reshape(attention_in.shape[1], -1),
        attention_out[0],
        cross_weights[0],
        expand_weights[0],
        contract_weights[0],
        norm_gains[0],
    )
    table = bias_tables[0]
    memory_width = 2 * cross_weights.shape[3]
    inputs = layer_inputs[0].astype(jnp.float32).reshape(section_rows * length, local_width)
    cotangents = (
        output_cotangents[0].astype(jnp.float32).reshape(section_rows * length, local_width)
    )
    is_encoder = lax.axis_index("section") == 0
    outputs = jnp.zeros((section_rows * length, local_width), jnp.float32)
    gradients = jnp.zeros((section_rows * length, local_width), jnp.float32)
    totals = (
        jnp.zeros(attention_in.shape[1:], jnp.float32),
        jnp.zeros(attention_out.shape[1:], jnp.float32),
        jnp.zeros(cross_weights.shape[1:], jnp.float32),
        jnp.zeros(expand_weights.shape[1:], jnp.float32),
        jnp.zeros(contract_weights.shape[1:], jnp.float32),
        jnp.zeros(norm_gains.shape[1:], jnp.float32),
        jnp.zeros(bias_tables.shape[1:], jnp.float32),
    )
    empty = jnp.zeros((unit_tokens, memory_width), jnp.bfloat16)
    received = empty
    returned = empty
    for tick in range(units + 2):
        state = (outputs, gradients, totals, received, returned)
        encoder_outputs, encoder_gradients, encoder_totals, encoder_received, encoder_returned = (
            state
        )
        send_forward = empty
        encoder_onehot, encoder_bias = layer_bias(table, length, False)
        if tick < units:
            encoder_first = tick * unit_tokens
            segments = segment_ids[0, tick * unit_rows : (tick + 1) * unit_rows]
            encoder_layer_out, normed_out, kept = encoder_pass(
                inputs, segments, weights, encoder_bias
            )
            cross_flat = weights[2].reshape(weights[2].shape[0], -1)
            send_forward = jnp.dot(
                normed_out, cross_flat, preferred_element_type=jnp.float32
            ).astype(jnp.bfloat16)
            encoder_outputs = encoder_outputs.at[encoder_first : encoder_first + unit_tokens].set(
                encoder_layer_out
            )
        if tick >= 2:
            encoder_unit = tick - 2
            encoder_first = encoder_unit * unit_tokens
            segments = segment_ids[0, encoder_unit * unit_rows : (encoder_unit + 1) * unit_rows]
            encoder_grad_in, encoder_parts = encoder_backward(
                inputs,
                segments,
                weights,
                encoder_onehot,
                encoder_bias,
                encoder_returned,
                cotangents,
            )
            encoder_gradients = encoder_gradients.at[
                encoder_first : encoder_first + unit_tokens
            ].set(encoder_grad_in)
            encoder_totals = jax.tree.map(jnp.add, encoder_totals, encoder_parts)
        encoder_state = (encoder_outputs, encoder_gradients, encoder_totals, send_forward, empty)
        decoder_outputs, decoder_gradients, decoder_totals, decoder_received, decoder_returned = (
            state
        )
        send_back = empty
        if 1 <= tick <= units:
            unit = tick - 1
            first = unit * unit_tokens
            onehot, bias = layer_bias(table, length, True)
            own_ids = segment_ids[1, unit * unit_rows : (unit + 1) * unit_rows]
            memory_ids = segment_ids[0, unit * unit_rows : (unit + 1) * unit_rows]
            layer_out, grad_in, parts, send_back = decoder_step(
                inputs, own_ids, memory_ids, weights, onehot, bias, decoder_received, cotangents
            )
            decoder_outputs = decoder_outputs.at[first : first + unit_tokens].set(layer_out)
            decoder_gradients = decoder_gradients.at[first : first + unit_tokens].set(grad_in)
            decoder_totals = jax.tree.map(jnp.add, decoder_totals, parts)
        decoder_state = (decoder_outputs, decoder_gradients, decoder_totals, empty, send_back)
        outputs, gradients, totals, send_forward, send_back = jax.tree.map(
            lambda first_value, second_value: jnp.where(is_encoder, first_value, second_value),
            encoder_state,
            decoder_state,
        )
        if tick < units:
            received = shifted(send_forward, "section", 1)
        if 1 <= tick <= units:
            returned = shifted(send_back, "section", -1)
    summed = (
        lax.psum(totals[0].astype(jnp.bfloat16), "dp").astype(jnp.float32),
        lax.psum(totals[1].astype(jnp.bfloat16), "dp").astype(jnp.float32),
        lax.psum(totals[2].astype(jnp.bfloat16), "dp").astype(jnp.float32),
        lax.psum(totals[3].astype(jnp.bfloat16), "dp").astype(jnp.float32),
        lax.psum(totals[4].astype(jnp.bfloat16), "dp").astype(jnp.float32),
        lax.psum(totals[5].astype(jnp.bfloat16), "dp").astype(jnp.float32),
        lax.psum(totals[6].astype(jnp.bfloat16), "dp").astype(jnp.float32),
    )
    layer_outputs = outputs.reshape(1, section_rows, length, local_width)
    input_gradient = gradients.reshape(1, section_rows, length, local_width)
    return (
        layer_outputs,
        input_gradient,
        summed[0][None],
        summed[1][None],
        summed[2][None],
        summed[3][None],
        summed[4][None],
        summed[5][None],
        summed[6][None],
    )


def solution(mesh):
    return jax.shard_map(
        body,
        mesh=mesh,
        in_specs=(
            P("section", "dp", None, "tensor"),
            P("section", "dp", None, "tensor"),
            P(None, "dp", None),
            P("section", None, None, "tensor"),
            P("section", "tensor", None),
            P("section", None, None, "tensor"),
            P("section", None, "tensor"),
            P("section", "tensor", None),
            P("section", None, "tensor"),
            P("section", None, "tensor"),
        ),
        out_specs=(
            P("section", "dp", None, "tensor"),
            P("section", "dp", None, "tensor"),
            P("section", None, None, "tensor"),
            P("section", "tensor", None),
            P("section", None, None, "tensor"),
            P("section", None, "tensor"),
            P("section", "tensor", None),
            P("section", None, "tensor"),
            P("section", None, "tensor"),
        ),
        check_vma=False,
    )
```

profile of v0, /device:TPU:1, one launch (start us, length us, event | category | flops | bytes accessed | tf_op | source)
XLA Modules:
  0.0 1716.8 jit_solution(18116386397803378750)
XLA Ops:
  23.4 12.1 fusion.225
  35.5 9.9 copy.70
  53.0 7.6 convolution_convert_fusion
  78.3 39.4 %while.102 = (s32[]{:T(128)}, bf16[2,512,8,64]{1,3,2,0:T(8,128)(2,1)}, bf16[2,512,8,64]{1,3,2,0:T(8,128)(2,1)}, pred[2,512,512]{1,2,0:T(8,128)(4,1)}, bf16[2,512...) while((s32[]{:T(128)}, ...), condition=%wide.region_5.6_spmd, body=%wide.region_2.5_spmd.sunk | while | flops 553915392 | bytes 78415992 | solution.py:110
  89.2 8.8 fusion.505
  108.9 8.8 fusion.505
  125.0 12.3 fusion.222
  137.4 10.0 copy.75
  164.8 21.0 %while.103 = (s32[]{:T(128)}, bf16[2,512,8,64]{1,3,2,0:T(8,128)(2,1)}, f32[2,8,512]{2,1,0:T(8,128)S(1)}, bf16[2,512,8,64]{1,3,2,0:T(8,128)(2,1)}, pred[2,512,512...) while((s32[]{:T(128)}, ...), condition=%wide.region_13.14_spmd, body=%wide.region_10.13_spmd.sunk | while | flops 556003328 | bytes 49154240 | solution.py:110
  193.1 21.1 %while.105 = (s32[]{:T(128)}, bf16[2,512,8,64]{1,3,2,0:T(8,128)(2,1)}, f32[2,8,512]{2,1,0:T(8,128)S(1)}, bf16[2,512,8,64]{1,3,2,0:T(8,128)(2,1)}, pred[2,512,512...) while((s32[]{:T(128)}, ...), condition=%wide.region_30.31_spmd, body=%wide.region_27.30_spmd.sunk | while | flops 556003328 | bytes 49154240 | solution.py:110
  234.9 32.3 %reduce-scatter.24.cloned.1.call-done = bf16[1024,512]{1,0:T(8,128)(2,1)} async-done(((bf16[1024,1024]{1,0:T(8,128)(2,1)}), bf16[1024,512]{1,0:T(8,128)(2,1)}) %reduce-scatter.24.cloned.1.call-update) | async-done | bytes 1048592 | tf_op jit(solution)/shard_map/reduce_scatter | solution.py:62
  267.2 34.6 %reduce-scatter.16.cloned.1.call-done = bf16[1024,512]{1,0:T(8,128)(2,1)} async-done(((bf16[1024,1024]{1,0:T(8,128)(2,1)}), bf16[1024,512]{1,0:T(8,128)(2,1)}) %reduce-scatter.16.cloned.1.call-update) | async-done | bytes 1048592 | tf_op jit(solution)/shard_map/reduce_scatter | solution.py:62
  316.4 30.8 %all-gather.17.cloned.1.call-done = bf16[1024,1024]{1,0:T(8,128)(2,1)} async-done(((bf16[1024,512]{1,0:T(8,128)(2,1)}), bf16[1024,1024]{1,0:T(8,128)(2,1)}) %all-gather.17.cloned.1.call-update) | async-done | bytes 2097168 | tf_op jit(solution)/shard_map/all_gather | solution.py:68
  358.2 24.3 %all-gather.19.cloned.1.call-done = bf16[1024,1024]{1,0:T(8,128)(2,1)} async-done(((bf16[1024,512]{1,0:T(8,128)(2,1)}), bf16[1024,1024]{1,0:T(8,128)(2,1)}) %all-gather.19.cloned.1.call-update) | async-done | bytes 2097168 | tf_op jit(solution)/shard_map/all_gather | solution.py:68
  404.8 17.5 %while.104 = (s32[]{:T(128)}, bf16[2,512,8,64]{1,3,2,0:T(8,128)(2,1)}, f32[2,8,512]{2,1,0:T(8,128)S(1)}, bf16[2,512,8,64]{1,3,2,0:T(8,128)(2,1)}, pred[2,512,512...) while((s32[]{:T(128)}, ...), condition=%wide.region_22.23_spmd, body=%wide.region_19.22_spmd.sunk | while | flops 562294784 | bytes 41289912 | solution.py:110
  428.7 31.9 %reduce-scatter.20.cloned.1.call-done = bf16[1024,512]{1,0:T(8,128)(2,1)} async-done(((bf16[1024,1024]{1,0:T(8,128)(2,1)}), bf16[1024,512]{1,0:T(8,128)(2,1)}) %reduce-scatter.20.cloned.1.call-update) | async-done | bytes 1048592 | tf_op jit(solution)/shard_map/reduce_scatter | solution.py:62
  472.2 33.0 %all-gather.21.cloned.1.call-done = bf16[1024,1024]{1,0:T(8,128)(2,1)} async-done(((bf16[1024,512]{1,0:T(8,128)(2,1)}), bf16[1024,1024]{1,0:T(8,128)(2,1)}) %all-gather.21.cloned.1.call-update) | async-done | bytes 2097168 | tf_op jit(solution)/shard_map/all_gather | solution.py:68
  505.3 10.9 fusion.214
  516.2 23.9 %all-gather.25.cloned.1.call-done = bf16[1024,1024]{1,0:T(8,128)(2,1)} async-done(((bf16[1024,512]{1,0:T(8,128)(2,1)}), bf16[1024,1024]{1,0:T(8,128)(2,1)}) %all-gather.25.cloned.1.call-update) | async-done | bytes 2097168 | tf_op jit(solution)/shard_map/all_gather | solution.py:68
  540.1 12.6 fusion.176
  560.7 14.5 all-gather.23.cloned.1.call-done
  592.2 17.8 %reduce-scatter.28.cloned.1.call-done = bf16[1024,512]{1,0:T(8,128)(2,1)} async-done(((bf16[1024,1024]{1,0:T(8,128)(2,1)}), bf16[1024,512]{1,0:T(8,128)(2,1)}) %reduce-scatter.28.cloned.1.call-update) | async-done | bytes 1048592 | tf_op jit(solution)/shard_map/reduce_scatter | solution.py:62
  610.0 34.5 %reduce-scatter.26.cloned.1.call-done = bf16[1024,512]{1,0:T(8,128)(2,1)} async-done(((bf16[1024,1024]{1,0:T(8,128)(2,1)}), bf16[1024,512]{1,0:T(8,128)(2,1)}) %reduce-scatter.26.cloned.1.call-update) | async-done | bytes 1048592 | tf_op jit(solution)/shard_map/reduce_scatter | solution.py:62
  658.3 34.0 %all-gather.27.cloned.1.call-done = bf16[1024,1024]{1,0:T(8,128)(2,1)} async-done(((bf16[1024,512]{1,0:T(8,128)(2,1)}), bf16[1024,1024]{1,0:T(8,128)(2,1)}) %all-gather.27.cloned.1.call-update) | async-done | bytes 2097168 | tf_op jit(solution)/shard_map/all_gather | solution.py:68
  706.7 30.0 %while.106 = (s32[]{:T(128)}, bf16[2,512,8,64]{1,3,2,0:T(8,128)(2,1)}, bf16[2,512,8,64]{1,3,2,0:T(8,128)(2,1)}, bf16[2,512,8,64]{1,3,2,0:T(8,128)(2,1)}, bf16[2,...) while((s32[]{:T(128)}, ...), condition=%wide.region_42.43_spmd, body=%wide.region_40.42_spmd.sunk | while | flops 1374154752 | bytes 108909960 | solution.py:142
  753.0 31.6 %reduce-scatter.30.cloned.1.call-done = bf16[1024,512]{1,0:T(8,128)(2,1)} async-done(((bf16[1024,1024]{1,0:T(8,128)(2,1)}), bf16[1024,512]{1,0:T(8,128)(2,1)}) %reduce-scatter.30.cloned.1.call-update) | async-done | bytes 1048592 | tf_op jit(solution)/shard_map/reduce_scatter | solution.py:62
  802.7 28.0 %all-gather.29.cloned.1.call-done = bf16[1024,1024]{1,0:T(8,128)(2,1)} async-done(((bf16[1024,512]{1,0:T(8,128)(2,1)}), bf16[1024,1024]{1,0:T(8,128)(2,1)}) %all-gather.29.cloned.1.call-update) | async-done | bytes 2097168 | tf_op jit(solution)/shard_map/all_gather | solution.py:68
  830.7 12.8 fusion.183
  851.4 11.1 fusion.289
  863.7 13.4 fusion.378
  877.1 22.9 %reduce-scatter.32.cloned.1.call-done = bf16[1024,512]{1,0:T(8,128)(2,1)} async-done(((bf16[1024,1024]{1,0:T(8,128)(2,1)}), bf16[1024,512]{1,0:T(8,128)(2,1)}) %reduce-scatter.32.cloned.1.call-update) | async-done | bytes 1048592 | tf_op jit(solution)/shard_map/reduce_scatter | solution.py:62
  908.0 26.5 %reduce-scatter.22.cloned.1.call-done = bf16[1024,512]{1,0:T(8,128)(2,1)} async-done(((bf16[1024,1024]{1,0:T(8,128)(2,1)}), bf16[1024,512]{1,0:T(8,128)(2,1)}) %reduce-scatter.22.cloned.1.call-update) | async-done | bytes 1048592 | tf_op jit(solution)/shard_map/reduce_scatter | solution.py:62
  940.4 11.2 fusion.388
  960.3 9.0 all-gather.35.cloned.1.call-done
  987.1 8.5 fusion.197
  995.6 8.5 all-gather.33.cloned.1.call-done
  1013.0 25.9 %all-gather.31.cloned.1.call-done = bf16[1024,1024]{1,0:T(8,128)(2,1)} async-done(((bf16[1024,512]{1,0:T(8,128)(2,1)}), bf16[1024,1024]{1,0:T(8,128)(2,1)}) %all-gather.31.cloned.1.call-update) | async-done | bytes 2097168 | tf_op jit(solution)/shard_map/all_gather | solution.py:68
  1053.2 51.0 %while.108 = (s32[]{:T(128)}, f32[8,512,512]{1,2,0:T(8,128)}, bf16[2,512,8,64]{1,3,2,0:T(8,128)(2,1)}, bf16[2,512,8,64]{1,3,2,0:T(8,128)(2,1)}, bf16[2,512,8,64]...) while((s32[]{:T(128)}, f32[8,512,512]{1,2,0:T(8,128)}, ...), condition=%wide.region_60.61_spmd.clone, body=%wide.region_58.60_spmd.clone.sunk | while | flops 1369960448 | bytes 129324336 | solution.py:142
  1089.0 8.7 select_add_fusion.5
  1120.2 61.3 %while.107 = (s32[]{:T(128)}, f32[8,512,512]{1,2,0:T(8,128)}, bf16[2,512,8,64]{1,3,2,0:T(8,128)(2,1)}, bf16[2,512,8,64]{1,3,2,0:T(8,128)(2,1)}, bf16[2,512,8,64]...) while((s32[]{:T(128)}, f32[8,512,512]{1,2,0:T(8,128)}, ...), condition=%wide.region_51.52_spmd.clone, body=%wide.region_49.51_spmd.clone.sunk | while | flops 1369960448 | bytes 196433280 | solution.py:142
  1166.3 8.7 select_add_fusion.4
  1194.5 11.4 fusion.196
  1219.4 10.4 copy.113
  1229.8 10.5 copy.114
  1240.3 19.0 %fusion.306 = f32[32,8]{0,1:T(8,128)S(1)} fusion(f32[512,512,8]{1,2,0:T(8,128)} %copy.113, s32[512,512]{1,0:T(8,128)S(1)} %copy-done.34, pred[]{:T(512)S(6)} %eq.128), kind=kOutput, calls=%fused_computation.387 | convolution fusion | flops 813695232 | bytes 9438209 | tf_op jit(solution)/shard_map/pb,ph->bh/dot_general | solution.py:316
  1259.3 17.0 fusion.307
  1279.4 19.4 %all-reduce.5 = (bf16[1,3,512]{2,0,1:T(2,128)(2,1)S(1)}, bf16[1,32,8]{1,2,0:T(8,128)(2,1)S(1)}) all-reduce(bf16[1,3,512]{2,0,1:T(2,128)(2,1)S(1)} %broadcast_in_dim.257, bf16[1,32,8]{1,2,0:T(8,128)(2,1)S(1)} %fusion.307), channel_id=1, replica_groups=mesh['section'=2,'dp'=8,'tensor'=2] {'dp'}, use_global_device_ids=true, to_apply=%region_75.76 | all-reduce | flops 1792 | bytes 7168 | tf_op jit(solution)/shard_map/psum | solution.py:448
  1308.7 381.4 %all-reduce.9.cloned.1.call-done = (bf16[1,1024,2,512]{3,1,2,0:T(8,128)(2,1)}, bf16[1,1024,3,512]{3,1,2,0:T(8,128)(2,1)}, bf16[1,512,1024]{2,1,0:T(8,128)(2,1)},...) async-done(((bf16[1,1024,2,512]{3,1,2,0:T(8,128)(2,1)}, bf16[1,1024,3,512]{3,1,2,0:T(8,128)(2,1)}, bf16[1,512,1024]{2,1,0:T(8,128)(2,1)}, ...) | async-done | bytes 14680080 | tf_op jit(solution)/shard_map/psum | solution.py:445
  (584 shorter events, 598.5 us)
Async XLA Ops:
  7.2 113.1 %copy-start = (bf16[1,512,1024]{2,1,0:T(8,128)(2,1)S(1)}, bf16[1,512,1024]{2,1,0:T(8,128)(2,1)}, u32[]{:S(2)}) copy-start(bf16[1,512,1024]{2,1,0:T(8,128)(2,1)} %param.44) | copy-start | bytes 3145732
  7.2 45.8 %all-gather.13.cloned.1.call-start = ((), (), s32[]{:S(2)}) async-start(), calls=%async_computation.13 | async-start | bytes 3145728 | tf_op jit(solution)/shard_map/all_gather | solution.py:68
  14.5 146.2 %copy-start.79 = (f32[1,1,512]{2,0,1:T(1,128)}, f32[1,1,512]{2,0,1:T(1,128)S(1)}, u32[]{:S(2)}) copy-start(f32[1,1,512]{2,0,1:T(1,128)S(1)} %get-tuple-element.874) | copy-start | bytes 6148
  17.0 137.9 %reduce-scatter.14.cloned.1.call-start = ((), (), s32[]{:S(2)}) async-start(), calls=%async_computation.14 | async-start | bytes 3145728 | tf_op jit(solution)/shard_map/reduce_scatter | solution.py:62
  122.9 98.4 %all-gather.15.cloned.1.call-start = ((), (), s32[]{:S(2)}) async-start(), calls=%async_computation.15 | async-start | bytes 3145728 | tf_op jit(solution)/shard_map/all_gather | solution.py:68
  163.6 71.3 %reduce-scatter.18.cloned.1.call-start = ((), (), s32[]{:S(2)}) async-start(), calls=%async_computation.17 | async-start | bytes 3145728 | tf_op jit(solution)/shard_map/reduce_scatter | solution.py:62
  192.0 75.2 %reduce-scatter.24.cloned.1.call-start = ((), (), s32[]{:S(2)}) async-start(), calls=%async_computation.23 | async-start | bytes 3145728 | tf_op jit(solution)/shard_map/reduce_scatter | solution.py:62
  221.2 80.6 %reduce-scatter.16.cloned.1.call-start = ((), (), s32[]{:S(2)}) async-start(), calls=%async_computation.16 | async-start | bytes 3145728 | tf_op jit(solution)/shard_map/reduce_scatter | solution.py:62
  228.4 73.4 %copy-start.11 = (bf16[1,2,512,512]{3,2,1,0:T(8,128)(2,1)S(1)}, bf16[1,2,512,512]{3,2,1,0:T(8,128)(2,1)}, u32[]{:S(2)}) copy-start(bf16[1,2,512,512]{3,2,1,0:T(8,128)(2,1)} %param.40) | copy-start | bytes 3145732
  234.8 74.3 %copy-start.76 = (f32[1,1,512]{2,0,1:T(1,128)S(1)}, f32[1,1,512]{2,0,1:T(1,128)}, u32[]{:S(2)}) copy-start(f32[1,1,512]{2,0,1:T(1,128)} %get-tuple-element.876) | copy-start | bytes 6148
  234.8 74.3 %copy-start.80 = (f32[1,1,512]{2,0,1:T(1,128)S(1)}, f32[1,1,512]{2,0,1:T(1,128)}, u32[]{:S(2)}) copy-start(f32[1,1,512]{2,0,1:T(1,128)} %copy-done.79) | copy-start | bytes 6148
  234.8 112.4 %all-gather.17.cloned.1.call-start = ((), (), s32[]{:S(2)}) async-start(), calls=%async_computation.18 | async-start | bytes 3145728 | tf_op jit(solution)/shard_map/all_gather | solution.py:68
  234.9 74.2 %copy-start.14 = (bf16[1024,512]{1,0:T(8,128)(2,1)S(1)}, bf16[1024,512]{1,0:T(8,128)(2,1)}, u32[]{:S(2)}) copy-start(bf16[1024,512]{1,0:T(8,128)(2,1)} %reduce-scatter.18.cloned.1.call-done) | copy-start | bytes 3145732
  312.8 69.7 %all-gather.19.cloned.1.call-start = ((), (), s32[]{:S(2)}) async-start(), calls=%async_computation.19 | async-start | bytes 3145728 | tf_op jit(solution)/shard_map/all_gather | solution.py:68
  316.4 144.3 %reduce-scatter.20.cloned.1.call-start = ((), (), s32[]{:S(2)}) async-start(), calls=%async_computation.20 | async-start | bytes 3145728 | tf_op jit(solution)/shard_map/reduce_scatter | solution.py:62
  353.1 37.1 %collective-permute-start = (bf16[1024,1024]{1,0:T(8,128)(2,1)}, bf16[1024,1024]{1,0:T(8,128)(2,1)}, u32[]{:S(2)}, u32[]{:S(2)}) collective-permute-start(bf16[1024,1024]{1,0:T(8,128)(2,1)} %convert_select_fusion), channel_id=1, source_target_pairs={{0,16},{1,17},{2,18},{3,19},{4,20},{5,21},{6,22},{7,23},{8,24},{9,... | collective-permute-start | bytes 6291464 | tf_op jit(solution)/shard_map/ppermute | solution.py:21
  428.7 76.6 %all-gather.21.cloned.1.call-start = ((), (), s32[]{:S(2)}) async-start(), calls=%async_computation.21 | async-start | bytes 3145728 | tf_op jit(solution)/shard_map/all_gather | solution.py:68
  466.8 186.4 %copy-start.77 = (f32[1024]{0:T(1024)}, f32[1024]{0:T(1024)S(1)}, u32[]{:S(2)}) copy-start(f32[1024]{0:T(1024)S(1)} %add_rsqrt_fusion.2) | copy-start | bytes 12292
  470.9 69.2 %all-gather.25.cloned.1.call-start = ((), (), s32[]{:S(2)}) async-start(), calls=%async_computation.26 | async-start | bytes 3145728 | tf_op jit(solution)/shard_map/all_gather | solution.py:68
  471.6 103.7 %all-gather.23.cloned.1.call-start = ((), (), s32[]{:S(2)}) async-start(), calls=%async_computation.24 | async-start | bytes 3145728 | tf_op jit(solution)/shard_map/all_gather | solution.py:68
  472.2 137.9 %reduce-scatter.28.cloned.1.call-start = ((), (), s32[]{:S(2)}) async-start(), calls=%async_computation.27 | async-start | bytes 3145728 | tf_op jit(solution)/shard_map/reduce_scatter | solution.py:62
  560.5 84.1 %reduce-scatter.26.cloned.1.call-start = ((), (), s32[]{:S(2)}) async-start(), calls=%async_computation.25 | async-start | bytes 3145728 | tf_op jit(solution)/shard_map/reduce_scatter | solution.py:62
  592.2 100.1 %all-gather.27.cloned.1.call-start = ((), (), s32[]{:S(2)}) async-start(), calls=%async_computation.28 | async-start | bytes 3145728 | tf_op jit(solution)/shard_map/all_gather | solution.py:68
  657.8 126.7 %reduce-scatter.30.cloned.1.call-start = ((), (), s32[]{:S(2)}) async-start(), calls=%async_computation.29 | async-start | bytes 3145728 | tf_op jit(solution)/shard_map/reduce_scatter | solution.py:62
  741.3 43.3 %copy-start.16 = (bf16[1024,512]{1,0:T(8,128)(2,1)S(1)}, bf16[1024,512]{1,0:T(8,128)(2,1)}, u32[]{:S(2)}) copy-start(bf16[1024,512]{1,0:T(8,128)(2,1)} %reduce-scatter.24.cloned.1.call-done) | copy-start | bytes 3145732
  741.3 6.5 collective-permute-start.1
  752.9 77.8 %all-gather.29.cloned.1.call-start = ((), (), s32[]{:S(2)}) async-start(), calls=%async_computation.30 | async-start | bytes 3145728 | tf_op jit(solution)/shard_map/all_gather | solution.py:68
  796.2 80.9 %reduce-scatter.36.cloned.1.call-start = ((), (), s32[]{:S(2)}) async-start(), calls=%async_computation.34 | async-start | bytes 3145728 | tf_op jit(solution)/shard_map/reduce_scatter | solution.py:62
  802.7 97.3 %reduce-scatter.32.cloned.1.call-start = ((), (), s32[]{:S(2)}) async-start(), calls=%async_computation.31 | async-start | bytes 3145728 | tf_op jit(solution)/shard_map/reduce_scatter | solution.py:62
  851.3 83.2 %reduce-scatter.22.cloned.1.call-start = ((), (), s32[]{:S(2)}) async-start(), calls=%async_computation.22 | async-start | bytes 3145728 | tf_op jit(solution)/shard_map/reduce_scatter | solution.py:62
  862.5 106.8 %all-gather.35.cloned.1.call-start = ((), (), s32[]{:S(2)}) async-start(), calls=%async_computation.37 | async-start | bytes 3145728 | tf_op jit(solution)/shard_map/all_gather | solution.py:68
  863.2 36.7 %copy-start.15 = (bf16[1024,512]{1,0:T(8,128)(2,1)S(1)}, bf16[1024,512]{1,0:T(8,128)(2,1)}, u32[]{:S(2)}) copy-start(bf16[1024,512]{1,0:T(8,128)(2,1)} %reduce-scatter.18.cloned.1.call-done) | copy-start | bytes 3145732
  863.2 36.7 %copy-start.81 = (f32[1,1,512]{2,0,1:T(1,128)S(1)}, f32[1,1,512]{2,0,1:T(1,128)}, u32[]{:S(2)}) copy-start(f32[1,1,512]{2,0,1:T(1,128)} %copy-done.79) | copy-start | bytes 6148
  863.2 36.7 %copy-start.85 = (f32[1024]{0:T(1024)S(1)}, f32[1024]{0:T(1024)}, u32[]{:S(2)}) copy-start(f32[1024]{0:T(1024)} %copy-done.84) | copy-start | bytes 12292
  863.3 36.7 %copy-start.87 = (f32[1024]{0:T(1024)S(1)}, f32[1024]{0:T(1024)}, u32[]{:S(2)}) copy-start(f32[1024]{0:T(1024)} %copy-done.86) | copy-start | bytes 12292
  863.3 140.8 %all-gather.33.cloned.1.call-start = ((), (), s32[]{:S(2)}) async-start(), calls=%async_computation.35 | async-start | bytes 3145728 | tf_op jit(solution)/shard_map/all_gather | solution.py:68
  877.1 30.9 %copy-start.97 = (f32[1024]{0:T(1024)S(1)}, f32[1024]{0:T(1024)}, u32[]{:S(2)}) copy-start(f32[1024]{0:T(1024)} %copy-done.96) | copy-start | bytes 12292
  877.1 57.4 %copy-start.78 = (f32[1024]{0:T(1024)S(1)}, f32[1024]{0:T(1024)}, u32[]{:S(2)}) copy-start(f32[1024]{0:T(1024)} %copy-done.77) | copy-start | bytes 12292
  877.1 57.4 %copy-start.91 = (f32[1024]{0:T(1024)S(1)}, f32[1024]{0:T(1024)}, u32[]{:S(2)}) copy-start(f32[1024]{0:T(1024)} %copy-done.90) | copy-start | bytes 12292
  940.1 98.7 %all-gather.31.cloned.1.call-start = ((), (), s32[]{:S(2)}) async-start(), calls=%async_computation.32 | async-start | bytes 3145728 | tf_op jit(solution)/shard_map/all_gather | solution.py:68
  960.0 316.4 %reduce-scatter.38.cloned.1.call-start = ((), (), s32[]{:S(2)}) async-start(), calls=%async_computation.36 | async-start | bytes 3145728 | tf_op jit(solution)/shard_map/reduce_scatter | solution.py:62
  1116.9 159.6 %reduce-scatter.34.cloned.1.call-start = ((), (), s32[]{:S(2)}) async-start(), calls=%async_computation.33 | async-start | bytes 3145728 | tf_op jit(solution)/shard_map/reduce_scatter | solution.py:62
  1194.5 495.6 %all-reduce.9.cloned.1.call-start = ((), (), s32[]{:S(2)}) async-start(), calls=%async_computation.38 | async-start | bytes 29360128 | tf_op jit(solution)/shard_map/psum | solution.py:445
  1259.3 20.0 %copy-start.99 = (f32[512]{0:T(512)S(1)}, f32[512]{0:T(512)}, u32[]{:S(2)}) copy-start(f32[512]{0:T(512)} %get-tuple-element.678) | copy-start | bytes 6148
  1259.3 20.0 %copy-start.100 = (f32[512]{0:T(512)S(1)}, f32[512]{0:T(512)}, u32[]{:S(2)}) copy-start(f32[512]{0:T(512)} %get-tuple-element.676) | copy-start | bytes 6148
  1259.3 20.0 %copy-start.101 = (f32[512]{0:T(512)S(1)}, f32[512]{0:T(512)}, u32[]{:S(2)}) copy-start(f32[512]{0:T(512)} %get-tuple-element.682) | copy-start | bytes 6148
  1259.3 20.0 %copy-start.102 = (f32[512]{0:T(512)S(1)}, f32[512]{0:T(512)}, u32[]{:S(2)}) copy-start(f32[512]{0:T(512)} %get-tuple-element.691) | copy-start | bytes 6148
  1259.3 44.9 %copy-start.89 = (f32[1024]{0:T(1024)S(1)}, f32[1024]{0:T(1024)}, u32[]{:S(2)}) copy-start(f32[1024]{0:T(1024)} %copy-done.88) | copy-start | bytes 12292
  (130 other events, 583.8 us)
Sparse Core Ops, SparseCore 0:
  17.2 35.7 all-gather.12
  123.1 31.8 reduce-scatter.13
  163.7 34.2 all-gather.14
  200.8 31.8 reduce-scatter.17
  235.3 31.8 reduce-scatter.23
  270.0 31.8 reduce-scatter.15
  312.9 34.2 all-gather.16
  349.4 33.1 all-gather.18
  428.8 31.8 reduce-scatter.19
  471.0 34.2 all-gather.20
  506.9 33.1 all-gather.24
  542.1 33.1 all-gather.22
  578.2 31.8 reduce-scatter.27
  612.7 31.8 reduce-scatter.25
  658.0 34.2 all-gather.26
  753.0 31.5 reduce-scatter.29
  796.4 34.2 all-gather.28
  833.3 31.8 reduce-scatter.35
  868.1 31.8 reduce-scatter.31
  902.6 31.8 reduce-scatter.21
  936.1 33.0 all-gather.34
  970.9 33.1 all-gather.32
  1005.7 33.1 all-gather.30
  1117.0 31.8 reduce-scatter.37
  1194.6 31.9 reduce-scatter.33
  1233.0 457.0 all-reduce.8
where the time goes:
time: 1730 us; the launch traced here: 1720 us
  waiting for transfers between devices  864 us (50%)
  matrix products  425 us (25%)
  local copies, waits for them, and re-layouts  215 us (12%)
  other arithmetic  136 us (8%)
  blocking collectives  51.1 us (3%)
    psum x1, waiting for transfers between devices, body(): lax.psum(totals[2].astype(jnp.bfloat16), 'dp').astype(jnp.float32)  381 us
    reduce_scatter x13, waiting for transfers between devices, feature_sum(): lax.psum_scatter(partial_value.astype(jnp.bfloat16), 'tensor', scatter_di...  240 us
    all_gather x12, waiting for transfers between devices, feature_gather(): return lax.all_gather(local, 'tensor', axis=1, tiled=True)  237 us
    dot_general x14, matrix products, score_block(): jnp.einsum('qhe,khe->hqk', query, keys, preferred_element_type=jnp.float32)  63.8 us
    unnamed x191, local copies, waits for them, and re-layouts  47.1 us
    while x12, local copies, waits for them, and re-layouts, attend_rows(): return lax.map(one_row, (query, keys, values, allowed))  36.7 us
  transfers between devices with their start and end apart: 28, of which 22 were waited for; matrix products, arithmetic and copies ran while one was open for 26% of the time, Pallas kernels for 0%

commit v1 on v0

v1 whole, which is shorter than its diff:
```python
import functools

import jax
import jax.numpy as jnp
import numpy as np
from jax import lax
from jax.experimental import pallas as pl
from jax.experimental.pallas import tpu as pltpu
from jax.sharding import Mesh
from jax.sharding import PartitionSpec as P

D = 1024
HEAD = 64
BUCKETS = 32
MAXDIST = 128


epsilon = 1e-06
masked_score = -1e30
highest = lax.Precision.HIGHEST
bf16 = jnp.bfloat16
f32 = jnp.float32


def dot_t(a, b):
    return lax.dot_general(a, b, (((1,), (1,)), ((), ())), preferred_element_type=f32)


def dot_n(a, b):
    return lax.dot_general(a, b, (((1,), (0,)), ((), ())), preferred_element_type=f32)


def t_dot(a, b):
    return lax.dot_general(a, b, (((0,), (0,)), ((), ())), preferred_element_type=f32)


def toeplitz(vector, length):
    wide = jnp.broadcast_to(vector, (length, 2 * length))
    return pltpu.roll(wide, length, 1, stride=1, stride_axis=0)[:, :length]


def diagonal_sums(block):
    length = block.shape[0]
    row = lax.broadcasted_iota(jnp.int32, (length, length), 0)
    column = lax.broadcasted_iota(jnp.int32, (length, length), 1)
    upside = dot_n((row + column == length - 1).astype(bf16), block)
    wide = jnp.concatenate([upside, jnp.zeros_like(upside)], axis=1)
    return jnp.sum(pltpu.roll(wide, 1, 1, stride=1, stride_axis=0), axis=0, keepdims=True)


def allowed_pairs(query_ids, key_ids, causal):
    allowed = query_ids == key_ids
    if causal:
        key = lax.broadcasted_iota(jnp.int32, allowed.shape, 1)
        query = lax.broadcasted_iota(jnp.int32, allowed.shape, 0)
        allowed = allowed & (key <= query)
    return allowed


def attend_kernel(causal, biased, q_ref, k_ref, v_ref, query_ids, key_ids, *rest):
    if biased:
        vector, out_ref, log_ref = rest
    else:
        out_ref, log_ref = rest
    q = q_ref[0] * bf16(HEAD**-0.5)
    k, v = k_ref[0], v_ref[0]
    lane = lax.broadcasted_iota(jnp.int32, (1, 2 * HEAD), 1)
    allowed = allowed_pairs(query_ids[0], key_ids[0], causal)
    out, logs = None, []
    for head in range(2):
        mine = (lane // HEAD) == head
        scores = dot_t(jnp.where(mine, q, jnp.zeros_like(q)), k)
        if biased:
            scores = scores + toeplitz(vector[0, head : head + 1], scores.shape[0])
        scores = jnp.where(allowed, scores, masked_score)
        peak = jnp.max(scores, axis=1, keepdims=True)
        exponent = jnp.exp(scores - peak)
        total = jnp.sum(exponent, axis=1, keepdims=True)
        weights = (exponent * (1.0 / total)).astype(bf16)
        mixed = dot_n(weights, v)
        out = mixed if out is None else jnp.where(mine, mixed, out)
        logs.append(peak + jnp.log(total))
    out_ref[...] = out.astype(bf16)
    log_ref[0, 0] = jnp.concatenate(logs, axis=1)


def attend_back_kernel(
    causal, biased, q_ref, k_ref, v_ref, query_ids, key_ids, up_ref, log_ref, *rest
):
    if biased:
        vector, dq_ref, dk_ref, dv_ref, diagonal_ref = rest
    else:
        dq_ref, dk_ref, dv_ref = rest
    q = q_ref[0] * bf16(HEAD**-0.5)
    k, v, up = k_ref[0], v_ref[0], up_ref[...]
    lane = lax.broadcasted_iota(jnp.int32, (1, 2 * HEAD), 1)
    allowed = allowed_pairs(query_ids[0], key_ids[0], causal)
    dq = dk = dv = None
    for head in range(2):
        mine = (lane // HEAD) == head
        own_q = jnp.where(mine, q, jnp.zeros_like(q))
        own_up = jnp.where(mine, up, jnp.zeros_like(up))
        scores = dot_t(own_q, k)
        if biased:
            scores = scores + toeplitz(vector[0, head : head + 1], scores.shape[0])
        scores = jnp.where(allowed, scores - log_ref[0, 0, :, head : head + 1], masked_score)
        weights = jnp.exp(scores)
        dots = dot_t(own_up, v)
        inner = jnp.sum(weights * dots, axis=1, keepdims=True)
        grad = (weights * (dots - inner)).astype(bf16)
        a, b, c = dot_n(grad, k), t_dot(grad, own_q), t_dot(weights.astype(bf16), own_up)
        dq = a if head == 0 else jnp.where(mine, a, dq)
        dk = b if head == 0 else dk + b
        dv = c if head == 0 else dv + c
        if biased:
            diagonal_ref[0, 0, head : head + 1] = diagonal_sums(grad)
    dq_ref[0] = (dq * (HEAD**-0.5)).astype(bf16)
    dk_ref[0] = dk.astype(bf16)
    dv_ref[0] = dv.astype(bf16)


little = pl.CostEstimate(flops=1, bytes_accessed=1, transcendentals=1)
kernel_params = pltpu.CompilerParams(vmem_limit_bytes=48 * 1024 * 1024)


def operand_specs(parts, length):
    def one(index):
        return pl.BlockSpec((1, length, 2 * HEAD), lambda r, p: (index, r, p))

    return [one(index) for index in parts] + [
        pl.BlockSpec((1, length, 1), lambda r, p: (r, 0, 0)),
        pl.BlockSpec((1, 1, length), lambda r, p: (r, 0, 0)),
    ]


def attend(query, stored, parts, query_ids, key_ids, vector, causal):
    rows, length = query_ids.shape
    width = query.shape[2]
    pairs = width // (2 * HEAD)
    biased = vector is not None
    specs, more = operand_specs(parts, length), ()
    if biased:
        specs.append(pl.BlockSpec((1, 2, 2 * length), lambda r, p: (p, 0, 0)))
        more = (vector.reshape(pairs, 2, 2 * length),)
    return pl.pallas_call(
        functools.partial(attend_kernel, causal, biased),
        grid=(rows, pairs),
        in_specs=specs,
        out_specs=[
            pl.BlockSpec((length, 2 * HEAD), lambda r, p: (r, p)),
            pl.BlockSpec((1, 1, length, 2), lambda r, p: (r, p, 0, 0)),
        ],
        out_shape=[
            jax.ShapeDtypeStruct((rows * length, width), bf16),
            jax.ShapeDtypeStruct((rows, pairs, length, 2), f32),
        ],
        compiler_params=kernel_params,
        cost_estimate=little,
    )(query, stored, stored, query_ids[:, :, None], key_ids[:, None, :], *more)


def attend_back(query, stored, parts, query_ids, key_ids, vector, causal, up, logs):
    rows, length = query_ids.shape
    width = query.shape[2]
    pairs = width // (2 * HEAD)
    biased = vector is not None
    each = pl.BlockSpec((1, length, 2 * HEAD), lambda r, p: (0, r, p))
    shape = jax.ShapeDtypeStruct((1, rows * length, width), bf16)
    specs = operand_specs(parts, length) + [
        pl.BlockSpec((length, 2 * HEAD), lambda r, p: (r, p)),
        pl.BlockSpec((1, 1, length, 2), lambda r, p: (r, p, 0, 0)),
    ]
    out_specs, out_shape, more = [each] * 3, [shape] * 3, ()
    if biased:
        specs.append(pl.BlockSpec((1, 2, 2 * length), lambda r, p: (p, 0, 0)))
        more = (vector.reshape(pairs, 2, 2 * length),)
        out_specs.append(pl.BlockSpec((1, 1, 2, 2 * length), lambda r, p: (r, p, 0, 0)))
        out_shape.append(jax.ShapeDtypeStruct((rows, pairs, 2, 2 * length), f32))
    return pl.pallas_call(
        functools.partial(attend_back_kernel, causal, biased),
        grid=(rows, pairs),
        in_specs=specs,
        out_specs=out_specs,
        out_shape=out_shape,
        compiler_params=kernel_params,
        cost_estimate=little,
    )(query, stored, stored, query_ids[:, :, None], key_ids[:, None, :], up, logs, *more)


def bucket_onehot(length, causal):
    count = BUCKETS if causal else BUCKETS // 2
    exact = count // 2
    distance = np.arange(length)
    spread = exact + (
        np.log(np.maximum(distance, 1) / exact) / np.log(MAXDIST / exact) * (count - exact)
    ).astype(np.int64)
    levels = np.where(distance < exact, distance, np.minimum(spread, count - 1))
    breaks = [
        int(np.argmax(levels >= level))
        for level in range(1, count)
        if bool((levels >= level).any())
    ]
    offset = np.arange(2 * length) - length
    if causal:
        reach = np.maximum(-offset, 0)
        bucket = np.zeros(2 * length, np.int64)
    else:
        reach = np.abs(offset)
        bucket = np.where(offset > 0, count, 0)
    for edge in breaks:
        bucket = bucket + (reach >= edge)
    return jnp.asarray(bucket[:, None] == np.arange(BUCKETS)[None, :], f32)


def swap_section(value):
    return lax.ppermute(value, "section", [(0, 1), (1, 0)])


def swap_tensor(value):
    return lax.ppermute(value, "tensor", [(0, 1), (1, 0)])


def ordered(index, mine, other, axis):
    return jnp.where(
        index == 0,
        jnp.concatenate([mine, other], axis=axis),
        jnp.concatenate([other, mine], axis=axis),
    )


def hold(value, *after):
    return lax.optimization_barrier((value, after))[0]


def joined_features(local, other, axis=1):
    if lax.axis_size("tensor") == 2:
        return ordered(lax.axis_index("tensor"), local, other, axis)
    return lax.all_gather(local, "tensor", axis=axis, tiled=True)


def gather_features(local, axis=1):
    return joined_features(local, swap_tensor(local) if lax.axis_size("tensor") == 2 else local, axis)


def own_features(full):
    count = lax.axis_size("tensor")
    width = full.shape[1] // count
    return lax.dynamic_slice_in_dim(full, lax.axis_index("tensor") * width, width, 1)


def total_features(low):
    if lax.axis_size("tensor") == 2:
        return low.astype(f32) + swap_tensor(low).astype(f32)
    return lax.psum(low, "tensor").astype(f32)


def scatter_features(low):
    if lax.axis_size("tensor") == 2:
        width = low.shape[1] // 2
        first = lax.axis_index("tensor") == 0
        left, right = low[:, :width], low[:, width:]
        received = swap_tensor(jnp.where(first, right, left))
        return jnp.where(first, left, right).astype(f32) + received.astype(f32)
    return lax.psum_scatter(low, "tensor", scatter_dimension=1, tiled=True).astype(f32)


def total_tokens(values):
    if lax.axis_size("tensor") == 2:
        return values + swap_tensor(values.reshape(-1, 128)).reshape(-1)
    return lax.psum(values, "tensor")


def smooth(values):
    return jax.nn.gelu(values, approximate=True)


def matmul(a, b):
    return jnp.dot(a, b, preferred_element_type=f32)


def matmul_t(a, b):
    return jnp.einsum("tc,dc->td", a, b, preferred_element_type=f32)


def weight_grad(a, b):
    return jnp.einsum("tc,td->cd", a, b, preferred_element_type=f32).astype(bf16)


def norm_forward(hidden, gain):
    inverse = lax.rsqrt(jnp.mean(hidden * hidden, axis=1, keepdims=True) + epsilon)
    return ((hidden * inverse * gain).astype(bf16), inverse)


def norm_backward(hidden, gain, inverse, upstream):
    scaled = upstream * gain
    inner = jnp.sum(scaled * hidden, axis=1, keepdims=True)
    return inverse * scaled - hidden * (inverse * inverse * inverse * inner / D)


def gain_gradient(hidden, inverse, upstream):
    return jnp.sum(upstream * hidden * inverse, axis=0)


def self_forward(hidden, gain, mixing, projecting, vector, ids, causal):
    normed, inverse = norm_forward(hidden, gain)
    projected = jnp.einsum("td,edc->etc", normed, mixing, preferred_element_type=f32).astype(bf16)
    mixed, logs = attend(projected, projected, (0, 1, 2), ids, ids, vector, causal)
    return (matmul(mixed, projecting).astype(bf16), (normed, inverse, projected, mixed, logs))


def self_backward(projecting, vector, ids, causal, kept, low):
    normed, inverse, projected, mixed, logs = kept
    up = matmul_t(low, projecting).astype(bf16)
    dq, dk, dv, diagonals = attend_back(
        projected, projected, (0, 1, 2), ids, ids, vector, causal, up, logs
    )
    return ((dq[0], dk[0], dv[0]), diagonals)


def mixing_back(parts, mixing):
    return sum(matmul_t(part, mixing[index]) for index, part in enumerate(parts)).astype(bf16)


def input_gradient_of(hidden, gain, inverse, partial_value, grad):
    inner = total_tokens(jnp.sum(partial_value.astype(f32) * gain * hidden, axis=1))[:, None]
    upstream = scatter_features(partial_value)
    own, own_gain = own_features(hidden), own_features(gain[None])
    result = inverse * upstream * own_gain - own * (inverse * inverse * inverse * inner / D)
    return (result + own_features(grad), gain_gradient(own, inverse, upstream))


def dense_forward(hidden, gain, expanding, contracting):
    normed, inverse = norm_forward(hidden, gain)
    before = matmul(normed, expanding)
    activated = smooth(before).astype(bf16)
    return (activated, (normed, inverse, before, activated))


def dense_backward(expanding, contracting, kept, low):
    normed, inverse, before, activated = kept
    upward = matmul_t(low, contracting)
    again, smooth_back = jax.vjp(smooth, before)
    before_grad = smooth_back(upward)[0].astype(bf16)
    return (before_grad, matmul_t(before_grad, expanding).astype(bf16))


def section_half(value):
    half = value.shape[0] // 2
    first = lax.axis_index("section") == 0
    received = swap_section(jnp.where(first, value[half:], value[:half]))
    return jnp.where(first, value[:half], value[half:]) + received


def section_own(encoder_value, decoder_value):
    first = lax.axis_index("section") == 0
    received = swap_section(jnp.where(first, decoder_value, encoder_value))
    return jnp.where(first, encoder_value, decoder_value) + received


def sum_rows(values):
    return lax.psum(values, ("z", "y"))


def sum_rows_small(value):
    if lax.axis_size("z") != 4 or lax.axis_size("y") != 2:
        return lax.psum(value, ("z", "y"))
    value = value.reshape(-1, 128)
    value = value + lax.ppermute(value, "y", [(0, 1), (1, 0)])
    value = value + lax.ppermute(value, "z", [(i, i ^ 1) for i in range(4)])
    return value + lax.ppermute(value, "z", [(i, i ^ 2) for i in range(4)])


ring = [2 * z for z in range(4)] + [2 * z + 1 for z in reversed(range(4))]


def along_ring(value, way):
    pairs = [(ring[i], ring[(i + way) % 8]) for i in range(8)]
    return lax.ppermute(value, ("z", "y"), pairs)


def ring_pieces(groups):
    z, y = lax.axis_index("z"), lax.axis_index("y")
    place = jnp.where(y == 0, z, 7 - z)
    ways = (1, -1)

    def piece(value, index):
        return lax.dynamic_index_in_dim(value, lax.rem(index + 16, 8), 0, keepdims=False)

    def put(value, part, index):
        return lax.dynamic_update_index_in_dim(value, part, lax.rem(index + 16, 8), 0)

    return place, ways, piece, put


def ring_start(groups):
    place, ways, piece, put = ring_pieces(groups)
    moving = [[piece(value, place) for value in pair] for pair in groups]
    return ring_step(groups, moving, 0)


def ring_step(groups, moving, step):
    place, ways, piece, put = ring_pieces(groups)
    moving = list(moving)
    for g, pair in enumerate(groups):
        received = [along_ring(moving[g][w], ways[w]) for w in range(2)]
        moving[g] = [
            received[w] + piece(pair[w], place - ways[w] * (step + 1)) for w in range(2)
        ]
    return moving


def ring_finish(groups, moving):
    place, ways, piece, put = ring_pieces(groups)
    for step in range(1, 7):
        moving = ring_step(groups, moving, step)
    totals = [
        [put(pair[w], moving[g][w], place + ways[w]) for w in range(2)]
        for g, pair in enumerate(groups)
    ]
    for step in range(7):
        for g, pair in enumerate(totals):
            moving[g] = [along_ring(moving[g][w], ways[w]) for w in range(2)]
            totals[g] = [
                put(totals[g][w], moving[g][w], place - ways[w] * step) for w in range(2)
            ]
        if step == 4:
            late = moving
    return (totals, late)


def body(
    layer_inputs,
    output_cotangents,
    segment_ids,
    attention_in,
    attention_out,
    cross_weights,
    expand_weights,
    contract_weights,
    norm_gains,
    bias_tables,
):
    all_rows, length, local_width = layer_inputs.shape[1:]
    rows = all_rows // 2
    tokens = rows * length
    section = lax.axis_index("section")
    first = section == 0

    def pick(mine, other):
        return (jnp.where(first, mine, other), jnp.where(first, other, mine))

    def both(mine, *after):
        return pick(mine, swap_section(hold(mine, *after)))

    def own_rows(value):
        mine = lax.dynamic_slice_in_dim(value[0], section * rows, rows, 0)
        give = lax.dynamic_slice_in_dim(value[0], (1 - section) * rows, rows, 0)
        return pick(mine.reshape(tokens, -1), swap_section(give).reshape(tokens, -1))

    def all_layer_rows(encoder_value, decoder_value):
        mine = jnp.where(first, encoder_value, decoder_value)
        other = swap_section(jnp.where(first, decoder_value, encoder_value))
        return ordered(section, mine, other, 0).reshape(1, all_rows, length, local_width)

    encoder_half, decoder_half = own_rows(layer_inputs)
    mixing = both(attention_in[0].transpose(1, 0, 2))
    encoder_in = gather_features(encoder_half).astype(f32)
    own_gains = gather_features(norm_gains[0])
    small_own = jnp.concatenate([own_gains.reshape(-1), bias_tables[0].reshape(-1)])
    small_both = both(small_own)
    gains = [part[: own_gains.size].reshape(own_gains.shape) for part in small_both]
    tables = [part[own_gains.size :].reshape(bias_tables.shape[1:]) for part in small_both]
    projecting, expanding, contracting, crossing = lax.all_gather(
        (attention_out[0], expand_weights[0], contract_weights[0], cross_weights[0].transpose(1, 0, 2)),
        "section",
    )
    encoder_cotangent, decoder_cotangent = own_rows(output_cotangents)
    later_halves = hold(jnp.stack([decoder_half, encoder_cotangent, decoder_cotangent]), encoder_in)
    later_others = swap_tensor(later_halves) if lax.axis_size("tensor") == 2 else later_halves
    encoder_in = hold(encoder_in, mixing)
    ids = lax.dynamic_slice_in_dim(segment_ids, section * rows, rows, 1)
    encoder_ids, decoder_ids = ids[0], ids[1]
    onehots = (bucket_onehot(length, False), bucket_onehot(length, True))
    vectors = [
        jnp.einsum("bh,jb->hj", table, onehot, precision=highest)
        for table, onehot in zip(tables, onehots)
    ]

    x1_part, encoder_self = self_forward(
        encoder_in, gains[0][0], mixing[0], projecting[0], vectors[0], encoder_ids, False
    )
    later_halves, later_others = hold((later_halves, later_others), x1_part)
    decoder_in, encoder_cotangent, decoder_cotangent = joined_features(later_halves, later_others, 2)
    decoder_in = decoder_in.astype(f32)
    z1_part, decoder_self = self_forward(
        decoder_in, gains[1][0], mixing[1], projecting[1], vectors[1], decoder_ids, True
    )
    x1 = encoder_in + total_features(x1_part)
    activated, encoder_dense = dense_forward(hold(x1, z1_part), gains[0][1], expanding[0], contracting[0])
    x2_part = matmul(activated, contracting[0]).astype(bf16)
    z1 = decoder_in + total_features(z1_part)
    cross_in, cross_inverse = norm_forward(z1, gains[1][1])
    query = matmul(cross_in, crossing[1][0]).astype(bf16)[None]
    x2 = x1 + total_features(x2_part)
    memory_in, memory_inverse = norm_forward(x2, gains[0][2])
    memory = jnp.einsum("td,edc->etc", memory_in, crossing[0], preferred_element_type=f32)
    memory = memory.astype(bf16)
    cross_mixed, cross_logs = attend(
        query, memory, (0, 0, 1), decoder_ids, encoder_ids, None, False
    )
    z2_part = matmul_t(cross_mixed, crossing[1][1]).astype(bf16)
    z2 = z1 + total_features(z2_part)
    activated, decoder_dense = dense_forward(z2, gains[1][2], expanding[1], contracting[1])

    before_grad, part = dense_backward(expanding[1], contracting[1], decoder_dense, decoder_cotangent)
    upstream = total_features(part)
    activated, before_grad, normed = hold((activated, before_grad, decoder_dense[0]), part)
    decoder_contract = weight_grad(activated, decoder_cotangent)
    decoder_expand = weight_grad(normed, before_grad)
    upstream = hold(upstream, decoder_contract, decoder_expand)
    first_halves = [section_half(decoder_contract), section_half(decoder_expand)]
    first_sums = sum_rows(first_halves)
    dz2 = norm_backward(z2, gains[1][2], decoder_dense[1], upstream) + decoder_cotangent.astype(f32)
    gain_two = gain_gradient(z2, decoder_dense[1], upstream)

    low = dz2.astype(bf16)
    up = matmul(hold(low, first_halves), crossing[1][1]).astype(bf16)
    dquery, dkeys, dvalues = attend_back(
        query, memory, (0, 0, 1), decoder_ids, encoder_ids, None, False, up, cross_logs
    )
    memory_part = sum(
        matmul_t(part[0], crossing[0][index]) for index, part in enumerate((dkeys, dvalues))
    ).astype(bf16)
    memory_up = total_features(memory_part)
    dquery, dkeys, dvalues, low = hold((dquery, dkeys, dvalues, low), memory_part)
    query_part = matmul_t(dquery[0], crossing[1][0]).astype(bf16)
    decoder_cross = jnp.stack([weight_grad(cross_in, dquery[0]), weight_grad(low, cross_mixed)])
    encoder_cross = jnp.stack(
        [weight_grad(memory_in, dkeys[0]), weight_grad(memory_in, dvalues[0])]
    )

    memory_up, decoder_cross, encoder_cross = lax.optimization_barrier(
        (memory_up, decoder_cross, encoder_cross)
    )

    dx2 = norm_backward(x2, gains[0][2], memory_inverse, memory_up) + encoder_cotangent.astype(f32)
    query_up = total_features(hold(query_part, memory_up))
    low = dx2.astype(bf16)
    before_grad, part = dense_backward(expanding[0], contracting[0], encoder_dense, low)
    upstream = total_features(part)

    before_grad, activated, normed, low, query_up = hold(
        (before_grad, encoder_dense[3], encoder_dense[0], low, query_up), part
    )
    encoder_contract = weight_grad(activated, low)
    encoder_expand = weight_grad(normed, before_grad)
    query_up = hold(query_up, encoder_contract, encoder_expand)
    dz1 = norm_backward(z1, gains[1][1], cross_inverse, query_up) + dz2
    decoder_low = dz1.astype(bf16)
    decoder_dqkv, decoder_diagonals = self_backward(
        projecting[1], vectors[1], decoder_ids, True, decoder_self, decoder_low
    )

    upstream = hold(upstream, decoder_dqkv)
    dx1 = norm_backward(x1, gains[0][1], encoder_dense[1], upstream) + dx2
    low = dx1.astype(bf16)
    encoder_dqkv, encoder_diagonals = self_backward(
        projecting[0], vectors[0], encoder_ids, False, encoder_self, low
    )

    decoder_dqkv, decoder_low, low = hold((decoder_dqkv, decoder_low, low), encoder_dqkv)
    encoder_mixing = jnp.stack([weight_grad(encoder_self[0], value) for value in encoder_dqkv])
    decoder_mixing = jnp.stack([weight_grad(decoder_self[0], value) for value in decoder_dqkv])
    encoder_projecting = weight_grad(encoder_self[3], low)
    decoder_projecting = weight_grad(decoder_self[3], decoder_low)

    encoder_dqkv, decoder_dqkv, activated = hold(
        (encoder_dqkv, decoder_dqkv, decoder_dense[3]),
        encoder_mixing, decoder_mixing, encoder_projecting, decoder_projecting,
    )
    encoder_part = mixing_back(encoder_dqkv, mixing[0])
    decoder_part = mixing_back(decoder_dqkv, mixing[1])
    out_part = matmul(activated, contracting[1]).astype(bf16)

    def narrowed(value, width):
        return jnp.concatenate(
            [value[:, at : at + width] for at in range(0, value.shape[1], width)], axis=0
        )

    def widened(value, width):
        count = width // value.shape[1]
        length = value.shape[0] // count
        return jnp.concatenate(
            [value[at * length : (at + 1) * length] for at in range(count)], axis=1
        )

    contract_sum = section_half(encoder_contract)
    expand_sum = section_half(encoder_expand)
    mixing_sum = section_own(encoder_mixing, decoder_mixing)
    projecting_sum = section_own(encoder_projecting, decoder_projecting)

    narrow = mixing_sum.shape[2]
    groups, encoder_part, decoder_part, out_part = lax.optimization_barrier((
        [
            [contract_sum, expand_sum],
            [
                mixing_sum[:2].reshape(-1, narrow),
                jnp.concatenate([mixing_sum[2], narrowed(projecting_sum, narrow)]),
            ],
        ],
        encoder_part, decoder_part, out_part,
    ))
    first_sums = hold(first_sums, groups)
    cross_sum = section_own(encoder_cross, decoder_cross)
    cross_sum = sum_rows(hold(cross_sum, first_sums))
    groups = [[value.reshape(8, -1, value.shape[1]) for value in pair] for pair in groups]
    whole_ring = lax.axis_size("z") == 4 and lax.axis_size("y") == 2
    moving = ring_start(groups) if whole_ring else groups

    encoder_part, decoder_part, out_part, memory_up, upstream = hold(
        (encoder_part, decoder_part, out_part, memory_up, upstream), moving
    )
    encoder_gain_two = gain_gradient(x2, memory_inverse, memory_up)
    encoder_gain_one = gain_gradient(x1, encoder_dense[1], upstream)
    gain_one = gain_gradient(z1, cross_inverse, query_up)
    encoder_grad, encoder_gain_zero = input_gradient_of(
        encoder_in, gains[0][0], encoder_self[1], encoder_part, dx1
    )
    decoder_grad, gain_zero = input_gradient_of(
        decoder_in, gains[1][0], decoder_self[1], decoder_part, dz1
    )
    decoder_out = own_features(z2) + scatter_features(out_part)

    def small(gain_zero, gain_one, gain_two, diagonals, onehot):
        ones = [gain_zero[None], own_features(gain_one[None]), own_features(gain_two[None])]
        summed = jnp.sum(diagonals, axis=0).reshape(-1, 2 * length)
        table = jnp.einsum("hj,jb->bh", summed, onehot, precision=highest)
        return jnp.concatenate(ones + [table.reshape(1, -1)], axis=1)

    decoder_small = small(gain_zero, gain_one, gain_two, decoder_diagonals, onehots[1])
    encoder_small = small(
        encoder_gain_zero, encoder_gain_one, encoder_gain_two, encoder_diagonals, onehots[0]
    )
    small_sum = sum_rows_small(section_own(encoder_small, decoder_small))
    if whole_ring:
        totals, late = ring_finish(groups, moving)
    else:
        totals = late = sum_rows(groups)
    (contract_sum, expand_sum), (query_key_sum, last) = [
        [value.reshape(-1, value.shape[2]) for value in pair] for pair in totals
    ]
    mixing_sum = jnp.concatenate([query_key_sum, last[:D]]).reshape(3, D, narrow)
    projecting_sum = widened(last[D:], D)
    cross_sum = hold(cross_sum, late)
    small_sum = small_sum.reshape(-1)

    def whole(encoder_sum, decoder_sum):
        mine = jnp.where(first, encoder_sum, decoder_sum)
        other = swap_section(jnp.where(first, decoder_sum, encoder_sum))
        return ordered(section, mine, other, 0).astype(f32)

    width = D // lax.axis_size("tensor")
    return (
        all_layer_rows(own_features(x2), decoder_out),
        all_layer_rows(encoder_grad, decoder_grad),
        mixing_sum.astype(f32).transpose(1, 0, 2)[None],
        projecting_sum.astype(f32)[None],
        cross_sum.astype(f32).transpose(1, 0, 2)[None],
        whole(expand_sum, first_sums[1])[None],
        whole(contract_sum, first_sums[0])[None],
        small_sum[: 3 * width].reshape(1, 3, width),
        small_sum[3 * width :].reshape(1, BUCKETS, -1),
    )


def solution(mesh):
    sections, groups, width = mesh.devices.shape
    along = 4 if groups % 4 == 0 else groups
    mesh = Mesh(
        mesh.devices.reshape(sections, along, groups // along, width),
        ("section", "z", "y", "tensor"),
    )
    return jax.shard_map(
        body,
        mesh=mesh,
        in_specs=(
            P("section", ("z", "y"), None, "tensor"),
            P("section", ("z", "y"), None, "tensor"),
            P(None, ("z", "y"), None),
            P("section", None, None, "tensor"),
            P("section", "tensor", None),
            P("section", None, None, "tensor"),
            P("section", None, "tensor"),
            P("section", "tensor", None),
            P("section", None, "tensor"),
            P("section", None, "tensor"),
        ),
        out_specs=(
            P("section", ("z", "y"), None, "tensor"),
            P("section", ("z", "y"), None, "tensor"),
            P("section", None, None, "tensor"),
            P("section", "tensor", None),
            P("section", None, None, "tensor"),
            P("section", None, "tensor"),
            P("section", "tensor", None),
            P("section", None, "tensor"),
            P("section", None, "tensor"),
        ),
        check_vma=False,
    )
```

time: 1730 us -> 677 us (0.39)
  waiting for transfers between devices: 864 us -> 199 us
  matrix products: 425 us -> 95 us
  local copies, waits for them, and re-layouts: 215 us -> 55.8 us
  starting transfers between devices: 7.02 us -> 106 us
  Pallas kernels: 0 us -> 65.9 us
  blocking collectives: 51.1 us -> 0 us
    psum x1 -> x2, waiting for transfers between devices: 381 us -> 0.01 us  [sum_rows(): return lax.psum(values, ('z', 'y'))]
    dot_general x85 -> x47, matrix products: 425 us -> 95 us  [the longest x8 35.6 us: matmul(): return jnp.dot(a, b, preferred_element_type=f32)]
    reduce_scatter x13 -> x0, waiting for transfers between devices: 240 us -> none  [feature_sum(): lax.psum_scatter(partial_value.astype(jnp.bfloat16), 'tensor', scatter_di...]
    all_gather x12 -> x4, waiting for transfers between devices: 237 us -> 0.01 us  [body(): lax.all_gather((attention_out[0], expand_weights[0], contract_weights[0],...]
    ppermute x2 -> x91, waiting for transfers between devices: 3.64 us -> 197 us  [the longest x56 97 us: along_ring(): return lax.ppermute(value, ('z', 'y'), pairs)]
    ppermute x2 -> x91, starting transfers between devices: 4.54 us -> 106 us  [the longest x56 56.8 us: along_ring(): return lax.ppermute(value, ('z', 'y'), pairs)]
    pallas_call x0 -> x6, Pallas kernels: none -> 65.9 us  [the longest x3 34.6 us: attend_back(): pl.pallas_call(functools.partial(attend_back_kernel, causal, biased), gri...]
    while x137 -> x0, local copies, waits for them, and re-layouts: 63.5 us -> none  [the longest x12 36.7 us: attend_rows(): return lax.map(one_row, (query, keys, values, allowed))]
  transfers between devices with their start and end apart: 28 -> 97, of which waited for: 22 -> 39; matrix products, arithmetic and copies ran while one was open for 26% -> 33% of each run, Pallas kernels for 0% -> 9%
where the time goes in v1:
time: 677 us; the launch traced here: 667 us
  waiting for transfers between devices  199 us (29%)
  other arithmetic  129 us (19%)
  starting transfers between devices  106 us (16%)
  matrix products  95 us (14%)
  Pallas kernels  65.9 us (10%)
  local copies, waits for them, and re-layouts  55.8 us (8%)
  between operations  16.7 us (2%)
    ppermute x56, waiting for transfers between devices, along_ring(): return lax.ppermute(value, ('z', 'y'), pairs)  97 us
    ppermute x16, waiting for transfers between devices, swap_tensor(): return lax.ppermute(value, 'tensor', [(0, 1), (1, 0)])  86.8 us
    ppermute x56, starting transfers between devices, along_ring(): return lax.ppermute(value, ('z', 'y'), pairs)  56.8 us
    unnamed x284, local copies, waits for them, and re-layouts  38.2 us
    dot_general x8, matrix products, matmul(): return jnp.dot(a, b, preferred_element_type=f32)  35.6 us
    pallas_call x3, Pallas kernels, attend_back(): pl.pallas_call(functools.partial(attend_back_kernel, causal, biased), gri...  34.6 us
    dot_general x16, matrix products, matmul_t(): return jnp.einsum('tc,dc->td', a, b, preferred_element_type=f32)  33.2 us
    ppermute x16, starting transfers between devices, swap_section(): return lax.ppermute(value, 'section', [(0, 1), (1, 0)])  32.7 us
  transfers between devices with their start and end apart: 97, of which 39 were waited for; matrix products, arithmetic and copies ran while one was open for 33% of the time, Pallas kernels for 9%

profile of v1, /device:TPU:1, one launch (start us, length us, event | category | flops | bytes accessed | tf_op | source)
XLA Modules:
  0.0 666.9 jit_solution(15410319284765547947)
XLA Ops:
  24.3 10.8 %collective-permute-done.1 = bf16[512,512]{1,0:T(8,128)(2,1)S(1)} collective-permute-done((bf16[512,512]{1,0:T(8,128)(2,1)S(1)}, bf16[512,512]{1,0:T(8,128)(2,1)S(1)}, u32[]{:S(2)}, u32[]{:S(2)}) %collective-permute-start.1) | collective-permute-done | bytes 524320 | tf_op jit(solution)/shard_map/ppermute | solution.py:220
  35.7 6.2 broadcast_select_fusion.1
  45.6 12.1 %shard_map.187 = (bf16[512,512]{1,0:T(8,128)(2,1)S(1)}, f32[1,4,512,2]{3,2,1,0:T(8,128)S(1)}) custom-call(bf16[3,512,512]{2,1,0:T(8,128)(2,1)S(1)} %fusion.30.q_ref.k_ref.v_ref, bf16[3,512,512]{2,1,0:T(8,128)(2,1)S(1)} %fusion.30.q_ref.k_ref.v_ref, bf16[3,512,512]{2,1,0:T(8,128)(2,1)S(1)} %fusion.30.q_ref.k_ref.v_ref, s32[1,512,1]{2,1,0:T(8,128)S(1)} %copy.60.query_ids, ...), custom_call_target="tpu_custom_call" | custom-call | flops 1 | bytes 1 | tf_op jit(solution)/shard_map/pallas_call | solution.py:145
  62.2 8.5 %collective-permute-done.7 = bf16[3,512,512]{2,1,0:T(8,128)(2,1)} collective-permute-done((bf16[3,512,512]{2,1,0:T(8,128)(2,1)}, bf16[3,512,512]{2,1,0:T(8,128)(2,1)}, u32[]{:S(2)}, u32[]{:S(2)}) %collective-permute-start.7) | collective-permute-done | bytes 1572896 | tf_op jit(solution)/shard_map/ppermute | solution.py:220
  70.7 3.5 maximum_select_fusion.2
  77.9 13.1 %shard_map.188 = (bf16[512,512]{1,0:T(8,128)(2,1)S(1)}, f32[1,4,512,2]{3,2,1,0:T(8,128)S(1)}) custom-call(bf16[3,512,512]{2,1,0:T(8,128)(2,1)S(1)} %fusion.31.q_ref.k_ref.v_ref, bf16[3,512,512]{2,1,0:T(8,128)(2,1)S(1)} %fusion.31.q_ref.k_ref.v_ref, bf16[3,512,512]{2,1,0:T(8,128)(2,1)S(1)} %fusion.31.q_ref.k_ref.v_ref, s32[1,512,1]{2,1,0:T(8,128)S(1)} %copy.66.query_ids, ...), custom_call_target="tpu_custom_call" | custom-call | flops 1 | bytes 1 | tf_op jit(solution)/shard_map/pallas_call | solution.py:145
  96.7 8.2 %multiply_convert_fusion.1 = (bf16[512,2048]{1,0:T(8,128)(2,1)}, f32[512,2048]{1,0:T(8,128)}) fusion(bf16[512,1024]{1,0:T(8,128)(2,1)} %multiply_convert_fusion.5, bf16[2,1024,2048]{2,1,0:T(8,128)(2,1)} %all-gather.8.cloned.1.call-done), kind=kOutput, calls=%fused_computation.29 | convolution fusion | flops 2156920832 | bytes 11534336 | tf_op jit(solution)/shard_map/dot_general | solution.py:278
  105.0 6.1 fusion.37
  114.4 3.6 multiply_reduce_fusion.11
  120.8 16.1 %collective-permute-done.8 = bf16[512,1024]{1,0:T(8,128)(2,1)} collective-permute-done((bf16[512,1024]{1,0:T(8,128)(2,1)}, bf16[512,1024]{1,0:T(8,128)(2,1)}, u32[]{:S(2)}, u32[]{:S(2)}) %collective-permute-start.8) | collective-permute-done | bytes 1048608 | tf_op jit(solution)/shard_map/ppermute | solution.py:220
  141.6 6.1 shard_map.189
  149.5 19.4 %collective-permute-done.10 = bf16[512,1024]{1,0:T(8,128)(2,1)S(1)} collective-permute-done((bf16[512,1024]{1,0:T(8,128)(2,1)S(1)}, bf16[512,1024]{1,0:T(8,128)(2,1)S(1)}, u32[]{:S(2)}, u32[]{:S(2)}) %collective-permute-start.10) | collective-permute-done | bytes 1048608 | tf_op jit(solution)/shard_map/ppermute | solution.py:220
  169.8 6.1 multiply_convert_fusion
  175.9 4.7 fusion.13
  190.5 5.0 collective-permute-start.12
  220.2 10.1 %shard_map.190 = (bf16[1,512,512]{2,1,0:T(8,128)(2,1)S(1)}, bf16[1,512,512]{2,1,0:T(8,128)(2,1)S(1)}, bf16[1,512,512]{2,1,0:T(8,128)(2,1)S(1)}) custom-call(bf16[1,512,512]{2,1,0:T(8,128)(2,1)S(1)} %copy-done.5, bf16[2,512,512]{2,1,0:T(8,128)(2,1)S(1)} %copy-done.1, bf16[2,512,512]{2,1,0:T(8,128)(2,1)S(1)} %copy-done.1, s32[1,512,1]{2,1,0:T(8,128)S(1)} %copy.66.query_ids, ...), custom_call_target="tpu_custom_call" | custom-call | flops 1 | bytes 1 | tf_op jit(solution)/shard_map/pallas_call | solution.py:179
  238.1 13.5 %collective-permute-done.14 = bf16[512,1024]{1,0:T(8,128)(2,1)S(1)} collective-permute-done((bf16[512,1024]{1,0:T(8,128)(2,1)S(1)}, bf16[512,1024]{1,0:T(8,128)(2,1)S(1)}, u32[]{:S(2)}, u32[]{:S(2)}) %collective-permute-start.14) | collective-permute-done | bytes 1048608 | tf_op jit(solution)/shard_map/ppermute | solution.py:220
  255.9 7.0 %fusion.6 = bf16[512,2048]{1,0:T(8,128)(2,1)S(1)} fusion(f32[512,2048]{1,0:T(8,128)S(1)} %copy-done.132, bf16[512,1024]{1,0:T(8,128)(2,1)S(1)} %fusion.92, bf16[2,2048,1024]{2,1,0:T(8,128)(2,1)} %all-gather.10.cloned.1.call-done), kind=kOutput, calls=%fused_computation.11 | convolution fusion | flops 2168455168 | bytes 11534336 | tf_op jit(solution)/shard_map/tc,dc->td/dot_general | solution.py:282
  267.7 6.5 collective-permute-start.58
  279.7 13.0 %collective-permute-start.16 = (bf16[1024,1024]{1,0:T(8,128)(2,1)}, bf16[1024,1024]{1,0:T(8,128)(2,1)}, u32[]{:S(2)}, u32[]{:S(2)}) collective-permute-start(bf16[1024,1024]{1,0:T(8,128)(2,1)} %broadcast_select_fusion.6), channel_id=1, source_target_pairs={{0,16},{16,0},{1,17},{17,1},{2,18},{18,2},{3,19},{19,3},{4,20},{20... | collective-permute-start | bytes 6291464 | tf_op jit(solution)/shard_map/ppermute | solution.py:216
  303.7 12.2 %shard_map.191 = (bf16[1,512,512]{2,1,0:T(8,128)(2,1)S(1)}, bf16[1,512,512]{2,1,0:T(8,128)(2,1)S(1)}, bf16[1,512,512]{2,1,0:T(8,128)(2,1)S(1)}, f32[1,4,2,1024]{3,2,1,0:T(2,128)S(1)}) custom-call(bf16[3,512,512]{2,1,0:T(8,128)(2,1)S(1)} %fusion.31.q_ref.k_ref.v_ref, bf16[3,512,512]{2,1,0:T(8,128)(2,1)S(1)} %fusion.31.q_ref.k_ref.v_ref, ...), custom_call_target="tpu_custom_call" | custom-call | flops 1 | bytes 1 | tf_op jit(solution)/shard_map/pallas_call | solution.py:179
  323.5 12.3 %shard_map.192 = (bf16[1,512,512]{2,1,0:T(8,128)(2,1)S(1)}, bf16[1,512,512]{2,1,0:T(8,128)(2,1)S(1)}, bf16[1,512,512]{2,1,0:T(8,128)(2,1)S(1)}, f32[1,4,2,1024]{3,2,1,0:T(2,128)S(1)}) custom-call(bf16[3,512,512]{2,1,0:T(8,128)(2,1)S(1)} %fusion.30.q_ref.k_ref.v_ref, bf16[3,512,512]{2,1,0:T(8,128)(2,1)S(1)} %fusion.30.q_ref.k_ref.v_ref, ...), custom_call_target="tpu_custom_call" | custom-call | flops 1 | bytes 1 | tf_op jit(solution)/shard_map/pallas_call | solution.py:179
  355.5 5.6 fusion.36
  373.3 3.5 select_add_fusion.3
  388.3 3.8 collective-permute-done.22
  395.6 7.8 %collective-permute-done.23 = bf16[256,512]{1,0:T(8,128)(2,1)} collective-permute-done((bf16[256,512]{1,0:T(8,128)(2,1)S(1)}, bf16[256,512]{1,0:T(8,128)(2,1)}, u32[]{:S(2)}, u32[]{:S(2)}) %collective-permute-start.23) | collective-permute-done | bytes 262176 | tf_op jit(solution)/shard_map/ppermute | solution.py:378
  407.8 4.5 collective-permute-start.45
  421.0 10.5 %collective-permute-done.72 = bf16[64,2048]{1,0:T(8,128)(2,1)S(1)} collective-permute-done((bf16[64,2048]{1,0:T(8,128)(2,1)S(1)}, bf16[64,2048]{1,0:T(8,128)(2,1)S(1)}, u32[]{:S(2)}, u32[]{:S(2)}) %collective-permute-start.72) | collective-permute-done | bytes 262176 | tf_op jit(solution)/shard_map/ppermute | solution.py:378
  439.0 5.8 collective-permute-done.27
  448.0 7.9 %collective-permute-done.29 = bf16[512,512]{1,0:T(8,128)(2,1)S(1)} collective-permute-done((bf16[512,512]{1,0:T(8,128)(2,1)S(1)}, bf16[512,512]{1,0:T(8,128)(2,1)S(1)}, u32[]{:S(2)}, u32[]{:S(2)}) %collective-permute-start.29) | collective-permute-done | bytes 524320 | tf_op jit(solution)/shard_map/ppermute | solution.py:220
  468.5 8.4 %collective-permute-done.89 = f32[14,128]{1,0:T(8,128)S(1)} collective-permute-done((f32[14,128]{1,0:T(8,128)S(1)}, f32[14,128]{1,0:T(8,128)S(1)}, u32[]{:S(2)}, u32[]{:S(2)}) %collective-permute-start.89) | collective-permute-done | bytes 7200 | tf_op jit(solution)/shard_map/ppermute | solution.py:369
  480.1 3.6 collective-permute-done.90
  489.9 7.0 %collective-permute-done.61 = bf16[128,1024]{1,0:T(8,128)(2,1)} collective-permute-done((bf16[128,1024]{1,0:T(8,128)(2,1)}, bf16[128,1024]{1,0:T(8,128)(2,1)}, u32[]{:S(2)}, u32[]{:S(2)}) %collective-permute-start.61) | collective-permute-done | bytes 262176 | tf_op jit(solution)/shard_map/ppermute | solution.py:378
  497.0 6.8 %collective-permute-start.35 = (bf16[256,512]{1,0:T(8,128)(2,1)S(1)}, bf16[256,512]{1,0:T(8,128)(2,1)S(1)}, u32[]{:S(2)}, u32[]{:S(2)}) collective-permute-start(bf16[256,512]{1,0:T(8,128)(2,1)S(1)} %bitcast_add_fusion.22), channel_id=1, source_target_pairs={{0,4},{4,8},{8,12},{12,14},{14,10},{10,6},{6,2},{2,0},{1,5},{5,9},... | collective-permute-start | bytes 786440 | tf_op jit(solution)/shard_map/ppermute | solution.py:378
  508.9 6.8 %collective-permute-done.48 = bf16[256,512]{1,0:T(8,128)(2,1)S(1)} collective-permute-done((bf16[256,512]{1,0:T(8,128)(2,1)S(1)}, bf16[256,512]{1,0:T(8,128)(2,1)S(1)}, u32[]{:S(2)}, u32[]{:S(2)}) %collective-permute-start.48) | collective-permute-done | bytes 262176 | tf_op jit(solution)/shard_map/ppermute | solution.py:378
  530.9 3.6 collective-permute-done.63
  542.3 4.4 collective-permute-done.64
  563.7 4.0 collective-permute-done.66
  574.1 4.8 collective-permute-done.67
  585.2 4.9 collective-permute-done.68
  596.4 4.9 collective-permute-done.69
  607.7 4.9 collective-permute-done.70
  618.4 5.5 collective-permute-done.71
  628.2 5.3 collective-permute-start.85
  640.2 5.2 copy.77
  647.3 3.6 convert_bitcast_fusion
  650.9 4.5 fusion.14
  655.4 4.4 fusion.15
  (677 shorter events, 303.8 us)
Async XLA Ops:
  7.2 51.3 %all-gather.6.cloned.1.call-start = ((), (), s32[]{:S(2)}) async-start(), calls=%async_computation | async-start | bytes 3145728 | tf_op jit(solution)/shard_map/all_gather | solution.py:473
  7.9 88.8 %all-gather.8.cloned.1.call-start = ((), (), s32[]{:S(2)}) async-start(), calls=%async_computation.1 | async-start | bytes 12582912 | tf_op jit(solution)/shard_map/all_gather | solution.py:473
  8.7 96.3 %all-gather.10.cloned.1.call-start = ((), (), s32[]{:S(2)}) async-start(), calls=%async_computation.2 | async-start | bytes 12582912 | tf_op jit(solution)/shard_map/all_gather | solution.py:473
  9.4 108.6 %all-gather.12.cloned.1.call-start = ((), (), s32[]{:S(2)}) async-start(), calls=%async_computation.4 | async-start | bytes 6291456 | tf_op jit(solution)/shard_map/all_gather | solution.py:473
  9.5 26.2 %collective-permute-start.2 = (bf16[3,1024,512]{2,1,0:T(8,128)(2,1)}, bf16[3,1024,512]{2,1,0:T(8,128)(2,1)}, u32[]{:S(2)}, u32[]{:S(2)}) collective-permute-start(bf16[3,1024,512]{2,1,0:T(8,128)(2,1)} %bitcast.4), channel_id=1, source_target_pairs={{0,16},{16,0},{1,17},{17,1},{2,18},{18,2},{3,19},{19,3},{4,20},{20... | collective-permute-start | bytes 9437192 | tf_op jit(solution)/shard_map/ppermute | solution.py:216
  17.4 370.8 %all-reduce.6.cloned.1.call-start = ((), (), s32[]{:S(2)}) async-start(), calls=%async_computation.5 | async-start | bytes 8388608 | tf_op jit(solution)/shard_map/psum | solution.py:361
  21.7 13.4 %collective-permute-start.1 = (bf16[512,512]{1,0:T(8,128)(2,1)S(1)}, bf16[512,512]{1,0:T(8,128)(2,1)S(1)}, u32[]{:S(2)}, u32[]{:S(2)}) collective-permute-start(bf16[512,512]{1,0:T(8,128)(2,1)S(1)} %bitcast_select_fusion.7), channel_id=1, source_target_pairs={{0,1},{1,0},{2,3},{3,2},{4,5},{5,4},{6,7},{7,6},{8,9},{9,8},{10,11... | collective-permute-start | bytes 1572872 | tf_op jit(solution)/shard_map/ppermute | solution.py:220
  35.4 35.3 %collective-permute-start.7 = (bf16[3,512,512]{2,1,0:T(8,128)(2,1)}, bf16[3,512,512]{2,1,0:T(8,128)(2,1)}, u32[]{:S(2)}, u32[]{:S(2)}) collective-permute-start(bf16[3,512,512]{2,1,0:T(8,128)(2,1)} %pad_maximum_fusion.6), channel_id=1, source_target_pairs={{0,1},{1,0},{2,3},{3,2},{4,5},{5,4},{6,7},{7,6},{8,9},{9,8},{10,11... | collective-permute-start | bytes 4718600 | tf_op jit(solution)/shard_map/ppermute | solution.py:220
  61.2 32.0 %collective-permute-start.5 = (bf16[512,1024]{1,0:T(8,128)(2,1)S(1)}, bf16[512,1024]{1,0:T(8,128)(2,1)S(1)}, u32[]{:S(2)}, u32[]{:S(2)}) collective-permute-start(bf16[512,1024]{1,0:T(8,128)(2,1)S(1)} %convolution_convert_fusion.21), channel_id=1, source_target_pairs={{0,1},{1,0},{2,3},{3,2},{4,5},{5,4},{6,7},{7,6},{8,9},{9,8},{10,11... | collective-permute-start | bytes 3145736 | tf_op jit(solution)/shard_map/ppermute | solution.py:220
  92.8 21.6 %collective-permute-start.9 = (bf16[512,1024]{1,0:T(8,128)(2,1)}, bf16[512,1024]{1,0:T(8,128)(2,1)}, u32[]{:S(2)}, u32[]{:S(2)}) collective-permute-start(bf16[512,1024]{1,0:T(8,128)(2,1)} %convolution_convert_fusion.20), channel_id=1, source_target_pairs={{0,1},{1,0},{2,3},{3,2},{4,5},{5,4},{6,7},{7,6},{8,9},{9,8},{10,11... | collective-permute-start | bytes 3145736 | tf_op jit(solution)/shard_map/ppermute | solution.py:220
  111.1 25.7 %collective-permute-start.8 = (bf16[512,1024]{1,0:T(8,128)(2,1)}, bf16[512,1024]{1,0:T(8,128)(2,1)}, u32[]{:S(2)}, u32[]{:S(2)}) collective-permute-start(bf16[512,1024]{1,0:T(8,128)(2,1)} %fusion.37), channel_id=1, source_target_pairs={{0,1},{1,0},{2,3},{3,2},{4,5},{5,4},{6,7},{7,6},{8,9},{9,8},{10,11... | collective-permute-start | bytes 3145736 | tf_op jit(solution)/shard_map/ppermute | solution.py:220
  148.5 20.4 %collective-permute-start.10 = (bf16[512,1024]{1,0:T(8,128)(2,1)S(1)}, bf16[512,1024]{1,0:T(8,128)(2,1)S(1)}, u32[]{:S(2)}, u32[]{:S(2)}) collective-permute-start(bf16[512,1024]{1,0:T(8,128)(2,1)S(1)} %convolution_convert_fusion.19), channel_id=1, source_target_pairs={{0,1},{1,0},{2,3},{3,2},{4,5},{5,4},{6,7},{7,6},{8,9},{9,8},{10,11... | collective-permute-start | bytes 3145736 | tf_op jit(solution)/shard_map/ppermute | solution.py:220
  184.0 20.5 %collective-permute-start.11 = (bf16[512,1024]{1,0:T(8,128)(2,1)}, bf16[512,1024]{1,0:T(8,128)(2,1)}, u32[]{:S(2)}, u32[]{:S(2)}) collective-permute-start(bf16[512,1024]{1,0:T(8,128)(2,1)} %fusion.35), channel_id=1, source_target_pairs={{0,1},{1,0},{2,3},{3,2},{4,5},{5,4},{6,7},{7,6},{8,9},{9,8},{10,11... | collective-permute-start | bytes 3145736 | tf_op jit(solution)/shard_map/ppermute | solution.py:220
  190.5 20.4 %collective-permute-start.12 = (bf16[1024,1024]{1,0:T(8,128)(2,1)}, bf16[1024,1024]{1,0:T(8,128)(2,1)}, u32[]{:S(2)}, u32[]{:S(2)}) collective-permute-start(bf16[1024,1024]{1,0:T(8,128)(2,1)} %broadcast_select_fusion.7), channel_id=1, source_target_pairs={{0,16},{16,0},{1,17},{17,1},{2,18},{18,2},{3,19},{19,3},{4,20},{20... | collective-permute-start | bytes 6291464 | tf_op jit(solution)/shard_map/ppermute | solution.py:216
  200.5 13.9 %collective-permute-start.13 = (bf16[512,2048]{1,0:T(8,128)(2,1)}, bf16[512,2048]{1,0:T(8,128)(2,1)}, u32[]{:S(2)}, u32[]{:S(2)}) collective-permute-start(bf16[512,2048]{1,0:T(8,128)(2,1)} %broadcast_select_fusion.5), channel_id=1, source_target_pairs={{0,16},{16,0},{1,17},{17,1},{2,18},{18,2},{3,19},{19,3},{4,20},{20... | collective-permute-start | bytes 6291464 | tf_op jit(solution)/shard_map/ppermute | solution.py:216
  217.7 399.8 %all-reduce.4.cloned.1.call-start = ((), (), s32[]{:S(2)}) async-start(), calls=%async_computation.3 | async-start | bytes 4194304 | tf_op jit(solution)/shard_map/psum | solution.py:361
  231.9 19.7 %collective-permute-start.14 = (bf16[512,1024]{1,0:T(8,128)(2,1)S(1)}, bf16[512,1024]{1,0:T(8,128)(2,1)S(1)}, u32[]{:S(2)}, u32[]{:S(2)}) collective-permute-start(bf16[512,1024]{1,0:T(8,128)(2,1)S(1)} %add_convert_fusion.2), channel_id=1, source_target_pairs={{0,1},{1,0},{2,3},{3,2},{4,5},{5,4},{6,7},{7,6},{8,9},{9,8},{10,11... | collective-permute-start | bytes 3145736 | tf_op jit(solution)/shard_map/ppermute | solution.py:220
  255.2 19.1 %collective-permute-start.15 = (bf16[512,1024]{1,0:T(8,128)(2,1)S(1)}, bf16[512,1024]{1,0:T(8,128)(2,1)S(1)}, u32[]{:S(2)}, u32[]{:S(2)}) collective-permute-start(bf16[512,1024]{1,0:T(8,128)(2,1)S(1)} %convolution_convert_fusion.14), channel_id=1, source_target_pairs={{0,1},{1,0},{2,3},{3,2},{4,5},{5,4},{6,7},{7,6},{8,9},{9,8},{10,11... | collective-permute-start | bytes 3145736 | tf_op jit(solution)/shard_map/ppermute | solution.py:220
  265.4 50.5 %collective-permute-start.18 = (bf16[512,1024]{1,0:T(8,128)(2,1)S(1)}, bf16[512,1024]{1,0:T(8,128)(2,1)}, u32[]{:S(2)}, u32[]{:S(2)}) collective-permute-start(bf16[512,1024]{1,0:T(8,128)(2,1)S(1)} %fusion.38), channel_id=1, source_target_pairs={{0,1},{1,0},{2,3},{3,2},{4,5},{5,4},{6,7},{7,6},{8,9},{9,8},{10,11... | collective-permute-start | bytes 3145736 | tf_op jit(solution)/shard_map/ppermute | solution.py:220
  267.7 98.0 %collective-permute-start.58 = (bf16[2,1024,512]{2,1,0:T(8,128)(2,1)}, bf16[2,1024,512]{2,1,0:T(8,128)(2,1)}, u32[]{:S(2)}, u32[]{:S(2)}) collective-permute-start(bf16[2,1024,512]{2,1,0:T(8,128)(2,1)} %broadcast_select_fusion.3), channel_id=1, source_target_pairs={{0,16},{16,0},{1,17},{17,1},{2,18},{18,2},{3,19},{19,3},{4,20},{20... | collective-permute-start | bytes 6291464 | tf_op jit(solution)/shard_map/ppermute | solution.py:216
  279.7 92.8 %collective-permute-start.16 = (bf16[1024,1024]{1,0:T(8,128)(2,1)}, bf16[1024,1024]{1,0:T(8,128)(2,1)}, u32[]{:S(2)}, u32[]{:S(2)}) collective-permute-start(bf16[1024,1024]{1,0:T(8,128)(2,1)} %broadcast_select_fusion.6), channel_id=1, source_target_pairs={{0,16},{16,0},{1,17},{17,1},{2,18},{18,2},{3,19},{19,3},{4,20},{20... | collective-permute-start | bytes 6291464 | tf_op jit(solution)/shard_map/ppermute | solution.py:216
  297.8 79.0 %collective-permute-start.17 = (bf16[512,2048]{1,0:T(8,128)(2,1)}, bf16[512,2048]{1,0:T(8,128)(2,1)}, u32[]{:S(2)}, u32[]{:S(2)}) collective-permute-start(bf16[512,2048]{1,0:T(8,128)(2,1)} %broadcast_select_fusion.4), channel_id=1, source_target_pairs={{0,16},{16,0},{1,17},{17,1},{2,18},{18,2},{3,19},{19,3},{4,20},{20... | collective-permute-start | bytes 6291464 | tf_op jit(solution)/shard_map/ppermute | solution.py:216
  343.0 36.0 %collective-permute-start.19 = (bf16[3,1024,512]{2,1,0:T(8,128)(2,1)}, bf16[3,1024,512]{2,1,0:T(8,128)(2,1)}, u32[]{:S(2)}, u32[]{:S(2)}) collective-permute-start(bf16[3,1024,512]{2,1,0:T(8,128)(2,1)} %broadcast_select_fusion), channel_id=1, source_target_pairs={{0,16},{16,0},{1,17},{17,1},{2,18},{18,2},{3,19},{19,3},{4,20},{20... | collective-permute-start | bytes 9437192 | tf_op jit(solution)/shard_map/ppermute | solution.py:216
  346.6 23.9 %collective-permute-start.20 = (bf16[512,1024]{1,0:T(8,128)(2,1)}, bf16[512,1024]{1,0:T(8,128)(2,1)}, u32[]{:S(2)}, u32[]{:S(2)}) collective-permute-start(bf16[512,1024]{1,0:T(8,128)(2,1)} %get-tuple-element.223), channel_id=1, source_target_pairs={{0,16},{16,0},{1,17},{17,1},{2,18},{18,2},{3,19},{19,3},{4,20},{20... | collective-permute-start | bytes 3145736 | tf_op jit(solution)/shard_map/ppermute | solution.py:216
  386.7 16.7 %collective-permute-start.23 = (bf16[256,512]{1,0:T(8,128)(2,1)S(1)}, bf16[256,512]{1,0:T(8,128)(2,1)}, u32[]{:S(2)}, u32[]{:S(2)}) collective-permute-start(bf16[256,512]{1,0:T(8,128)(2,1)S(1)} %dynamic-slice_bitcast_fusion.3), channel_id=1, source_target_pairs={{0,4},{4,8},{8,12},{12,14},{14,10},{10,6},{6,2},{2,0},{1,5},{5,9},... | collective-permute-start | bytes 786440 | tf_op jit(solution)/shard_map/ppermute | solution.py:378
  388.2 16.3 %collective-permute-start.24 = (bf16[256,512]{1,0:T(8,128)(2,1)S(1)}, bf16[256,512]{1,0:T(8,128)(2,1)S(1)}, u32[]{:S(2)}, u32[]{:S(2)}) collective-permute-start(bf16[256,512]{1,0:T(8,128)(2,1)S(1)} %dynamic-slice_bitcast_fusion.2), channel_id=1, source_target_pairs={{0,2},{4,0},{8,4},{12,8},{14,12},{10,14},{6,10},{2,6},{1,3},{5,1},... | collective-permute-start | bytes 786440 | tf_op jit(solution)/shard_map/ppermute | solution.py:378
  407.8 25.7 %collective-permute-start.45 = (bf16[256,512]{1,0:T(8,128)(2,1)S(1)}, bf16[256,512]{1,0:T(8,128)(2,1)S(1)}, u32[]{:S(2)}, u32[]{:S(2)}) collective-permute-start(bf16[256,512]{1,0:T(8,128)(2,1)S(1)} %bitcast_add_fusion.25), channel_id=1, source_target_pairs={{0,2},{4,0},{8,4},{12,8},{14,12},{10,14},{6,10},{2,6},{1,3},{5,1},... | collective-permute-start | bytes 786440 | tf_op jit(solution)/shard_map/ppermute | solution.py:378
  412.4 22.7 %collective-permute-start.32 = (bf16[256,512]{1,0:T(8,128)(2,1)S(1)}, bf16[256,512]{1,0:T(8,128)(2,1)S(1)}, u32[]{:S(2)}, u32[]{:S(2)}) collective-permute-start(bf16[256,512]{1,0:T(8,128)(2,1)S(1)} %bitcast_add_fusion.26), channel_id=1, source_target_pairs={{0,4},{4,8},{8,12},{12,14},{14,10},{10,6},{6,2},{2,0},{1,5},{5,9},... | collective-permute-start | bytes 786440 | tf_op jit(solution)/shard_map/ppermute | solution.py:378
  412.4 24.3 %collective-permute-start.59 = (bf16[128,1024]{1,0:T(8,128)(2,1)S(1)}, bf16[128,1024]{1,0:T(8,128)(2,1)S(1)}, u32[]{:S(2)}, u32[]{:S(2)}) collective-permute-start(bf16[128,1024]{1,0:T(8,128)(2,1)S(1)} %bitcast_add_fusion.28), channel_id=1, source_target_pairs={{0,4},{4,8},{8,12},{12,14},{14,10},{10,6},{6,2},{2,0},{1,5},{5,9},... | collective-permute-start | bytes 786440 | tf_op jit(solution)/shard_map/ppermute | solution.py:378
  413.5 18.0 %collective-permute-start.72 = (bf16[64,2048]{1,0:T(8,128)(2,1)S(1)}, bf16[64,2048]{1,0:T(8,128)(2,1)S(1)}, u32[]{:S(2)}, u32[]{:S(2)}) collective-permute-start(bf16[64,2048]{1,0:T(8,128)(2,1)S(1)} %bitcast_add_fusion.27), channel_id=1, source_target_pairs={{0,2},{4,0},{8,4},{12,8},{14,12},{10,14},{6,10},{2,6},{1,3},{5,1},... | collective-permute-start | bytes 786440 | tf_op jit(solution)/shard_map/ppermute | solution.py:378
  420.4 25.5 %collective-permute-start.25 = (bf16[512,512]{1,0:T(8,128)(2,1)S(1)}, bf16[512,512]{1,0:T(8,128)(2,1)S(1)}, u32[]{:S(2)}, u32[]{:S(2)}) collective-permute-start(bf16[512,512]{1,0:T(8,128)(2,1)S(1)} %broadcast_select_fusion.13), channel_id=1, source_target_pairs={{0,1},{1,0},{2,3},{3,2},{4,5},{5,4},{6,7},{7,6},{8,9},{9,8},{10,11... | collective-permute-start | bytes 1572872 | tf_op jit(solution)/shard_map/ppermute | solution.py:220
  431.5 13.2 %collective-permute-start.27 = (bf16[512,512]{1,0:T(8,128)(2,1)S(1)}, bf16[512,512]{1,0:T(8,128)(2,1)S(1)}, u32[]{:S(2)}, u32[]{:S(2)}) collective-permute-start(bf16[512,512]{1,0:T(8,128)(2,1)S(1)} %broadcast_select_fusion.11), channel_id=1, source_target_pairs={{0,1},{1,0},{2,3},{3,2},{4,5},{5,4},{6,7},{7,6},{8,9},{9,8},{10,11... | collective-permute-start | bytes 1572872 | tf_op jit(solution)/shard_map/ppermute | solution.py:220
  433.5 22.4 %collective-permute-start.29 = (bf16[512,512]{1,0:T(8,128)(2,1)S(1)}, bf16[512,512]{1,0:T(8,128)(2,1)S(1)}, u32[]{:S(2)}, u32[]{:S(2)}) collective-permute-start(bf16[512,512]{1,0:T(8,128)(2,1)S(1)} %broadcast_select_fusion.9), channel_id=1, source_target_pairs={{0,1},{1,0},{2,3},{3,2},{4,5},{5,4},{6,7},{7,6},{8,9},{9,8},{10,11... | collective-permute-start | bytes 1572872 | tf_op jit(solution)/shard_map/ppermute | solution.py:220
  435.0 27.1 %collective-permute-start.46 = (bf16[256,512]{1,0:T(8,128)(2,1)S(1)}, bf16[256,512]{1,0:T(8,128)(2,1)S(1)}, u32[]{:S(2)}, u32[]{:S(2)}) collective-permute-start(bf16[256,512]{1,0:T(8,128)(2,1)S(1)} %bitcast_add_fusion.18), channel_id=1, source_target_pairs={{0,2},{4,0},{8,4},{12,8},{14,12},{10,14},{6,10},{2,6},{1,3},{5,1},... | collective-permute-start | bytes 786440 | tf_op jit(solution)/shard_map/ppermute | solution.py:378
  436.6 30.1 %collective-permute-start.33 = (bf16[256,512]{1,0:T(8,128)(2,1)S(1)}, bf16[256,512]{1,0:T(8,128)(2,1)S(1)}, u32[]{:S(2)}, u32[]{:S(2)}) collective-permute-start(bf16[256,512]{1,0:T(8,128)(2,1)S(1)} %bitcast_add_fusion.24), channel_id=1, source_target_pairs={{0,4},{4,8},{8,12},{12,14},{14,10},{10,6},{6,2},{2,0},{1,5},{5,9},... | collective-permute-start | bytes 786440 | tf_op jit(solution)/shard_map/ppermute | solution.py:378
  444.8 32.2 %collective-permute-start.60 = (bf16[128,1024]{1,0:T(8,128)(2,1)S(1)}, bf16[128,1024]{1,0:T(8,128)(2,1)S(1)}, u32[]{:S(2)}, u32[]{:S(2)}) collective-permute-start(bf16[128,1024]{1,0:T(8,128)(2,1)S(1)} %bitcast_add_fusion.12), channel_id=1, source_target_pairs={{0,4},{4,8},{8,12},{12,14},{14,10},{10,6},{6,2},{2,0},{1,5},{5,9},... | collective-permute-start | bytes 786440 | tf_op jit(solution)/shard_map/ppermute | solution.py:378
  445.9 11.6 %collective-permute-start.73 = (bf16[64,2048]{1,0:T(8,128)(2,1)S(1)}, bf16[64,2048]{1,0:T(8,128)(2,1)S(1)}, u32[]{:S(2)}, u32[]{:S(2)}) collective-permute-start(bf16[64,2048]{1,0:T(8,128)(2,1)S(1)} %bitcast_add_fusion.6), channel_id=1, source_target_pairs={{0,2},{4,0},{8,4},{12,8},{14,12},{10,14},{6,10},{2,6},{1,3},{5,1},... | collective-permute-start | bytes 786440 | tf_op jit(solution)/shard_map/ppermute | solution.py:378
  455.9 92.6 %collective-permute-start.26 = (f32[512,512]{1,0:T(8,128)}, f32[512,512]{1,0:T(8,128)}, u32[]{:S(2)}, u32[]{:S(2)}) collective-permute-start(f32[512,512]{1,0:T(8,128)} %get-tuple-element.198), channel_id=1, source_target_pairs={{0,16},{16,0},{1,17},{17,1},{2,18},{18,2},{3,19},{19,3},{4,20},{20... | collective-permute-start | bytes 3145736 | tf_op jit(solution)/shard_map/ppermute | solution.py:216
  461.7 91.6 %collective-permute-start.31 = (f32[512,512]{1,0:T(8,128)}, f32[512,512]{1,0:T(8,128)}, u32[]{:S(2)}, u32[]{:S(2)}) collective-permute-start(f32[512,512]{1,0:T(8,128)} %broadcast_select_fusion.14), channel_id=1, source_target_pairs={{0,16},{16,0},{1,17},{17,1},{2,18},{18,2},{3,19},{19,3},{4,20},{20... | collective-permute-start | bytes 3145736 | tf_op jit(solution)/shard_map/ppermute | solution.py:216
  465.4 20.9 %collective-permute-start.47 = (bf16[256,512]{1,0:T(8,128)(2,1)}, bf16[256,512]{1,0:T(8,128)(2,1)}, u32[]{:S(2)}, u32[]{:S(2)}) collective-permute-start(bf16[256,512]{1,0:T(8,128)(2,1)} %bitcast_add_fusion.17), channel_id=1, source_target_pairs={{0,2},{4,0},{8,4},{12,8},{14,12},{10,14},{6,10},{2,6},{1,3},{5,1},... | collective-permute-start | bytes 786440 | tf_op jit(solution)/shard_map/ppermute | solution.py:378
  483.6 13.4 %collective-permute-start.61 = (bf16[128,1024]{1,0:T(8,128)(2,1)}, bf16[128,1024]{1,0:T(8,128)(2,1)}, u32[]{:S(2)}, u32[]{:S(2)}) collective-permute-start(bf16[128,1024]{1,0:T(8,128)(2,1)} %bitcast_add_fusion.11), channel_id=1, source_target_pairs={{0,4},{4,8},{8,12},{12,14},{14,10},{10,6},{6,2},{2,0},{1,5},{5,9},... | collective-permute-start | bytes 786440 | tf_op jit(solution)/shard_map/ppermute | solution.py:378
  486.2 19.7 %collective-permute-start.74 = (bf16[64,2048]{1,0:T(8,128)(2,1)S(1)}, bf16[64,2048]{1,0:T(8,128)(2,1)S(1)}, u32[]{:S(2)}, u32[]{:S(2)}) collective-permute-start(bf16[64,2048]{1,0:T(8,128)(2,1)S(1)} %bitcast_add_fusion.5), channel_id=1, source_target_pairs={{0,2},{4,0},{8,4},{12,8},{14,12},{10,14},{6,10},{2,6},{1,3},{5,1},... | collective-permute-start | bytes 786440 | tf_op jit(solution)/shard_map/ppermute | solution.py:378
  487.7 28.1 %collective-permute-start.48 = (bf16[256,512]{1,0:T(8,128)(2,1)S(1)}, bf16[256,512]{1,0:T(8,128)(2,1)S(1)}, u32[]{:S(2)}, u32[]{:S(2)}) collective-permute-start(bf16[256,512]{1,0:T(8,128)(2,1)S(1)} %bitcast_add_fusion.16), channel_id=1, source_target_pairs={{0,2},{4,0},{8,4},{12,8},{14,12},{10,14},{6,10},{2,6},{1,3},{5,1},... | collective-permute-start | bytes 786440 | tf_op jit(solution)/shard_map/ppermute | solution.py:378
  497.0 18.8 %collective-permute-start.35 = (bf16[256,512]{1,0:T(8,128)(2,1)S(1)}, bf16[256,512]{1,0:T(8,128)(2,1)S(1)}, u32[]{:S(2)}, u32[]{:S(2)}) collective-permute-start(bf16[256,512]{1,0:T(8,128)(2,1)S(1)} %bitcast_add_fusion.22), channel_id=1, source_target_pairs={{0,4},{4,8},{8,12},{12,14},{14,10},{10,6},{6,2},{2,0},{1,5},{5,9},... | collective-permute-start | bytes 786440 | tf_op jit(solution)/shard_map/ppermute | solution.py:378
  506.0 15.0 %collective-permute-start.62 = (bf16[128,1024]{1,0:T(8,128)(2,1)S(1)}, bf16[128,1024]{1,0:T(8,128)(2,1)S(1)}, u32[]{:S(2)}, u32[]{:S(2)}) collective-permute-start(bf16[128,1024]{1,0:T(8,128)(2,1)S(1)} %bitcast_add_fusion.10), channel_id=1, source_target_pairs={{0,4},{4,8},{8,12},{12,14},{14,10},{10,6},{6,2},{2,0},{1,5},{5,9},... | collective-permute-start | bytes 786440 | tf_op jit(solution)/shard_map/ppermute | solution.py:378
  541.0 15.6 %collective-permute-start.51 = (bf16[256,512]{1,0:T(8,128)(2,1)S(1)}, bf16[256,512]{1,0:T(8,128)(2,1)S(1)}, u32[]{:S(2)}, u32[]{:S(2)}) collective-permute-start(bf16[256,512]{1,0:T(8,128)(2,1)S(1)} %bitcast_add_fusion.13), channel_id=1, source_target_pairs={{0,2},{4,0},{8,4},{12,8},{14,12},{10,14},{6,10},{2,6},{1,3},{5,1},... | collective-permute-start | bytes 786440 | tf_op jit(solution)/shard_map/ppermute | solution.py:378
  628.2 22.7 %collective-permute-start.85 = (bf16[512,2048]{1,0:T(8,128)(2,1)S(1)}, bf16[512,2048]{1,0:T(8,128)(2,1)S(1)}, u32[]{:S(2)}, u32[]{:S(2)}) collective-permute-start(bf16[512,2048]{1,0:T(8,128)(2,1)S(1)} %get-tuple-element.202), channel_id=1, source_target_pairs={{0,16},{16,0},{1,17},{17,1},{2,18},{18,2},{3,19},{19,3},{4,20},{20... | collective-permute-start | bytes 6291464 | tf_op jit(solution)/shard_map/ppermute | solution.py:216
  638.5 16.9 %collective-permute-start.86 = (bf16[1024,1024]{1,0:T(8,128)(2,1)}, bf16[1024,1024]{1,0:T(8,128)(2,1)S(1)}, u32[]{:S(2)}, u32[]{:S(2)}) collective-permute-start(bf16[1024,1024]{1,0:T(8,128)(2,1)} %get-tuple-element.200), channel_id=1, source_target_pairs={{0,16},{16,0},{1,17},{17,1},{2,18},{18,2},{3,19},{19,3},{4,20},{20... | collective-permute-start | bytes 6291464 | tf_op jit(solution)/shard_map/ppermute | solution.py:216
  (188 other events, 1423.1 us)
Sparse Core Ops, SparseCore 0:
  9.6 13.0 all-gather.5
  24.2 21.0 all-gather.7
  46.8 21.0 all-gather.9
  69.8 14.8 all-gather.11
  217.8 161.8 all-reduce.5
  388.4 128.6 all-reduce.3

commit v2 on v1

--- a/solution.py
+++ b/solution.py
@@ -34,9 +34,11 @@
     return lax.dot_general(a, b, (((0,), (0,)), ((), ())), preferred_element_type=f32)
 
 
-def toeplitz(vector, length):
-    wide = jnp.broadcast_to(vector, (length, 2 * length))
-    return pltpu.roll(wide, length, 1, stride=1, stride_axis=0)[:, :length]
+def toeplitz(vector, start, rows, count):
+    length = vector.shape[1] // 2
+    near = vector[:, length - start - rows : length - start + count]
+    wide = jnp.broadcast_to(near, (rows, rows + count))
+    return pltpu.roll(wide, count, 1, stride=1, stride_axis=0)[:, :count]
 
 
 def diagonal_sums(block):
@@ -48,40 +50,40 @@
     return jnp.sum(pltpu.roll(wide, 1, 1, stride=1, stride_axis=0), axis=0, keepdims=True)
 
 
-def allowed_pairs(query_ids, key_ids, causal):
-    allowed = query_ids == key_ids
-    if causal:
-        key = lax.broadcasted_iota(jnp.int32, allowed.shape, 1)
-        query = lax.broadcasted_iota(jnp.int32, allowed.shape, 0)
-        allowed = allowed & (key <= query)
-    return allowed
-
-
 def attend_kernel(causal, biased, q_ref, k_ref, v_ref, query_ids, key_ids, *rest):
     if biased:
         vector, out_ref, log_ref = rest
     else:
         out_ref, log_ref = rest
-    q = q_ref[0] * bf16(HEAD**-0.5)
-    k, v = k_ref[0], v_ref[0]
     lane = lax.broadcasted_iota(jnp.int32, (1, 2 * HEAD), 1)
-    allowed = allowed_pairs(query_ids[0], key_ids[0], causal)
-    out, logs = None, []
-    for head in range(2):
-        mine = (lane // HEAD) == head
-        scores = dot_t(jnp.where(mine, q, jnp.zeros_like(q)), k)
-        if biased:
-            scores = scores + toeplitz(vector[0, head : head + 1], scores.shape[0])
-        scores = jnp.where(allowed, scores, masked_score)
-        peak = jnp.max(scores, axis=1, keepdims=True)
-        exponent = jnp.exp(scores - peak)
-        total = jnp.sum(exponent, axis=1, keepdims=True)
-        weights = (exponent * (1.0 / total)).astype(bf16)
-        mixed = dot_n(weights, v)
-        out = mixed if out is None else jnp.where(mine, mixed, out)
-        logs.append(peak + jnp.log(total))
-    out_ref[...] = out.astype(bf16)
-    log_ref[0, 0] = jnp.concatenate(logs, axis=1)
+    length = q_ref.shape[1]
+    rows = min(256, length) if biased else length
+    for start in range(0, length, rows):
+        count = start + rows if causal else length
+        block = slice(start, start + rows)
+        q = q_ref[0, block] * bf16(HEAD**-0.5)
+        k, v = k_ref[0, :count], v_ref[0, :count]
+        allowed = query_ids[0, block] == key_ids[0, :, :count]
+        if causal:
+            key = lax.broadcasted_iota(jnp.int32, allowed.shape, 1)
+            query = lax.broadcasted_iota(jnp.int32, allowed.shape, 0) + start
+            allowed = allowed & (key <= query)
+        out, logs = None, []
+        for head in range(2):
+            mine = (lane // HEAD) == head
+            scores = dot_t(jnp.where(mine, q, jnp.zeros_like(q)), k)
+            if biased:
+                scores = scores + toeplitz(vector[0, head : head + 1], start, rows, count)
+            scores = jnp.where(allowed, scores, masked_score)
+            peak = jnp.max(scores, axis=1, keepdims=True)
+            exponent = jnp.exp(scores - peak)
+            total = jnp.sum(exponent, axis=1, keepdims=True)
+            weights = (exponent * (1.0 / total)).astype(bf16)
+            mixed = dot_n(weights, v)
+            out = mixed if out is None else jnp.where(mine, mixed, out)
+            logs.append(peak + jnp.log(total))
+        out_ref[block] = out.astype(bf16)
+        log_ref[0, 0, block] = jnp.concatenate(logs, axis=1)
 
 
 def attend_back_kernel(
@@ -94,21 +96,26 @@
     q = q_ref[0] * bf16(HEAD**-0.5)
     k, v, up = k_ref[0], v_ref[0], up_ref[...]
     lane = lax.broadcasted_iota(jnp.int32, (1, 2 * HEAD), 1)
-    allowed = allowed_pairs(query_ids[0], key_ids[0], causal)
+    allowed = key_ids[0] == query_ids[0]
+    if causal:
+        key = lax.broadcasted_iota(jnp.int32, allowed.shape, 0)
+        query = lax.broadcasted_iota(jnp.int32, allowed.shape, 1)
+        allowed = allowed & (key <= query)
     dq = dk = dv = None
     for head in range(2):
         mine = (lane // HEAD) == head
         own_q = jnp.where(mine, q, jnp.zeros_like(q))
         own_up = jnp.where(mine, up, jnp.zeros_like(up))
-        scores = dot_t(own_q, k)
+        scores = dot_t(k, own_q)
         if biased:
-            scores = scores + toeplitz(vector[0, head : head + 1], scores.shape[0])
-        scores = jnp.where(allowed, scores - log_ref[0, 0, :, head : head + 1], masked_score)
+            size = scores.shape[0]
+            scores = scores + toeplitz(vector[0, head : head + 1], 0, size, size)
+        scores = jnp.where(allowed, scores - log_ref[0, 0, head : head + 1, :], masked_score)
         weights = jnp.exp(scores)
-        dots = dot_t(own_up, v)
-        inner = jnp.sum(weights * dots, axis=1, keepdims=True)
+        dots = dot_t(v, own_up)
+        inner = jnp.sum(weights * dots, axis=0, keepdims=True)
         grad = (weights * (dots - inner)).astype(bf16)
-        a, b, c = dot_n(grad, k), t_dot(grad, own_q), t_dot(weights.astype(bf16), own_up)
+        a, b, c = t_dot(grad, k), dot_n(grad, own_q), dot_n(weights.astype(bf16), own_up)
         dq = a if head == 0 else jnp.where(mine, a, dq)
         dk = b if head == 0 else dk + b
         dv = c if head == 0 else dv + c
@@ -117,6 +124,10 @@
     dq_ref[0] = (dq * (HEAD**-0.5)).astype(bf16)
     dk_ref[0] = dk.astype(bf16)
     dv_ref[0] = dv.astype(bf16)
+
+
+def turned(vector):
+    return jnp.roll(jnp.flip(vector, axis=-1), 1, axis=-1)
 
 
 little = pl.CostEstimate(flops=1, bytes_accessed=1, transcendentals=1)
@@ -142,7 +153,7 @@
     if biased:
         specs.append(pl.BlockSpec((1, 2, 2 * length), lambda r, p: (p, 0, 0)))
         more = (vector.reshape(pairs, 2, 2 * length),)
-    return pl.pallas_call(
+    mixed, logs = pl.pallas_call(
         functools.partial(attend_kernel, causal, biased),
         grid=(rows, pairs),
         in_specs=specs,
@@ -157,6 +168,7 @@
         compiler_params=kernel_params,
         cost_estimate=little,
     )(query, stored, stored, query_ids[:, :, None], key_ids[:, None, :], *more)
+    return (mixed, logs.swapaxes(2, 3))
 
 
 def attend_back(query, stored, parts, query_ids, key_ids, vector, causal, up, logs):
@@ -166,17 +178,19 @@
     biased = vector is not None
     each = pl.BlockSpec((1, length, 2 * HEAD), lambda r, p: (0, r, p))
     shape = jax.ShapeDtypeStruct((1, rows * length, width), bf16)
-    specs = operand_specs(parts, length) + [
+    specs = operand_specs(parts, length)[:3] + [
+        pl.BlockSpec((1, 1, length), lambda r, p: (r, 0, 0)),
+        pl.BlockSpec((1, length, 1), lambda r, p: (r, 0, 0)),
         pl.BlockSpec((length, 2 * HEAD), lambda r, p: (r, p)),
-        pl.BlockSpec((1, 1, length, 2), lambda r, p: (r, p, 0, 0)),
+        pl.BlockSpec((1, 1, 2, length), lambda r, p: (r, p, 0, 0)),
     ]
     out_specs, out_shape, more = [each] * 3, [shape] * 3, ()
     if biased:
         specs.append(pl.BlockSpec((1, 2, 2 * length), lambda r, p: (p, 0, 0)))
-        more = (vector.reshape(pairs, 2, 2 * length),)
+        more = (turned(vector).reshape(pairs, 2, 2 * length),)
         out_specs.append(pl.BlockSpec((1, 1, 2, 2 * length), lambda r, p: (r, p, 0, 0)))
         out_shape.append(jax.ShapeDtypeStruct((rows, pairs, 2, 2 * length), f32))
-    return pl.pallas_call(
+    result = pl.pallas_call(
         functools.partial(attend_back_kernel, causal, biased),
         grid=(rows, pairs),
         in_specs=specs,
@@ -184,7 +198,8 @@
         out_shape=out_shape,
         compiler_params=kernel_params,
         cost_estimate=little,
-    )(query, stored, stored, query_ids[:, :, None], key_ids[:, None, :], up, logs, *more)
+    )(query, stored, stored, query_ids[:, None, :], key_ids[:, :, None], up, logs, *more)
+    return list(result[:3]) + [turned(part) for part in result[3:]]
 
 
 def bucket_onehot(length, causal):
@@ -248,26 +263,47 @@
     return lax.dynamic_slice_in_dim(full, lax.axis_index("tensor") * width, width, 1)
 
 
+def exchange(low):
+    if lax.axis_size("tensor") == 2:
+        return (low, swap_tensor(low))
+    return (lax.psum(low, "tensor"), jnp.zeros_like(low))
+
+
+def total(parts):
+    return parts[0].astype(f32) + parts[1].astype(f32)
+
+
 def total_features(low):
+    return total(exchange(low))
+
+
+def scatter_begin(lows):
     if lax.axis_size("tensor") == 2:
-        return low.astype(f32) + swap_tensor(low).astype(f32)
-    return lax.psum(low, "tensor").astype(f32)
-
-
-def scatter_features(low):
+        width = lows[0].shape[1] // 2
+        first = lax.axis_index("tensor") == 0
+        give = jnp.stack([jnp.where(first, low[:, width:], low[:, :width]) for low in lows])
+        keep = [jnp.where(first, low[:, :width], low[:, width:]) for low in lows]
+        return (keep, swap_tensor(give))
+    return (
+        [lax.psum_scatter(low, "tensor", scatter_dimension=1, tiled=True) for low in lows],
+        None,
+    )
+
+
+def scatter_end(kept, received):
+    if received is None:
+        return [part.astype(f32) for part in kept]
+    return [part.astype(f32) + received[index].astype(f32) for index, part in enumerate(kept)]
+
+
+def total_begin(values):
     if lax.axis_size("tensor") == 2:
-        width = low.shape[1] // 2
-        first = lax.axis_index("tensor") == 0
-        left, right = low[:, :width], low[:, width:]
-        received = swap_tensor(jnp.where(first, right, left))
-        return jnp.where(first, left, right).astype(f32) + received.astype(f32)
-    return lax.psum_scatter(low, "tensor", scatter_dimension=1, tiled=True).astype(f32)
-
-
-def total_tokens(values):
-    if lax.axis_size("tensor") == 2:
-        return values + swap_tensor(values.reshape(-1, 128)).reshape(-1)
-    return lax.psum(values, "tensor")
+        return (values, swap_tensor(values.reshape(-1, 128)))
+    return (lax.psum(values, "tensor"), None)
+
+
+def total_end(values, received):
+    return values if received is None else values + received.reshape(values.shape)
 
 
 def smooth(values):
@@ -321,11 +357,10 @@
     return sum(matmul_t(part, mixing[index]) for index, part in enumerate(parts)).astype(bf16)
 
 
-def input_gradient_of(hidden, gain, inverse, partial_value, grad):
-    inner = total_tokens(jnp.sum(partial_value.astype(f32) * gain * hidden, axis=1))[:, None]
-    upstream = scatter_features(partial_value)
+def input_gradient_of(hidden, gain, inverse, upstream, inner, grad):
     own, own_gain = own_features(hidden), own_features(gain[None])
-    result = inverse * upstream * own_gain - own * (inverse * inverse * inverse * inner / D)
+    result = inverse * upstream * own_gain
+    result = result - own * (inverse * inverse * inverse * inner[:, None] / D)
     return (result + own_features(grad), gain_gradient(own, inverse, upstream))
 
 
@@ -344,6 +379,15 @@
     return (before_grad, matmul_t(before_grad, expanding).astype(bf16))
 
 
+def weight_own(encoder_pair, decoder_pair):
+    first = lax.axis_index("section") == 0
+    keep = [jnp.where(first, e, d) for e, d in zip(encoder_pair, decoder_pair)]
+    give = [jnp.where(first, d, e) for e, d in zip(encoder_pair, decoder_pair)]
+    received = swap_section(weight_grad(*give))
+    total = jnp.einsum("tc,td->cd", *keep, preferred_element_type=f32) + received.astype(f32)
+    return total.astype(bf16)
+
+
 def section_half(value):
     half = value.shape[0] // 2
     first = lax.axis_index("section") == 0
@@ -361,13 +405,12 @@
     return lax.psum(values, ("z", "y"))
 
 
-def sum_rows_small(value):
-    if lax.axis_size("z") != 4 or lax.axis_size("y") != 2:
-        return lax.psum(value, ("z", "y"))
-    value = value.reshape(-1, 128)
-    value = value + lax.ppermute(value, "y", [(0, 1), (1, 0)])
-    value = value + lax.ppermute(value, "z", [(i, i ^ 1) for i in range(4)])
-    return value + lax.ppermute(value, "z", [(i, i ^ 2) for i in range(4)])
+def swap_y(value):
+    return lax.ppermute(value, "y", [(0, 1), (1, 0)])
+
+
+def swap_z(value, distance):
+    return lax.ppermute(value, "z", [(i, i ^ distance) for i in range(4)])
 
 
 ring = [2 * z for z in range(4)] + [2 * z + 1 for z in reversed(range(4))]
@@ -378,54 +421,58 @@
     return lax.ppermute(value, ("z", "y"), pairs)
 
 
-def ring_pieces(groups):
-    z, y = lax.axis_index("z"), lax.axis_index("y")
-    place = jnp.where(y == 0, z, 7 - z)
+class RingSum:
+
     ways = (1, -1)
 
-    def piece(value, index):
+    def __init__(self, groups):
+        self.groups, self.count = groups, 0
+        self.around = lax.axis_size("z") == 4 and lax.axis_size("y") == 2
+        z, y = lax.axis_index("z"), lax.axis_index("y")
+        self.place = jnp.where(y == 0, z, 7 - z)
+        if self.around:
+            self.moving = [[self.piece(v, self.place) for v in pair] for pair in groups]
+
+    def piece(self, value, index):
         return lax.dynamic_index_in_dim(value, lax.rem(index + 16, 8), 0, keepdims=False)
 
-    def put(value, part, index):
+    def put(self, value, part, index):
         return lax.dynamic_update_index_in_dim(value, part, lax.rem(index + 16, 8), 0)
 
-    return place, ways, piece, put
-
-
-def ring_start(groups):
-    place, ways, piece, put = ring_pieces(groups)
-    moving = [[piece(value, place) for value in pair] for pair in groups]
-    return ring_step(groups, moving, 0)
-
-
-def ring_step(groups, moving, step):
-    place, ways, piece, put = ring_pieces(groups)
-    moving = list(moving)
-    for g, pair in enumerate(groups):
-        received = [along_ring(moving[g][w], ways[w]) for w in range(2)]
-        moving[g] = [
-            received[w] + piece(pair[w], place - ways[w] * (step + 1)) for w in range(2)
+    def step(self, group=0):
+        if not self.around:
+            return ()
+        place, ways, step = self.place, self.ways, self.count % 7
+        if self.count == 7:
+            self.totals = [
+                [self.put(v, m, place + way) for v, m, way in zip(pair, moving, ways)]
+                for pair, moving in zip(self.groups, self.moving)
+            ]
+        self.moving = [
+            [along_ring(m, way) for m, way in zip(moving, ways)] for moving in self.moving
         ]
-    return moving
-
-
-def ring_finish(groups, moving):
-    place, ways, piece, put = ring_pieces(groups)
-    for step in range(1, 7):
-        moving = ring_step(groups, moving, step)
-    totals = [
-        [put(pair[w], moving[g][w], place + ways[w]) for w in range(2)]
-        for g, pair in enumerate(groups)
-    ]
-    for step in range(7):
-        for g, pair in enumerate(totals):
-            moving[g] = [along_ring(moving[g][w], ways[w]) for w in range(2)]
-            totals[g] = [
-                put(totals[g][w], moving[g][w], place - ways[w] * step) for w in range(2)
+        if self.count < 7:
+            self.moving = [
+                [
+                    m + self.piece(v, place - way * (step + 1))
+                    for v, m, way in zip(pair, moving, ways)
+                ]
+                for pair, moving in zip(self.groups, self.moving)
             ]
-        if step == 4:
-            late = moving
-    return (totals, late)
+        else:
+            self.totals = [
+                [self.put(t, m, place - way * step) for t, m, way in zip(pair, moving, ways)]
+                for pair, moving in zip(self.totals, self.moving)
+            ]
+        self.count += 1
+        return self.moving[group]
+
+    def sums(self):
+        if not self.around:
+            return sum_rows(self.groups)
+        while self.count < 14:
+            self.step()
+        return self.totals
 
 
 def body(
@@ -457,11 +504,6 @@
         give = lax.dynamic_slice_in_dim(value[0], (1 - section) * rows, rows, 0)
         return pick(mine.reshape(tokens, -1), swap_section(give).reshape(tokens, -1))
 
-    def all_layer_rows(encoder_value, decoder_value):
-        mine = jnp.where(first, encoder_value, decoder_value)
-        other = swap_section(jnp.where(first, decoder_value, encoder_value))
-        return ordered(section, mine, other, 0).reshape(1, all_rows, length, local_width)
-
     encoder_half, decoder_half = own_rows(layer_inputs)
     mixing = both(attention_in[0].transpose(1, 0, 2))
     encoder_in = gather_features(encoder_half).astype(f32)
@@ -475,8 +517,8 @@
         "section",
     )
     encoder_cotangent, decoder_cotangent = own_rows(output_cotangents)
-    later_halves = hold(jnp.stack([decoder_half, encoder_cotangent, decoder_cotangent]), encoder_in)
-    later_others = swap_tensor(later_halves) if lax.axis_size("tensor") == 2 else later_halves
+    decoder_halves = hold(jnp.stack([decoder_half, decoder_cotangent]), encoder_in)
+    decoder_others = swap_tensor(decoder_halves) if lax.axis_size("tensor") == 2 else decoder_halves
     encoder_in = hold(encoder_in, mixing)
     ids = lax.dynamic_slice_in_dim(segment_ids, section * rows, rows, 1)
     encoder_ids, decoder_ids = ids[0], ids[1]
@@ -489,8 +531,8 @@
     x1_part, encoder_self = self_forward(
         encoder_in, gains[0][0], mixing[0], projecting[0], vectors[0], encoder_ids, False
     )
-    later_halves, later_others = hold((later_halves, later_others), x1_part)
-    decoder_in, encoder_cotangent, decoder_cotangent = joined_features(later_halves, later_others, 2)
+    decoder_halves, decoder_others = hold((decoder_halves, decoder_others), x1_part)
+    decoder_in, decoder_cotangent = joined_features(decoder_halves, decoder_others, 2)
     decoder_in = decoder_in.astype(f32)
     z1_part, decoder_self = self_forward(
         decoder_in, gains[1][0], mixing[1], projecting[1], vectors[1], decoder_ids, True
@@ -502,6 +544,7 @@
     cross_in, cross_inverse = norm_forward(z1, gains[1][1])
     query = matmul(cross_in, crossing[1][0]).astype(bf16)[None]
     x2 = x1 + total_features(x2_part)
+    encoder_cotangent = gather_features(hold(encoder_cotangent, x2))
     memory_in, memory_inverse = norm_forward(x2, gains[0][2])
     memory = jnp.einsum("td,edc->etc", memory_in, crossing[0], preferred_element_type=f32)
     memory = memory.astype(bf16)
@@ -509,6 +552,7 @@
         query, memory, (0, 0, 1), decoder_ids, encoder_ids, None, False
     )
     z2_part = matmul_t(cross_mixed, crossing[1][1]).astype(bf16)
+    z2_part, encoder_cotangent = lax.optimization_barrier((z2_part, encoder_cotangent))
     z2 = z1 + total_features(z2_part)
     activated, decoder_dense = dense_forward(z2, gains[1][2], expanding[1], contracting[1])
 
@@ -539,22 +583,24 @@
         [weight_grad(memory_in, dkeys[0]), weight_grad(memory_in, dvalues[0])]
     )
 
+    cross_sum = section_own(encoder_cross, decoder_cross)
     memory_up, decoder_cross, encoder_cross = lax.optimization_barrier(
         (memory_up, decoder_cross, encoder_cross)
     )
 
     dx2 = norm_backward(x2, gains[0][2], memory_inverse, memory_up) + encoder_cotangent.astype(f32)
-    query_up = total_features(hold(query_part, memory_up))
+    query_own, query_other = exchange(hold(query_part, memory_up))
     low = dx2.astype(bf16)
     before_grad, part = dense_backward(expanding[0], contracting[0], encoder_dense, low)
     upstream = total_features(part)
 
-    before_grad, activated, normed, low, query_up = hold(
-        (before_grad, encoder_dense[3], encoder_dense[0], low, query_up), part
+    before_grad, activated, normed, low, query_own = hold(
+        (before_grad, encoder_dense[3], encoder_dense[0], low, query_own), part
     )
     encoder_contract = weight_grad(activated, low)
     encoder_expand = weight_grad(normed, before_grad)
-    query_up = hold(query_up, encoder_contract, encoder_expand)
+    query_own = hold(query_own, encoder_contract, encoder_expand)
+    query_up = total((query_own, query_other))
     dz1 = norm_backward(z1, gains[1][1], cross_inverse, query_up) + dz2
     decoder_low = dz1.astype(bf16)
     decoder_dqkv, decoder_diagonals = self_backward(
@@ -569,18 +615,16 @@
     )
 
     decoder_dqkv, decoder_low, low = hold((decoder_dqkv, decoder_low, low), encoder_dqkv)
-    encoder_mixing = jnp.stack([weight_grad(encoder_self[0], value) for value in encoder_dqkv])
-    decoder_mixing = jnp.stack([weight_grad(decoder_self[0], value) for value in decoder_dqkv])
-    encoder_projecting = weight_grad(encoder_self[3], low)
-    decoder_projecting = weight_grad(decoder_self[3], decoder_low)
-
-    encoder_dqkv, decoder_dqkv, activated = hold(
-        (encoder_dqkv, decoder_dqkv, decoder_dense[3]),
-        encoder_mixing, decoder_mixing, encoder_projecting, decoder_projecting,
-    )
+    mixing_sum = [
+        weight_own((encoder_self[0], e), (decoder_self[0], d))
+        for e, d in zip(encoder_dqkv, decoder_dqkv)
+    ]
+    projecting_sum = weight_own((encoder_self[3], low), (decoder_self[3], decoder_low))
+
+    encoder_dqkv, decoder_dqkv = hold((encoder_dqkv, decoder_dqkv), mixing_sum, projecting_sum)
+    out_part = matmul(decoder_dense[3], contracting[1]).astype(bf16)
     encoder_part = mixing_back(encoder_dqkv, mixing[0])
     decoder_part = mixing_back(decoder_dqkv, mixing[1])
-    out_part = matmul(activated, contracting[1]).astype(bf16)
 
     def narrowed(value, width):
         return jnp.concatenate(
@@ -596,40 +640,54 @@
 
     contract_sum = section_half(encoder_contract)
     expand_sum = section_half(encoder_expand)
-    mixing_sum = section_own(encoder_mixing, decoder_mixing)
-    projecting_sum = section_own(encoder_projecting, decoder_projecting)
+    mixing_sum = jnp.stack(mixing_sum)
 
     narrow = mixing_sum.shape[2]
-    groups, encoder_part, decoder_part, out_part = lax.optimization_barrier((
+    inners = jnp.stack(
         [
-            [contract_sum, expand_sum],
+            jnp.sum(part.astype(f32) * gain[0] * hidden, axis=1)
+            for part, gain, hidden in zip(
+                (encoder_part, decoder_part), gains, (encoder_in, decoder_in)
+            )
+        ]
+    )
+    kept, received = scatter_begin((encoder_part, decoder_part, out_part))
+    inners, other_inners = total_begin(inners)
+    groups, kept, inners = lax.optimization_barrier(
+        (
             [
-                mixing_sum[:2].reshape(-1, narrow),
-                jnp.concatenate([mixing_sum[2], narrowed(projecting_sum, narrow)]),
+                [contract_sum, expand_sum],
+                [
+                    mixing_sum[:2].reshape(-1, narrow),
+                    jnp.concatenate([mixing_sum[2], narrowed(projecting_sum, narrow)]),
+                ],
             ],
-        ],
-        encoder_part, decoder_part, out_part,
-    ))
+            kept,
+            inners,
+        )
+    )
     first_sums = hold(first_sums, groups)
-    cross_sum = section_own(encoder_cross, decoder_cross)
     cross_sum = sum_rows(hold(cross_sum, first_sums))
-    groups = [[value.reshape(8, -1, value.shape[1]) for value in pair] for pair in groups]
-    whole_ring = lax.axis_size("z") == 4 and lax.axis_size("y") == 2
-    moving = ring_start(groups) if whole_ring else groups
-
-    encoder_part, decoder_part, out_part, memory_up, upstream = hold(
-        (encoder_part, decoder_part, out_part, memory_up, upstream), moving
-    )
+    ring_sum = RingSum(
+        [[value.reshape(8, -1, value.shape[1]) for value in pair] for pair in groups]
+    )
+    ring_sum.step()
+    ring_sum.step()
+    now = ring_sum.step()
+
+    received, other_inners = hold((received, other_inners), now)
+    inners = total_end(inners, other_inners)
+    encoder_up, decoder_up, out_sum = scatter_end(kept, received)
     encoder_gain_two = gain_gradient(x2, memory_inverse, memory_up)
     encoder_gain_one = gain_gradient(x1, encoder_dense[1], upstream)
     gain_one = gain_gradient(z1, cross_inverse, query_up)
     encoder_grad, encoder_gain_zero = input_gradient_of(
-        encoder_in, gains[0][0], encoder_self[1], encoder_part, dx1
+        encoder_in, gains[0][0], encoder_self[1], encoder_up, inners[0], dx1
     )
     decoder_grad, gain_zero = input_gradient_of(
-        decoder_in, gains[1][0], decoder_self[1], decoder_part, dz1
-    )
-    decoder_out = own_features(z2) + scatter_features(out_part)
+        decoder_in, gains[1][0], decoder_self[1], decoder_up, inners[1], dz1
+    )
+    decoder_out = own_features(z2) + out_sum
 
     def small(gain_zero, gain_one, gain_two, diagonals, onehot):
         ones = [gain_zero[None], own_features(gain_one[None]), own_features(gain_two[None])]
@@ -637,22 +695,39 @@
         table = jnp.einsum("hj,jb->bh", summed, onehot, precision=highest)
         return jnp.concatenate(ones + [table.reshape(1, -1)], axis=1)
 
-    decoder_small = small(gain_zero, gain_one, gain_two, decoder_diagonals, onehots[1])
-    encoder_small = small(
-        encoder_gain_zero, encoder_gain_one, encoder_gain_two, encoder_diagonals, onehots[0]
-    )
-    small_sum = sum_rows_small(section_own(encoder_small, decoder_small))
-    if whole_ring:
-        totals, late = ring_finish(groups, moving)
+    small_sum = section_own(
+        small(
+            encoder_gain_zero, encoder_gain_one, encoder_gain_two, encoder_diagonals, onehots[0]
+        ),
+        small(gain_zero, gain_one, gain_two, decoder_diagonals, onehots[1]),
+    )
+    mine, give = pick(
+        jnp.stack([own_features(x2), encoder_grad]), jnp.stack([decoder_out, decoder_grad])
+    )
+    other = swap_section(give)
+    ring_sum.step()
+    ring_sum.step()
+    now = ring_sum.step()
+    layer_outputs, input_gradient = ordered(section, mine, hold(other, now), 1).reshape(
+        2, 1, all_rows, length, local_width
+    )
+    if ring_sum.around:
+        small_sum = small_sum.reshape(-1, 128)
+        small_sum = small_sum + hold(swap_y(hold(small_sum, now)), ring_sum.step())
+        ring_sum.step()
+        small_sum = small_sum + hold(swap_z(small_sum, 1), ring_sum.step())
+        ring_sum.step()
+        small_sum = small_sum + hold(swap_z(small_sum, 2), ring_sum.step())
+        small_sum = small_sum.reshape(-1)
     else:
-        totals = late = sum_rows(groups)
+        small_sum = sum_rows(small_sum).reshape(-1)
+    late = ring_sum.step()
     (contract_sum, expand_sum), (query_key_sum, last) = [
-        [value.reshape(-1, value.shape[2]) for value in pair] for pair in totals
+        [value.reshape(-1, value.shape[2]) for value in pair] for pair in ring_sum.sums()
     ]
     mixing_sum = jnp.concatenate([query_key_sum, last[:D]]).reshape(3, D, narrow)
     projecting_sum = widened(last[D:], D)
     cross_sum = hold(cross_sum, late)
-    small_sum = small_sum.reshape(-1)
 
     def whole(encoder_sum, decoder_sum):
         mine = jnp.where(first, encoder_sum, decoder_sum)
@@ -661,8 +736,8 @@
 
     width = D // lax.axis_size("tensor")
     return (
-        all_layer_rows(own_features(x2), decoder_out),
-        all_layer_rows(encoder_grad, decoder_grad),
+        layer_outputs,
+        input_gradient,
         mixing_sum.astype(f32).transpose(1, 0, 2)[None],
         projecting_sum.astype(f32)[None],
         cross_sum.astype(f32).transpose(1, 0, 2)[None],

time: 677 us -> 647 us (0.956)
  waiting for transfers between devices: 199 us -> 180 us
  matrix products: 95 us -> 105 us
  other arithmetic: 129 us -> 119 us
  starting transfers between devices: 106 us -> 97.7 us
    ppermute x16 -> x14, waiting for transfers between devices: 86.8 us -> 47.5 us  [swap_tensor(): return lax.ppermute(value, 'tensor', [(0, 1), (1, 0)])]
    ppermute x56, waiting for transfers between devices: 97 us -> 130 us  [along_ring(): return lax.ppermute(value, ('z', 'y'), pairs)]
    ppermute x56, starting transfers between devices: 56.8 us -> 43.8 us  [along_ring(): return lax.ppermute(value, ('z', 'y'), pairs)]
    ppermute x3, waiting for transfers between devices: 12 us -> 0.01 us  [the longest x2 0.01 us: swap_z(): return lax.ppermute(value, 'z', [(i, i ^ distance) for i in range(4)])]
    dot_general x0 -> x4, matrix products: none -> 9.75 us  [weight_own(): jnp.einsum('tc,td->cd', *keep, preferred_element_type=f32)]
    unnamed x284 -> x320, local copies, waits for them, and re-layouts: 38.2 us -> 29.4 us
    another operation x6 -> x8, local copies, waits for them, and re-layouts: 1.56 us -> 9.03 us
    add x35, other arithmetic: 27.1 us -> 19.8 us  [the longest x28 16.3 us: step(): m + self.piece(v, place - way * (step + 1))]
  transfers between devices with their start and end apart: 97 -> 96, of which waited for: 39 -> 31; matrix products, arithmetic and copies ran while one was open for 33% -> 37% of each run, Pallas kernels for 9% -> 10%
where the time goes in v2:
time: 647 us; the launch traced here: 637 us
  waiting for transfers between devices  180 us (28%)
  other arithmetic  119 us (18%)
  matrix products  105 us (16%)
  starting transfers between devices  97.7 us (15%)
  Pallas kernels  61.5 us (10%)
  local copies, waits for them, and re-layouts  57 us (9%)
  between operations  17.3 us (3%)
    ppermute x56, waiting for transfers between devices, along_ring(): return lax.ppermute(value, ('z', 'y'), pairs)  130 us
    ppermute x14, waiting for transfers between devices, swap_tensor(): return lax.ppermute(value, 'tensor', [(0, 1), (1, 0)])  47.5 us
    ppermute x56, starting transfers between devices, along_ring(): return lax.ppermute(value, ('z', 'y'), pairs)  43.8 us
    ppermute x17, starting transfers between devices, swap_section(): return lax.ppermute(value, 'section', [(0, 1), (1, 0)])  34.8 us
    pallas_call x3, Pallas kernels, attend_back(): pl.pallas_call(functools.partial(attend_back_kernel, causal, biased), gri...  34.5 us
    dot_general x8, matrix products, matmul(): return jnp.dot(a, b, preferred_element_type=f32)  34.2 us
    dot_general x16, matrix products, matmul_t(): return jnp.einsum('tc,dc->td', a, b, preferred_element_type=f32)  31.1 us
    unnamed x320, local copies, waits for them, and re-layouts  29.4 us
  transfers between devices with their start and end apart: 96, of which 31 were waited for; matrix products, arithmetic and copies ran while one was open for 37% of the time, Pallas kernels for 10%

profile of v2, /device:TPU:1, one launch (start us, length us, event | category | flops | bytes accessed | tf_op | source)
XLA Modules:
  0.0 637.3 jit_solution(5935715583499297990)
XLA Ops:
  22.8 11.5 %collective-permute-done.1 = bf16[512,512]{1,0:T(8,128)(2,1)S(1)} collective-permute-done((bf16[512,512]{1,0:T(8,128)(2,1)S(1)}, bf16[512,512]{1,0:T(8,128)(2,1)S(1)}, u32[]{:S(2)}, u32[]{:S(2)}) %collective-permute-start.1) | collective-permute-done | bytes 524320 | tf_op jit(solution)/shard_map/ppermute | solution.py:235
  35.4 6.2 broadcast_select_fusion
  45.1 11.8 %shard_map.187 = (bf16[512,512]{1,0:T(8,128)(2,1)S(1)}, f32[1,4,512,2]{3,2,1,0:T(8,128)S(1)}) custom-call(bf16[3,512,512]{2,1,0:T(8,128)(2,1)S(1)} %fusion.33.q_ref.k_ref.v_ref, bf16[3,512,512]{2,1,0:T(8,128)(2,1)S(1)} %fusion.33.q_ref.k_ref.v_ref, bf16[3,512,512]{2,1,0:T(8,128)(2,1)S(1)} %fusion.33.q_ref.k_ref.v_ref, ...), custom_call_target="tpu_custom_call" | custom-call | flops 1 | bytes 1 | tf_op jit(solution)/shard_map/pallas_call | solution.py:156
  61.5 4.3 maximum_select_fusion.3
  68.1 9.1 %shard_map.188 = (bf16[512,512]{1,0:T(8,128)(2,1)S(1)}, f32[1,4,512,2]{3,2,1,0:T(8,128)S(1)}) custom-call(bf16[3,512,512]{2,1,0:T(8,128)(2,1)S(1)} %fusion.34.q_ref.k_ref.v_ref, bf16[3,512,512]{2,1,0:T(8,128)(2,1)S(1)} %fusion.34.q_ref.k_ref.v_ref, bf16[3,512,512]{2,1,0:T(8,128)(2,1)S(1)} %fusion.34.q_ref.k_ref.v_ref, s32[1,512,1]{2,1,0:T(8,128)S(1)} %copy-done.2, ...), custom_call_target="tpu_custom_call" | custom-call | flops 1 | bytes 1 | tf_op jit(solution)/shard_map/pallas_call | solution.py:156
  79.3 4.8 collective-permute-done.5
  87.3 8.3 %multiply_convert_fusion.1 = (bf16[512,2048]{1,0:T(8,128)(2,1)}, f32[512,2048]{1,0:T(8,128)}) fusion(bf16[512,1024]{1,0:T(8,128)(2,1)} %multiply_convert_fusion.5, bf16[2,1024,2048]{2,1,0:T(8,128)(2,1)} %all-gather.8.cloned.1.call-done), kind=kOutput, calls=%fused_computation.30 | convolution fusion | flops 2156920832 | bytes 11534336 | tf_op jit(solution)/shard_map/dot_general | solution.py:314
  95.6 6.3 fusion.40
  106.7 3.4 multiply_reduce_fusion.10
  112.9 16.2 %collective-permute-done.8 = bf16[512,1024]{1,0:T(8,128)(2,1)} collective-permute-done((bf16[512,1024]{1,0:T(8,128)(2,1)}, bf16[512,1024]{1,0:T(8,128)(2,1)}, u32[]{:S(2)}, u32[]{:S(2)}) %collective-permute-start.8) | collective-permute-done | bytes 1048608 | tf_op jit(solution)/shard_map/ppermute | solution.py:235
  135.3 6.0 shard_map.189
  168.9 8.1 %multiply_convert_fusion = (bf16[512,2048]{1,0:T(8,128)(2,1)S(1)}, f32[512,2048]{1,0:T(8,128)}) fusion(bf16[512,1024]{1,0:T(8,128)(2,1)S(1)} %multiply_convert_fusion.2, bf16[2,1024,2048]{2,1,0:T(8,128)(2,1)} %all-gather.8.cloned.1.call-done), kind=kOutput, calls=%fused_computation.29 | convolution fusion | flops 2156920832 | bytes 11534336 | tf_op jit(solution)/shard_map/dot_general | solution.py:314
  177.1 6.9 %fusion.13 = bf16[512,2048]{1,0:T(8,128)(2,1)S(1)} fusion(f32[512,2048]{1,0:T(8,128)} %get-tuple-element.243, bf16[2,2048,1024]{2,1,0:T(8,128)(2,1)S(1)} %bitcast.585, bf16[2,512,1024]{2,1,0:T(8,128)(2,1)S(1)} %copy-done.41), kind=kOutput, calls=%fused_computation.18 | convolution fusion | flops 2168455168 | bytes 11534336 | tf_op jit(solution)/shard_map/tc,dc->td/dot_general | solution.py:318
  190.5 3.9 collective-permute-start.13
  200.5 6.9 %collective-permute-done.12 = bf16[512,1024]{1,0:T(8,128)(2,1)S(1)} collective-permute-done((bf16[512,1024]{1,0:T(8,128)(2,1)S(1)}, bf16[512,1024]{1,0:T(8,128)(2,1)S(1)}, u32[]{:S(2)}, u32[]{:S(2)}) %collective-permute-start.12) | collective-permute-done | bytes 1048608 | tf_op jit(solution)/shard_map/ppermute | solution.py:235
  216.6 9.7 %shard_map.190 = (bf16[1,512,512]{2,1,0:T(8,128)(2,1)S(1)}, bf16[1,512,512]{2,1,0:T(8,128)(2,1)S(1)}, bf16[1,512,512]{2,1,0:T(8,128)(2,1)S(1)}) custom-call(bf16[1,512,512]{2,1,0:T(8,128)(2,1)S(1)} %copy-done.6, bf16[2,512,512]{2,1,0:T(8,128)(2,1)S(1)} %copy-done.1, bf16[2,512,512]{2,1,0:T(8,128)(2,1)S(1)} %copy-done.1, ...), custom_call_target="tpu_custom_call" | custom-call | flops 1 | bytes 1 | tf_op jit(solution)/shard_map/pallas_call | solution.py:193
  234.3 4.9 collective-permute-start.67
  242.1 5.9 collective-permute-done.15
  251.8 4.9 fusion.6
  266.7 6.4 %collective-permute-start.16 = (bf16[1024,1024]{1,0:T(8,128)(2,1)}, bf16[1024,1024]{1,0:T(8,128)(2,1)}, u32[]{:S(2)}, u32[]{:S(2)}) collective-permute-start(bf16[1024,1024]{1,0:T(8,128)(2,1)} %broadcast_select_fusion.4), channel_id=1, source_target_pairs={{0,16},{16,0},{1,17},{17,1},{2,18},{18,2},{3,19},{19,3},{4,20},{20... | collective-permute-start | bytes 6291464 | tf_op jit(solution)/shard_map/ppermute | solution.py:231
  280.6 3.7 multiply_reduce_fusion.1
  284.3 4.2 fusion.130
  289.6 12.5 %shard_map.191 = (bf16[1,512,512]{2,1,0:T(8,128)(2,1)S(1)}, bf16[1,512,512]{2,1,0:T(8,128)(2,1)S(1)}, bf16[1,512,512]{2,1,0:T(8,128)(2,1)S(1)}, f32[1,4,2,1024]{3,2,1,0:T(2,128)S(1)}) custom-call(bf16[3,512,512]{2,1,0:T(8,128)(2,1)S(1)} %fusion.34.q_ref.k_ref.v_ref, bf16[3,512,512]{2,1,0:T(8,128)(2,1)S(1)} %fusion.34.q_ref.k_ref.v_ref, ...), custom_call_target="tpu_custom_call" | custom-call | flops 1 | bytes 1 | tf_op jit(solution)/shard_map/pallas_call | solution.py:193
  310.6 12.3 %shard_map.192 = (bf16[1,512,512]{2,1,0:T(8,128)(2,1)S(1)}, bf16[1,512,512]{2,1,0:T(8,128)(2,1)S(1)}, bf16[1,512,512]{2,1,0:T(8,128)(2,1)S(1)}, f32[1,4,2,1024]{3,2,1,0:T(2,128)S(1)}) custom-call(bf16[3,512,512]{2,1,0:T(8,128)(2,1)S(1)} %fusion.33.q_ref.k_ref.v_ref, bf16[3,512,512]{2,1,0:T(8,128)(2,1)S(1)} %fusion.33.q_ref.k_ref.v_ref, ...), custom_call_target="tpu_custom_call" | custom-call | flops 1 | bytes 1 | tf_op jit(solution)/shard_map/pallas_call | solution.py:193
  338.8 4.7 select_add_fusion.1
  343.5 3.5 select_add_fusion.2
  378.4 4.1 collective-permute-done.26
  384.8 4.3 collective-permute-done.53
  390.7 3.6 collective-permute-done.27
  396.5 4.2 collective-permute-done.54
  407.3 3.9 collective-permute-done.55
  430.2 6.8 %collective-permute-done.37 = bf16[64,2048]{1,0:T(8,128)(2,1)S(1)} collective-permute-done((bf16[64,2048]{1,0:T(8,128)(2,1)S(1)}, bf16[64,2048]{1,0:T(8,128)(2,1)S(1)}, u32[]{:S(2)}, u32[]{:S(2)}) %collective-permute-start.37) | collective-permute-done | bytes 262176 | tf_op jit(solution)/shard_map/ppermute | solution.py:421
  438.0 16.7 %collective-permute-done.57 = bf16[256,512]{1,0:T(8,128)(2,1)S(1)} collective-permute-done((bf16[256,512]{1,0:T(8,128)(2,1)S(1)}, bf16[256,512]{1,0:T(8,128)(2,1)S(1)}, u32[]{:S(2)}, u32[]{:S(2)}) %collective-permute-start.57) | collective-permute-done | bytes 262176 | tf_op jit(solution)/shard_map/ppermute | solution.py:421
  467.1 7.5 %collective-permute-start.32 = (f32[2,512,512]{2,1,0:T(8,128)}, f32[2,512,512]{2,1,0:T(8,128)}, u32[]{:S(2)}, u32[]{:S(2)}) collective-permute-start(f32[2,512,512]{2,1,0:T(8,128)} %get-tuple-element.215), channel_id=1, source_target_pairs={{0,16},{16,0},{1,17},{17,1},{2,18},{18,2},{3,19},{19,3},{4,20},{20... | collective-permute-start | bytes 6291464 | tf_op jit(solution)/shard_map/ppermute | solution.py:231
  483.4 3.7 collective-permute-done.59
  487.2 5.6 collective-permute-done.74
  497.8 12.0 %collective-permute-done.69 = bf16[128,1024]{1,0:T(8,128)(2,1)S(1)} collective-permute-done((bf16[128,1024]{1,0:T(8,128)(2,1)S(1)}, bf16[128,1024]{1,0:T(8,128)(2,1)S(1)}, u32[]{:S(2)}, u32[]{:S(2)}) %collective-permute-start.69) | collective-permute-done | bytes 262176 | tf_op jit(solution)/shard_map/ppermute | solution.py:421
  516.1 4.6 collective-permute-done.70
  520.6 6.9 %collective-permute-done.76 = bf16[64,2048]{1,0:T(8,128)(2,1)S(1)} collective-permute-done((bf16[64,2048]{1,0:T(8,128)(2,1)S(1)}, bf16[64,2048]{1,0:T(8,128)(2,1)S(1)}, u32[]{:S(2)}, u32[]{:S(2)}) %collective-permute-start.76) | collective-permute-done | bytes 262176 | tf_op jit(solution)/shard_map/ppermute | solution.py:421
  527.6 16.3 %collective-permute-done.61 = bf16[256,512]{1,0:T(8,128)(2,1)S(1)} collective-permute-done((bf16[256,512]{1,0:T(8,128)(2,1)S(1)}, bf16[256,512]{1,0:T(8,128)(2,1)S(1)}, u32[]{:S(2)}, u32[]{:S(2)}) %collective-permute-start.61) | collective-permute-done | bytes 262176 | tf_op jit(solution)/shard_map/ppermute | solution.py:421
  546.2 14.0 %collective-permute-done.62 = bf16[256,512]{1,0:T(8,128)(2,1)S(1)} collective-permute-done((bf16[256,512]{1,0:T(8,128)(2,1)S(1)}, bf16[256,512]{1,0:T(8,128)(2,1)S(1)}, u32[]{:S(2)}, u32[]{:S(2)}) %collective-permute-start.62) | collective-permute-done | bytes 262176 | tf_op jit(solution)/shard_map/ppermute | solution.py:421
  562.6 3.8 collective-permute-done.71
  567.1 3.9 collective-permute-done.78
  589.4 5.2 copy.66
  606.6 7.3 %collective-permute-start.82 = (bf16[512,2048]{1,0:T(8,128)(2,1)S(1)}, bf16[512,2048]{1,0:T(8,128)(2,1)S(1)}, u32[]{:S(2)}, u32[]{:S(2)}) collective-permute-start(bf16[512,2048]{1,0:T(8,128)(2,1)S(1)} %get-tuple-element.211), channel_id=1, source_target_pairs={{0,16},{16,0},{1,17},{17,1},{2,18},{18,2},{3,19},{19,3},{4,20},{20... | collective-permute-start | bytes 6291464 | tf_op jit(solution)/shard_map/ppermute | solution.py:231
  617.5 3.6 convert_bitcast_fusion
  621.1 4.5 fusion.14
  625.6 4.4 fusion.15
  (725 shorter events, 286.5 us)
Async XLA Ops:
  7.2 50.8 %all-gather.6.cloned.1.call-start = ((), (), s32[]{:S(2)}) async-start(), calls=%async_computation | async-start | bytes 3145728 | tf_op jit(solution)/shard_map/all_gather | solution.py:515
  7.9 79.3 %all-gather.8.cloned.1.call-start = ((), (), s32[]{:S(2)}) async-start(), calls=%async_computation.1 | async-start | bytes 12582912 | tf_op jit(solution)/shard_map/all_gather | solution.py:515
  8.7 86.9 %all-gather.10.cloned.1.call-start = ((), (), s32[]{:S(2)}) async-start(), calls=%async_computation.2 | async-start | bytes 12582912 | tf_op jit(solution)/shard_map/all_gather | solution.py:515
  9.4 100.7 %all-gather.12.cloned.1.call-start = ((), (), s32[]{:S(2)}) async-start(), calls=%async_computation.4 | async-start | bytes 6291456 | tf_op jit(solution)/shard_map/all_gather | solution.py:515
  9.5 25.9 %collective-permute-start.2 = (bf16[3,1024,512]{2,1,0:T(8,128)(2,1)}, bf16[3,1024,512]{2,1,0:T(8,128)(2,1)}, u32[]{:S(2)}, u32[]{:S(2)}) collective-permute-start(bf16[3,1024,512]{2,1,0:T(8,128)(2,1)} %bitcast.4), channel_id=1, source_target_pairs={{0,16},{16,0},{1,17},{17,1},{2,18},{18,2},{3,19},{19,3},{4,20},{20... | collective-permute-start | bytes 9437192 | tf_op jit(solution)/shard_map/ppermute | solution.py:231
  16.4 397.1 %all-reduce.6.cloned.1.call-start = ((), (), s32[]{:S(2)}) async-start(), calls=%async_computation.5 | async-start | bytes 8388608 | tf_op jit(solution)/shard_map/psum | solution.py:405
  34.7 26.9 %collective-permute-start.7 = (bf16[2,512,512]{2,1,0:T(8,128)(2,1)}, bf16[2,512,512]{2,1,0:T(8,128)(2,1)}, u32[]{:S(2)}, u32[]{:S(2)}) collective-permute-start(bf16[2,512,512]{2,1,0:T(8,128)(2,1)} %pad_maximum_fusion.8), channel_id=1, source_target_pairs={{0,1},{1,0},{2,3},{3,2},{4,5},{5,4},{6,7},{7,6},{8,9},{9,8},{10,11... | collective-permute-start | bytes 3145736 | tf_op jit(solution)/shard_map/ppermute | solution.py:235
  60.4 23.7 %collective-permute-start.5 = (bf16[512,1024]{1,0:T(8,128)(2,1)S(1)}, bf16[512,1024]{1,0:T(8,128)(2,1)S(1)}, u32[]{:S(2)}, u32[]{:S(2)}) collective-permute-start(bf16[512,1024]{1,0:T(8,128)(2,1)S(1)} %convolution_convert_fusion.17), channel_id=1, source_target_pairs={{0,1},{1,0},{2,3},{3,2},{4,5},{5,4},{6,7},{7,6},{8,9},{9,8},{10,11... | collective-permute-start | bytes 3145736 | tf_op jit(solution)/shard_map/ppermute | solution.py:235
  78.9 27.7 %collective-permute-start.9 = (bf16[512,1024]{1,0:T(8,128)(2,1)}, bf16[512,1024]{1,0:T(8,128)(2,1)}, u32[]{:S(2)}, u32[]{:S(2)}) collective-permute-start(bf16[512,1024]{1,0:T(8,128)(2,1)} %convolution_convert_fusion.16), channel_id=1, source_target_pairs={{0,1},{1,0},{2,3},{3,2},{4,5},{5,4},{6,7},{7,6},{8,9},{9,8},{10,11... | collective-permute-start | bytes 3145736 | tf_op jit(solution)/shard_map/ppermute | solution.py:235
  101.9 27.2 %collective-permute-start.8 = (bf16[512,1024]{1,0:T(8,128)(2,1)}, bf16[512,1024]{1,0:T(8,128)(2,1)}, u32[]{:S(2)}, u32[]{:S(2)}) collective-permute-start(bf16[512,1024]{1,0:T(8,128)(2,1)} %fusion.40), channel_id=1, source_target_pairs={{0,1},{1,0},{2,3},{3,2},{4,5},{5,4},{6,7},{7,6},{8,9},{9,8},{10,11... | collective-permute-start | bytes 3145736 | tf_op jit(solution)/shard_map/ppermute | solution.py:235
  144.3 22.2 %collective-permute-start.11 = (bf16[512,1024]{1,0:T(8,128)(2,1)}, bf16[512,1024]{1,0:T(8,128)(2,1)}, u32[]{:S(2)}, u32[]{:S(2)}) collective-permute-start(bf16[512,1024]{1,0:T(8,128)(2,1)} %convolution_convert_fusion.15), channel_id=1, source_target_pairs={{0,1},{1,0},{2,3},{3,2},{4,5},{5,4},{6,7},{7,6},{8,9},{9,8},{10,11... | collective-permute-start | bytes 3145736 | tf_op jit(solution)/shard_map/ppermute | solution.py:235
  186.4 21.1 %collective-permute-start.12 = (bf16[512,1024]{1,0:T(8,128)(2,1)S(1)}, bf16[512,1024]{1,0:T(8,128)(2,1)S(1)}, u32[]{:S(2)}, u32[]{:S(2)}) collective-permute-start(bf16[512,1024]{1,0:T(8,128)(2,1)S(1)} %fusion.38), channel_id=1, source_target_pairs={{0,1},{1,0},{2,3},{3,2},{4,5},{5,4},{6,7},{7,6},{8,9},{9,8},{10,11... | collective-permute-start | bytes 3145736 | tf_op jit(solution)/shard_map/ppermute | solution.py:235
  190.5 20.2 %collective-permute-start.13 = (bf16[1024,1024]{1,0:T(8,128)(2,1)S(1)}, bf16[1024,1024]{1,0:T(8,128)(2,1)S(1)}, u32[]{:S(2)}, u32[]{:S(2)}) collective-permute-start(bf16[1024,1024]{1,0:T(8,128)(2,1)S(1)} %broadcast_select_fusion.5), channel_id=1, source_target_pairs={{0,16},{16,0},{1,17},{17,1},{2,18},{18,2},{3,19},{19,3},{4,20},{20... | collective-permute-start | bytes 6291464 | tf_op jit(solution)/shard_map/ppermute | solution.py:231
  197.0 15.4 %collective-permute-start.14 = (bf16[512,2048]{1,0:T(8,128)(2,1)S(1)}, bf16[512,2048]{1,0:T(8,128)(2,1)S(1)}, u32[]{:S(2)}, u32[]{:S(2)}) collective-permute-start(bf16[512,2048]{1,0:T(8,128)(2,1)S(1)} %broadcast_select_fusion.3), channel_id=1, source_target_pairs={{0,16},{16,0},{1,17},{17,1},{2,18},{18,2},{3,19},{19,3},{4,20},{20... | collective-permute-start | bytes 6291464 | tf_op jit(solution)/shard_map/ppermute | solution.py:231
  214.1 366.4 %all-reduce.4.cloned.1.call-start = ((), (), s32[]{:S(2)}) async-start(), calls=%async_computation.3 | async-start | bytes 4194304 | tf_op jit(solution)/shard_map/psum | solution.py:405
  227.8 20.3 %collective-permute-start.15 = (bf16[512,1024]{1,0:T(8,128)(2,1)S(1)}, bf16[512,1024]{1,0:T(8,128)(2,1)S(1)}, u32[]{:S(2)}, u32[]{:S(2)}) collective-permute-start(bf16[512,1024]{1,0:T(8,128)(2,1)S(1)} %add_convert_fusion.6), channel_id=1, source_target_pairs={{0,1},{1,0},{2,3},{3,2},{4,5},{5,4},{6,7},{7,6},{8,9},{9,8},{10,11... | collective-permute-start | bytes 3145736 | tf_op jit(solution)/shard_map/ppermute | solution.py:235
  234.3 44.5 %collective-permute-start.67 = (bf16[2,1024,512]{2,1,0:T(8,128)(2,1)S(1)}, bf16[2,1024,512]{2,1,0:T(8,128)(2,1)S(1)}, u32[]{:S(2)}, u32[]{:S(2)}) collective-permute-start(bf16[2,1024,512]{2,1,0:T(8,128)(2,1)S(1)} %broadcast_select_fusion.6), channel_id=1, source_target_pairs={{0,16},{16,0},{1,17},{17,1},{2,18},{18,2},{3,19},{19,3},{4,20},{20... | collective-permute-start | bytes 6291464 | tf_op jit(solution)/shard_map/ppermute | solution.py:231
  249.2 31.4 %collective-permute-start.19 = (bf16[512,1024]{1,0:T(8,128)(2,1)}, bf16[512,1024]{1,0:T(8,128)(2,1)}, u32[]{:S(2)}, u32[]{:S(2)}) collective-permute-start(bf16[512,1024]{1,0:T(8,128)(2,1)} %convolution_convert_fusion.10), channel_id=1, source_target_pairs={{0,1},{1,0},{2,3},{3,2},{4,5},{5,4},{6,7},{7,6},{8,9},{9,8},{10,11... | collective-permute-start | bytes 3145736 | tf_op jit(solution)/shard_map/ppermute | solution.py:235
  260.1 42.1 %collective-permute-start.18 = (bf16[512,1024]{1,0:T(8,128)(2,1)}, bf16[512,1024]{1,0:T(8,128)(2,1)}, u32[]{:S(2)}, u32[]{:S(2)}) collective-permute-start(bf16[512,1024]{1,0:T(8,128)(2,1)} %fusion.41), channel_id=1, source_target_pairs={{0,1},{1,0},{2,3},{3,2},{4,5},{5,4},{6,7},{7,6},{8,9},{9,8},{10,11... | collective-permute-start | bytes 3145736 | tf_op jit(solution)/shard_map/ppermute | solution.py:235
  266.7 76.8 %collective-permute-start.16 = (bf16[1024,1024]{1,0:T(8,128)(2,1)}, bf16[1024,1024]{1,0:T(8,128)(2,1)}, u32[]{:S(2)}, u32[]{:S(2)}) collective-permute-start(bf16[1024,1024]{1,0:T(8,128)(2,1)} %broadcast_select_fusion.4), channel_id=1, source_target_pairs={{0,16},{16,0},{1,17},{17,1},{2,18},{18,2},{3,19},{19,3},{4,20},{20... | collective-permute-start | bytes 6291464 | tf_op jit(solution)/shard_map/ppermute | solution.py:231
  278.2 60.6 %collective-permute-start.17 = (bf16[512,2048]{1,0:T(8,128)(2,1)}, bf16[512,2048]{1,0:T(8,128)(2,1)}, u32[]{:S(2)}, u32[]{:S(2)}) collective-permute-start(bf16[512,2048]{1,0:T(8,128)(2,1)} %broadcast_select_fusion.2), channel_id=1, source_target_pairs={{0,16},{16,0},{1,17},{17,1},{2,18},{18,2},{3,19},{19,3},{4,20},{20... | collective-permute-start | bytes 6291464 | tf_op jit(solution)/shard_map/ppermute | solution.py:231
  324.9 25.2 %collective-permute-start.21 = (bf16[1024,512]{1,0:T(8,128)(2,1)}, bf16[1024,512]{1,0:T(8,128)(2,1)}, u32[]{:S(2)}, u32[]{:S(2)}) collective-permute-start(bf16[1024,512]{1,0:T(8,128)(2,1)} %convolution_convert_fusion.8), channel_id=1, source_target_pairs={{0,16},{16,0},{1,17},{17,1},{2,18},{18,2},{3,19},{19,3},{4,20},{20... | collective-permute-start | bytes 3145736 | tf_op jit(solution)/shard_map/ppermute | solution.py:231
  328.1 25.8 %collective-permute-start.20 = (bf16[1024,512]{1,0:T(8,128)(2,1)}, bf16[1024,512]{1,0:T(8,128)(2,1)}, u32[]{:S(2)}, u32[]{:S(2)}) collective-permute-start(bf16[1024,512]{1,0:T(8,128)(2,1)} %convolution_convert_fusion.9), channel_id=1, source_target_pairs={{0,16},{16,0},{1,17},{17,1},{2,18},{18,2},{3,19},{19,3},{4,20},{20... | collective-permute-start | bytes 3145736 | tf_op jit(solution)/shard_map/ppermute | solution.py:231
  329.8 17.2 %collective-permute-start.23 = (bf16[512,1024]{1,0:T(8,128)(2,1)}, bf16[512,1024]{1,0:T(8,128)(2,1)}, u32[]{:S(2)}, u32[]{:S(2)}) collective-permute-start(bf16[512,1024]{1,0:T(8,128)(2,1)} %convolution_convert_fusion.6), channel_id=1, source_target_pairs={{0,16},{16,0},{1,17},{17,1},{2,18},{18,2},{3,19},{19,3},{4,20},{20... | collective-permute-start | bytes 3145736 | tf_op jit(solution)/shard_map/ppermute | solution.py:231
  338.8 18.1 %collective-permute-start.22 = (bf16[1024,512]{1,0:T(8,128)(2,1)}, bf16[1024,512]{1,0:T(8,128)(2,1)S(1)}, u32[]{:S(2)}, u32[]{:S(2)}) collective-permute-start(bf16[1024,512]{1,0:T(8,128)(2,1)} %convolution_convert_fusion.7), channel_id=1, source_target_pairs={{0,16},{16,0},{1,17},{17,1},{2,18},{18,2},{3,19},{19,3},{4,20},{20... | collective-permute-start | bytes 3145736 | tf_op jit(solution)/shard_map/ppermute | solution.py:231
  374.1 85.5 %collective-permute-start.24 = (bf16[3,512,512]{2,1,0:T(8,128)(2,1)}, bf16[3,512,512]{2,1,0:T(8,128)(2,1)}, u32[]{:S(2)}, u32[]{:S(2)}) collective-permute-start(bf16[3,512,512]{2,1,0:T(8,128)(2,1)} %pad_maximum_fusion.7), channel_id=1, source_target_pairs={{0,1},{1,0},{2,3},{3,2},{4,5},{5,4},{6,7},{7,6},{8,9},{9,8},{10,11... | collective-permute-start | bytes 4718600 | tf_op jit(solution)/shard_map/ppermute | solution.py:235
  375.2 83.0 %collective-permute-start.25 = (f32[8,128]{1,0:T(8,128)S(1)}, f32[8,128]{1,0:T(8,128)S(1)}, u32[]{:S(2)}, u32[]{:S(2)}) collective-permute-start(f32[8,128]{1,0:T(8,128)S(1)} %reshape.732), channel_id=1, source_target_pairs={{0,1},{1,0},{2,3},{3,2},{4,5},{5,4},{6,7},{7,6},{8,9},{9,8},{10,11... | collective-permute-start | bytes 12296 | tf_op jit(solution)/shard_map/ppermute | solution.py:235
  421.6 15.4 %collective-permute-start.37 = (bf16[64,2048]{1,0:T(8,128)(2,1)S(1)}, bf16[64,2048]{1,0:T(8,128)(2,1)S(1)}, u32[]{:S(2)}, u32[]{:S(2)}) collective-permute-start(bf16[64,2048]{1,0:T(8,128)(2,1)S(1)} %bitcast_add_fusion.19), channel_id=1, source_target_pairs={{0,2},{4,0},{8,4},{12,8},{14,12},{10,14},{6,10},{2,6},{1,3},{5,1},... | collective-permute-start | bytes 786440 | tf_op jit(solution)/shard_map/ppermute | solution.py:421
  422.9 31.8 %collective-permute-start.57 = (bf16[256,512]{1,0:T(8,128)(2,1)S(1)}, bf16[256,512]{1,0:T(8,128)(2,1)S(1)}, u32[]{:S(2)}, u32[]{:S(2)}) collective-permute-start(bf16[256,512]{1,0:T(8,128)(2,1)S(1)} %bitcast_add_fusion.6), channel_id=1, source_target_pairs={{0,2},{4,0},{8,4},{12,8},{14,12},{10,14},{6,10},{2,6},{1,3},{5,1},... | collective-permute-start | bytes 786440 | tf_op jit(solution)/shard_map/ppermute | solution.py:421
  426.2 30.2 %collective-permute-start.43 = (bf16[256,512]{1,0:T(8,128)(2,1)S(1)}, bf16[256,512]{1,0:T(8,128)(2,1)S(1)}, u32[]{:S(2)}, u32[]{:S(2)}) collective-permute-start(bf16[256,512]{1,0:T(8,128)(2,1)S(1)} %bitcast_add_fusion.13), channel_id=1, source_target_pairs={{0,4},{4,8},{8,12},{12,14},{14,10},{10,6},{6,2},{2,0},{1,5},{5,9},... | collective-permute-start | bytes 786440 | tf_op jit(solution)/shard_map/ppermute | solution.py:421
  437.0 41.5 %collective-permute-start.35 = (bf16[128,1024]{1,0:T(8,128)(2,1)}, bf16[128,1024]{1,0:T(8,128)(2,1)}, u32[]{:S(2)}, u32[]{:S(2)}) collective-permute-start(bf16[128,1024]{1,0:T(8,128)(2,1)} %bitcast_add_fusion.21), channel_id=1, source_target_pairs={{0,4},{4,8},{8,12},{12,14},{14,10},{10,6},{6,2},{2,0},{1,5},{5,9},... | collective-permute-start | bytes 786440 | tf_op jit(solution)/shard_map/ppermute | solution.py:421
  454.7 26.8 %collective-permute-start.38 = (bf16[64,2048]{1,0:T(8,128)(2,1)S(1)}, bf16[64,2048]{1,0:T(8,128)(2,1)}, u32[]{:S(2)}, u32[]{:S(2)}) collective-permute-start(bf16[64,2048]{1,0:T(8,128)(2,1)S(1)} %bitcast_add_fusion.18), channel_id=1, source_target_pairs={{0,2},{4,0},{8,4},{12,8},{14,12},{10,14},{6,10},{2,6},{1,3},{5,1},... | collective-permute-start | bytes 786440 | tf_op jit(solution)/shard_map/ppermute | solution.py:421
  456.4 18.3 %collective-permute-start.58 = (bf16[256,512]{1,0:T(8,128)(2,1)}, bf16[256,512]{1,0:T(8,128)(2,1)}, u32[]{:S(2)}, u32[]{:S(2)}) collective-permute-start(bf16[256,512]{1,0:T(8,128)(2,1)} %bitcast_add_fusion.5), channel_id=1, source_target_pairs={{0,2},{4,0},{8,4},{12,8},{14,12},{10,14},{6,10},{2,6},{1,3},{5,1},... | collective-permute-start | bytes 786440 | tf_op jit(solution)/shard_map/ppermute | solution.py:421
  458.1 17.6 %collective-permute-start.44 = (bf16[256,512]{1,0:T(8,128)(2,1)}, bf16[256,512]{1,0:T(8,128)(2,1)}, u32[]{:S(2)}, u32[]{:S(2)}) collective-permute-start(bf16[256,512]{1,0:T(8,128)(2,1)} %bitcast_add_fusion.12), channel_id=1, source_target_pairs={{0,4},{4,8},{8,12},{12,14},{14,10},{10,6},{6,2},{2,0},{1,5},{5,9},... | collective-permute-start | bytes 786440 | tf_op jit(solution)/shard_map/ppermute | solution.py:421
  467.1 133.3 %collective-permute-start.32 = (f32[2,512,512]{2,1,0:T(8,128)}, f32[2,512,512]{2,1,0:T(8,128)}, u32[]{:S(2)}, u32[]{:S(2)}) collective-permute-start(f32[2,512,512]{2,1,0:T(8,128)} %get-tuple-element.215), channel_id=1, source_target_pairs={{0,16},{16,0},{1,17},{17,1},{2,18},{18,2},{3,19},{19,3},{4,20},{20... | collective-permute-start | bytes 6291464 | tf_op jit(solution)/shard_map/ppermute | solution.py:231
  476.7 16.1 %collective-permute-start.45 = (bf16[256,512]{1,0:T(8,128)(2,1)S(1)}, bf16[256,512]{1,0:T(8,128)(2,1)S(1)}, u32[]{:S(2)}, u32[]{:S(2)}) collective-permute-start(bf16[256,512]{1,0:T(8,128)(2,1)S(1)} %bitcast_add_fusion.11), channel_id=1, source_target_pairs={{0,4},{4,8},{8,12},{12,14},{14,10},{10,6},{6,2},{2,0},{1,5},{5,9},... | collective-permute-start | bytes 786440 | tf_op jit(solution)/shard_map/ppermute | solution.py:421
  492.7 20.8 %collective-permute-start.60 = (bf16[256,512]{1,0:T(8,128)(2,1)S(1)}, bf16[256,512]{1,0:T(8,128)(2,1)S(1)}, u32[]{:S(2)}, u32[]{:S(2)}) collective-permute-start(bf16[256,512]{1,0:T(8,128)(2,1)S(1)} %bitcast_add_fusion.3), channel_id=1, source_target_pairs={{0,2},{4,0},{8,4},{12,8},{14,12},{10,14},{6,10},{2,6},{1,3},{5,1},... | collective-permute-start | bytes 786440 | tf_op jit(solution)/shard_map/ppermute | solution.py:421
  492.9 21.5 %collective-permute-start.46 = (bf16[256,512]{1,0:T(8,128)(2,1)S(1)}, bf16[256,512]{1,0:T(8,128)(2,1)S(1)}, u32[]{:S(2)}, u32[]{:S(2)}) collective-permute-start(bf16[256,512]{1,0:T(8,128)(2,1)S(1)} %bitcast_add_fusion.10), channel_id=1, source_target_pairs={{0,4},{4,8},{8,12},{12,14},{14,10},{10,6},{6,2},{2,0},{1,5},{5,9},... | collective-permute-start | bytes 786440 | tf_op jit(solution)/shard_map/ppermute | solution.py:421
  494.4 17.6 %collective-permute-start.75 = (bf16[64,2048]{1,0:T(8,128)(2,1)S(1)}, bf16[64,2048]{1,0:T(8,128)(2,1)S(1)}, u32[]{:S(2)}, u32[]{:S(2)}) collective-permute-start(bf16[64,2048]{1,0:T(8,128)(2,1)S(1)} %bitcast_add_fusion.1), channel_id=1, source_target_pairs={{0,2},{4,0},{8,4},{12,8},{14,12},{10,14},{6,10},{2,6},{1,3},{5,1},... | collective-permute-start | bytes 786440 | tf_op jit(solution)/shard_map/ppermute | solution.py:421
  514.5 29.4 %collective-permute-start.61 = (bf16[256,512]{1,0:T(8,128)(2,1)S(1)}, bf16[256,512]{1,0:T(8,128)(2,1)S(1)}, u32[]{:S(2)}, u32[]{:S(2)}) collective-permute-start(bf16[256,512]{1,0:T(8,128)(2,1)S(1)} %collective-permute-done.60), channel_id=1, source_target_pairs={{0,2},{4,0},{8,4},{12,8},{14,12},{10,14},{6,10},{2,6},{1,3},{5,1},... | collective-permute-start | bytes 786440 | tf_op jit(solution)/shard_map/ppermute | solution.py:421
  516.0 27.9 %collective-permute-start.47 = (bf16[256,512]{1,0:T(8,128)(2,1)S(1)}, bf16[256,512]{1,0:T(8,128)(2,1)S(1)}, u32[]{:S(2)}, u32[]{:S(2)}) collective-permute-start(bf16[256,512]{1,0:T(8,128)(2,1)S(1)} %collective-permute-done.46), channel_id=1, source_target_pairs={{0,4},{4,8},{8,12},{12,14},{14,10},{10,6},{6,2},{2,0},{1,5},{5,9},... | collective-permute-start | bytes 786440 | tf_op jit(solution)/shard_map/ppermute | solution.py:421
  527.6 49.8 %collective-permute-start.89 = (f32[14,128]{1,0:T(8,128)S(1)}, f32[14,128]{1,0:T(8,128)S(1)}, u32[]{:S(2)}, u32[]{:S(2)}) collective-permute-start(f32[14,128]{1,0:T(8,128)S(1)} %fusion.187), channel_id=1, source_target_pairs={{0,8},{4,12},{8,0},{12,4},{1,9},{5,13},{9,1},{13,5},{2,10},{6,14},... | collective-permute-start | bytes 21512 | tf_op jit(solution)/shard_map/ppermute | solution.py:413
  527.6 32.8 %collective-permute-start.77 = (bf16[64,2048]{1,0:T(8,128)(2,1)S(1)}, bf16[64,2048]{1,0:T(8,128)(2,1)S(1)}, u32[]{:S(2)}, u32[]{:S(2)}) collective-permute-start(bf16[64,2048]{1,0:T(8,128)(2,1)S(1)} %collective-permute-done.76), channel_id=1, source_target_pairs={{0,2},{4,0},{8,4},{12,8},{14,12},{10,14},{6,10},{2,6},{1,3},{5,1},... | collective-permute-start | bytes 786440 | tf_op jit(solution)/shard_map/ppermute | solution.py:421
  543.9 16.3 %collective-permute-start.62 = (bf16[256,512]{1,0:T(8,128)(2,1)S(1)}, bf16[256,512]{1,0:T(8,128)(2,1)S(1)}, u32[]{:S(2)}, u32[]{:S(2)}) collective-permute-start(bf16[256,512]{1,0:T(8,128)(2,1)S(1)} %collective-permute-done.61), channel_id=1, source_target_pairs={{0,2},{4,0},{8,4},{12,8},{14,12},{10,14},{6,10},{2,6},{1,3},{5,1},... | collective-permute-start | bytes 786440 | tf_op jit(solution)/shard_map/ppermute | solution.py:421
  543.9 17.8 %collective-permute-start.48 = (bf16[256,512]{1,0:T(8,128)(2,1)S(1)}, bf16[256,512]{1,0:T(8,128)(2,1)S(1)}, u32[]{:S(2)}, u32[]{:S(2)}) collective-permute-start(bf16[256,512]{1,0:T(8,128)(2,1)S(1)} %collective-permute-done.47), channel_id=1, source_target_pairs={{0,4},{4,8},{8,12},{12,14},{14,10},{10,6},{6,2},{2,0},{1,5},{5,9},... | collective-permute-start | bytes 786440 | tf_op jit(solution)/shard_map/ppermute | solution.py:421
  571.0 15.8 %collective-permute-start.64 = (bf16[256,512]{1,0:T(8,128)(2,1)S(1)}, bf16[256,512]{1,0:T(8,128)(2,1)S(1)}, u32[]{:S(2)}, u32[]{:S(2)}) collective-permute-start(bf16[256,512]{1,0:T(8,128)(2,1)S(1)} %collective-permute-done.63), channel_id=1, source_target_pairs={{0,2},{4,0},{8,4},{12,8},{14,12},{10,14},{6,10},{2,6},{1,3},{5,1},... | collective-permute-start | bytes 786440 | tf_op jit(solution)/shard_map/ppermute | solution.py:421
  594.7 20.8 %collective-permute-start.66 = (bf16[256,512]{1,0:T(8,128)(2,1)S(1)}, bf16[256,512]{1,0:T(8,128)(2,1)S(1)}, u32[]{:S(2)}, u32[]{:S(2)}) collective-permute-start(bf16[256,512]{1,0:T(8,128)(2,1)S(1)} %collective-permute-done.65), channel_id=1, source_target_pairs={{0,2},{4,0},{8,4},{12,8},{14,12},{10,14},{6,10},{2,6},{1,3},{5,1},... | collective-permute-start | bytes 786440 | tf_op jit(solution)/shard_map/ppermute | solution.py:421
  598.6 18.7 %collective-permute-start.52 = (bf16[256,512]{1,0:T(8,128)(2,1)S(1)}, bf16[256,512]{1,0:T(8,128)(2,1)S(1)}, u32[]{:S(2)}, u32[]{:S(2)}) collective-permute-start(bf16[256,512]{1,0:T(8,128)(2,1)S(1)} %collective-permute-done.51), channel_id=1, source_target_pairs={{0,4},{4,8},{8,12},{12,14},{14,10},{10,6},{6,2},{2,0},{1,5},{5,9},... | collective-permute-start | bytes 786440 | tf_op jit(solution)/shard_map/ppermute | solution.py:421
  (201 other events, 1922.4 us)
Sparse Core Ops, SparseCore 0:
  9.6 13.0 all-gather.5
  24.2 21.0 all-gather.7
  46.8 21.0 all-gather.9
  69.8 14.8 all-gather.11
  214.2 161.2 all-reduce.5
  413.7 139.6 all-reduce.3

commit v3 on v2

--- a/solution.py
+++ b/solution.py
@@ -130,7 +130,7 @@
     return jnp.roll(jnp.flip(vector, axis=-1), 1, axis=-1)
 
 
-little = pl.CostEstimate(flops=1, bytes_accessed=1, transcendentals=1)
+little = pl.CostEstimate(flops=12_000_000_000, bytes_accessed=30_000_000, transcendentals=4_000_000)
 kernel_params = pltpu.CompilerParams(vmem_limit_bytes=48 * 1024 * 1024)
 
 
@@ -505,7 +505,7 @@
         return pick(mine.reshape(tokens, -1), swap_section(give).reshape(tokens, -1))
 
     encoder_half, decoder_half = own_rows(layer_inputs)
-    mixing = both(attention_in[0].transpose(1, 0, 2))
+    mixing = lax.all_gather(attention_in[0].transpose(1, 0, 2), "section")
     encoder_in = gather_features(encoder_half).astype(f32)
     own_gains = gather_features(norm_gains[0])
     small_own = jnp.concatenate([own_gains.reshape(-1), bias_tables[0].reshape(-1)])
@@ -513,13 +513,20 @@
     gains = [part[: own_gains.size].reshape(own_gains.shape) for part in small_both]
     tables = [part[own_gains.size :].reshape(bias_tables.shape[1:]) for part in small_both]
     projecting, expanding, contracting, crossing = lax.all_gather(
-        (attention_out[0], expand_weights[0], contract_weights[0], cross_weights[0].transpose(1, 0, 2)),
+        hold(
+            (
+                attention_out[0],
+                expand_weights[0],
+                contract_weights[0],
+                cross_weights[0].transpose(1, 0, 2),
+            ),
+            encoder_half,
+        ),
         "section",
     )
     encoder_cotangent, decoder_cotangent = own_rows(output_cotangents)
     decoder_halves = hold(jnp.stack([decoder_half, decoder_cotangent]), encoder_in)
     decoder_others = swap_tensor(decoder_halves) if lax.axis_size("tensor") == 2 else decoder_halves
-    encoder_in = hold(encoder_in, mixing)
     ids = lax.dynamic_slice_in_dim(segment_ids, section * rows, rows, 1)
     encoder_ids, decoder_ids = ids[0], ids[1]
     onehots = (bucket_onehot(length, False), bucket_onehot(length, True))

time: 647 us -> 645 us (level)
  other arithmetic: 119 us -> 107 us
  local copies, waits for them, and re-layouts: 57 us -> 66.2 us
    unnamed x320 -> x316, local copies, waits for them, and re-layouts: 29.4 us -> 43.6 us
    ppermute x14, waiting for transfers between devices: 47.5 us -> 54.3 us  [swap_tensor(): return lax.ppermute(value, 'tensor', [(0, 1), (1, 0)])]
    ppermute x17 -> x16, starting transfers between devices: 34.8 us -> 33.7 us  [swap_section(): return lax.ppermute(value, 'section', [(0, 1), (1, 0)])]
  transfers between devices with their start and end apart: 96 -> 96, of which waited for: 31 -> 34; matrix products, arithmetic and copies ran while one was open for 37% -> 37% of each run, Pallas kernels for 10% -> 10%
where the time goes in v3:
time: 645 us; the launch traced here: 639 us
  waiting for transfers between devices  183 us (28%)
  other arithmetic  107 us (17%)
  matrix products  105 us (16%)
  starting transfers between devices  99.2 us (15%)
  local copies, waits for them, and re-layouts  66.2 us (10%)
  Pallas kernels  61.6 us (10%)
  between operations  17.1 us (3%)
    ppermute x56, waiting for transfers between devices, along_ring(): return lax.ppermute(value, ('z', 'y'), pairs)  126 us
    ppermute x14, waiting for transfers between devices, swap_tensor(): return lax.ppermute(value, 'tensor', [(0, 1), (1, 0)])  54.3 us
    ppermute x56, starting transfers between devices, along_ring(): return lax.ppermute(value, ('z', 'y'), pairs)  49.8 us
    unnamed x316, local copies, waits for them, and re-layouts  43.6 us
    pallas_call x3, Pallas kernels, attend_back(): pl.pallas_call(functools.partial(attend_back_kernel, causal, biased), gri...  34.6 us
    ppermute x16, starting transfers between devices, swap_section(): return lax.ppermute(value, 'section', [(0, 1), (1, 0)])  33.7 us
    dot_general x8, matrix products, matmul(): return jnp.dot(a, b, preferred_element_type=f32)  31.5 us
    dot_general x16, matrix products, matmul_t(): return jnp.einsum('tc,dc->td', a, b, preferred_element_type=f32)  30 us
  transfers between devices with their start and end apart: 96, of which 34 were waited for; matrix products, arithmetic and copies ran while one was open for 37% of the time, Pallas kernels for 10%

profile of v3, /device:TPU:1, one launch (start us, length us, event | category | flops | bytes accessed | tf_op | source)
XLA Modules:
  0.0 639.2 jit_solution(16354870920987388426)
XLA Ops:
  23.8 10.8 %collective-permute-done.1 = bf16[512,512]{1,0:T(8,128)(2,1)S(1)} collective-permute-done((bf16[512,512]{1,0:T(8,128)(2,1)S(1)}, bf16[512,512]{1,0:T(8,128)(2,1)S(1)}, u32[]{:S(2)}, u32[]{:S(2)}) %collective-permute-start.1) | collective-permute-done | bytes 524320 | tf_op jit(solution)/shard_map/ppermute | solution.py:235
  37.4 4.2 fusion.58.q_ref.k_ref.v_ref
  41.6 11.8 %shard_map.187 = (bf16[512,512]{1,0:T(8,128)(2,1)S(1)}, f32[1,4,512,2]{3,2,1,0:T(8,128)S(1)}) custom-call(bf16[3,512,512]{2,1,0:T(8,128)(2,1)S(1)} %fusion.58.q_ref.k_ref.v_ref, bf16[3,512,512]{2,1,0:T(8,128)(2,1)S(1)} %fusion.58.q_ref.k_ref.v_ref, bf16[3,512,512]{2,1,0:T(8,128)(2,1)S(1)} %fusion.58.q_ref.k_ref.v_ref, ...), custom_call_target="tpu_custom_call" | custom-call | flops 12000000000 | bytes 30000000 | tf_op jit(solution)/shard_map/pallas_call | solution.py:156
  64.9 9.2 %shard_map.188 = (bf16[512,512]{1,0:T(8,128)(2,1)S(1)}, f32[1,4,512,2]{3,2,1,0:T(8,128)S(1)}) custom-call(bf16[3,512,512]{2,1,0:T(8,128)(2,1)S(1)} %fusion.55.q_ref.k_ref.v_ref, bf16[3,512,512]{2,1,0:T(8,128)(2,1)S(1)} %fusion.55.q_ref.k_ref.v_ref, bf16[3,512,512]{2,1,0:T(8,128)(2,1)S(1)} %fusion.55.q_ref.k_ref.v_ref, ...), custom_call_target="tpu_custom_call" | custom-call | flops 12000000000 | bytes 30000000 | tf_op jit(solution)/shard_map/pallas_call | solution.py:156
  76.6 6.0 collective-permute-done.4
  84.9 8.3 %multiply_convert_fusion.1 = (bf16[512,2048]{1,0:T(8,128)(2,1)}, f32[512,2048]{1,0:T(8,128)}) fusion(bf16[512,1024]{1,0:T(8,128)(2,1)S(1)} %multiply_convert_fusion.5, bf16[2048,2048]{1,0:T(8,128)(2,1)} %all-gather.15.cloned.1.call-done), kind=kOutput, calls=%fused_computation.26 | convolution fusion | flops 2156920832 | bytes 11534336 | tf_op jit(solution)/shard_map/dot_general | solution.py:314
  93.2 6.3 fusion.64
  111.4 16.2 %collective-permute-done.7 = bf16[512,1024]{1,0:T(8,128)(2,1)} collective-permute-done((bf16[512,1024]{1,0:T(8,128)(2,1)}, bf16[512,1024]{1,0:T(8,128)(2,1)}, u32[]{:S(2)}, u32[]{:S(2)}) %collective-permute-start.7) | collective-permute-done | bytes 1048608 | tf_op jit(solution)/shard_map/ppermute | solution.py:235
  133.2 6.0 shard_map.189
  148.8 12.6 %reverse.9 = f32[8,1024]{1,0:T(8,128)S(1)} reverse(f32[8,1024]{1,0:T(8,128)S(1)} %bitcast.525), dimensions={1} | reverse | bytes 65536
  173.1 5.8 multiply_convert_fusion
  179.0 4.7 fusion.13
  189.7 3.6 collective-permute-start.12
  199.5 8.1 %collective-permute-done.11 = bf16[512,1024]{1,0:T(8,128)(2,1)S(1)} collective-permute-done((bf16[512,1024]{1,0:T(8,128)(2,1)S(1)}, bf16[512,1024]{1,0:T(8,128)(2,1)S(1)}, u32[]{:S(2)}, u32[]{:S(2)}) %collective-permute-start.11) | collective-permute-done | bytes 1048608 | tf_op jit(solution)/shard_map/ppermute | solution.py:235
  216.7 10.0 %shard_map.190 = (bf16[1,512,512]{2,1,0:T(8,128)(2,1)S(1)}, bf16[1,512,512]{2,1,0:T(8,128)(2,1)S(1)}, bf16[1,512,512]{2,1,0:T(8,128)(2,1)S(1)}) custom-call(bf16[1,512,512]{2,1,0:T(8,128)(2,1)S(1)} %copy-done.6, bf16[2,512,512]{2,1,0:T(8,128)(2,1)S(1)} %copy-done.16, bf16[2,512,512]{2,1,0:T(8,128)(2,1)S(1)} %copy-done.16, ...), custom_call_target="tpu_custom_call" | custom-call | flops 12000000000 | bytes 30000000 | tf_op jit(solution)/shard_map/pallas_call | solution.py:193
  234.2 4.5 collective-permute-start.66
  241.6 7.2 %collective-permute-done.14 = bf16[512,1024]{1,0:T(8,128)(2,1)S(1)} collective-permute-done((bf16[512,1024]{1,0:T(8,128)(2,1)S(1)}, bf16[512,1024]{1,0:T(8,128)(2,1)S(1)}, u32[]{:S(2)}, u32[]{:S(2)}) %collective-permute-start.14) | collective-permute-done | bytes 1048608 | tf_op jit(solution)/shard_map/ppermute | solution.py:235
  252.6 4.9 fusion.6
  266.9 5.6 collective-permute-start.15
  282.9 3.9 fusion.164
  288.7 12.3 %shard_map.191 = (bf16[1,512,512]{2,1,0:T(8,128)(2,1)S(1)}, bf16[1,512,512]{2,1,0:T(8,128)(2,1)S(1)}, bf16[1,512,512]{2,1,0:T(8,128)(2,1)S(1)}, f32[1,4,2,1024]{3,2,1,0:T(2,128)S(1)}) custom-call(bf16[3,512,512]{2,1,0:T(8,128)(2,1)S(1)} %copy-done.18, bf16[3,512,512]{2,1,0:T(8,128)(2,1)S(1)} %copy-done.18, bf16[3,512,512]{2,1,0:T(8,128)(2,1)S(1)} %copy-done.18, ...), custom_call_target="tpu_custom_call" | custom-call | flops 12000000000 | bytes 30000000 | tf_op jit(solution)/shard_map/pallas_call | solution.py:193
  309.9 12.3 %shard_map.192 = (bf16[1,512,512]{2,1,0:T(8,128)(2,1)S(1)}, bf16[1,512,512]{2,1,0:T(8,128)(2,1)S(1)}, bf16[1,512,512]{2,1,0:T(8,128)(2,1)S(1)}, f32[1,4,2,1024]{3,2,1,0:T(2,128)S(1)}) custom-call(bf16[3,512,512]{2,1,0:T(8,128)(2,1)S(1)} %copy-done.20, bf16[3,512,512]{2,1,0:T(8,128)(2,1)S(1)} %copy-done.20, bf16[3,512,512]{2,1,0:T(8,128)(2,1)S(1)} %copy-done.20, ...), custom_call_target="tpu_custom_call" | custom-call | flops 12000000000 | bytes 30000000 | tf_op jit(solution)/shard_map/pallas_call | solution.py:193
  338.8 4.7 select_add_fusion.1
  343.5 3.4 select_add_fusion.2
  351.1 3.5 add_convert_fusion.4
  354.6 3.5 add_convert_fusion.5
  378.5 4.0 collective-permute-done.25
  385.4 3.9 collective-permute-done.52
  390.7 3.4 collective-permute-done.26
  396.9 3.8 collective-permute-done.53
  429.7 7.1 %collective-permute-done.36 = bf16[64,2048]{1,0:T(8,128)(2,1)S(1)} collective-permute-done((bf16[64,2048]{1,0:T(8,128)(2,1)S(1)}, bf16[64,2048]{1,0:T(8,128)(2,1)S(1)}, u32[]{:S(2)}, u32[]{:S(2)}) %collective-permute-start.36) | collective-permute-done | bytes 262176 | tf_op jit(solution)/shard_map/ppermute | solution.py:421
  437.9 16.5 %collective-permute-done.56 = bf16[256,512]{1,0:T(8,128)(2,1)S(1)} collective-permute-done((bf16[256,512]{1,0:T(8,128)(2,1)S(1)}, bf16[256,512]{1,0:T(8,128)(2,1)S(1)}, u32[]{:S(2)}, u32[]{:S(2)}) %collective-permute-start.56) | collective-permute-done | bytes 262176 | tf_op jit(solution)/shard_map/ppermute | solution.py:421
  458.5 3.5 multiply_reduce_fusion.14
  466.0 8.4 %collective-permute-start.31 = (f32[2,512,512]{2,1,0:T(8,128)}, f32[2,512,512]{2,1,0:T(8,128)}, u32[]{:S(2)}, u32[]{:S(2)}) collective-permute-start(f32[2,512,512]{2,1,0:T(8,128)} %get-tuple-element.219), channel_id=1, source_target_pairs={{0,16},{16,0},{1,17},{17,1},{2,18},{18,2},{3,19},{19,3},{4,20},{20... | collective-permute-start | bytes 6291464 | tf_op jit(solution)/shard_map/ppermute | solution.py:231
  483.2 4.3 collective-permute-done.58
  487.5 5.6 collective-permute-done.73
  498.1 11.5 %collective-permute-done.68 = bf16[128,1024]{1,0:T(8,128)(2,1)S(1)} collective-permute-done((bf16[128,1024]{1,0:T(8,128)(2,1)S(1)}, bf16[128,1024]{1,0:T(8,128)(2,1)S(1)}, u32[]{:S(2)}, u32[]{:S(2)}) %collective-permute-start.68) | collective-permute-done | bytes 262176 | tf_op jit(solution)/shard_map/ppermute | solution.py:421
  516.1 4.9 collective-permute-done.69
  521.1 9.1 %collective-permute-done.75 = bf16[64,2048]{1,0:T(8,128)(2,1)S(1)} collective-permute-done((bf16[64,2048]{1,0:T(8,128)(2,1)S(1)}, bf16[64,2048]{1,0:T(8,128)(2,1)S(1)}, u32[]{:S(2)}, u32[]{:S(2)}) %collective-permute-start.75) | collective-permute-done | bytes 262176 | tf_op jit(solution)/shard_map/ppermute | solution.py:421
  530.2 15.6 %collective-permute-done.60 = bf16[256,512]{1,0:T(8,128)(2,1)S(1)} collective-permute-done((bf16[256,512]{1,0:T(8,128)(2,1)S(1)}, bf16[256,512]{1,0:T(8,128)(2,1)S(1)}, u32[]{:S(2)}, u32[]{:S(2)}) %collective-permute-start.60) | collective-permute-done | bytes 262176 | tf_op jit(solution)/shard_map/ppermute | solution.py:421
  548.1 12.6 %collective-permute-done.61 = bf16[256,512]{1,0:T(8,128)(2,1)S(1)} collective-permute-done((bf16[256,512]{1,0:T(8,128)(2,1)S(1)}, bf16[256,512]{1,0:T(8,128)(2,1)S(1)}, u32[]{:S(2)}, u32[]{:S(2)}) %collective-permute-start.61) | collective-permute-done | bytes 262176 | tf_op jit(solution)/shard_map/ppermute | solution.py:421
  563.4 3.8 collective-permute-done.70
  569.7 4.7 collective-permute-done.77
  592.0 5.2 copy.58
  609.6 6.3 collective-permute-start.81
  619.5 3.6 convert_bitcast_fusion
  623.1 4.5 fusion.14
  627.7 4.4 fusion.15
  (723 shorter events, 285.7 us)
Async XLA Ops:
  7.2 30.2 %all-gather.11.cloned.1.call-start = ((), (), s32[]{:S(2)}) async-start(), calls=%async_computation.1 | async-start | bytes 9437184 | tf_op jit(solution)/shard_map/all_gather | solution.py:508
  7.9 46.6 %all-gather.13.cloned.1.call-start = ((), (), s32[]{:S(2)}) async-start(), calls=%async_computation.2 | async-start | bytes 3145728 | tf_op jit(solution)/shard_map/all_gather | solution.py:515
  11.9 73.0 %all-gather.15.cloned.1.call-start = ((), (), s32[]{:S(2)}) async-start(), calls=%async_computation.3 | async-start | bytes 12582912 | tf_op jit(solution)/shard_map/all_gather | solution.py:515
  12.7 80.5 %all-gather.17.cloned.1.call-start = ((), (), s32[]{:S(2)}) async-start(), calls=%async_computation.4 | async-start | bytes 12582912 | tf_op jit(solution)/shard_map/all_gather | solution.py:515
  13.3 95.3 %all-gather.19.cloned.1.call-start = ((), (), s32[]{:S(2)}) async-start(), calls=%async_computation.5 | async-start | bytes 6291456 | tf_op jit(solution)/shard_map/all_gather | solution.py:515
  22.2 391.8 %all-reduce.6.cloned.1.call-start = ((), (), s32[]{:S(2)}) async-start(), calls=%async_computation.6 | async-start | bytes 8388608 | tf_op jit(solution)/shard_map/psum | solution.py:405
  36.6 23.6 %collective-permute-start.6 = (bf16[2,512,512]{2,1,0:T(8,128)(2,1)S(1)}, bf16[2,512,512]{2,1,0:T(8,128)(2,1)}, u32[]{:S(2)}, u32[]{:S(2)}) collective-permute-start(bf16[2,512,512]{2,1,0:T(8,128)(2,1)S(1)} %pad_maximum_fusion.8), channel_id=1, source_target_pairs={{0,1},{1,0},{2,3},{3,2},{4,5},{5,4},{6,7},{7,6},{8,9},{9,8},{10,11... | collective-permute-start | bytes 3145736 | tf_op jit(solution)/shard_map/ppermute | solution.py:235
  56.9 25.7 %collective-permute-start.4 = (bf16[512,1024]{1,0:T(8,128)(2,1)S(1)}, bf16[512,1024]{1,0:T(8,128)(2,1)S(1)}, u32[]{:S(2)}, u32[]{:S(2)}) collective-permute-start(bf16[512,1024]{1,0:T(8,128)(2,1)S(1)} %convolution_convert_fusion.16), channel_id=1, source_target_pairs={{0,1},{1,0},{2,3},{3,2},{4,5},{5,4},{6,7},{7,6},{8,9},{9,8},{10,11... | collective-permute-start | bytes 3145736 | tf_op jit(solution)/shard_map/ppermute | solution.py:235
  75.8 29.3 %collective-permute-start.8 = (bf16[512,1024]{1,0:T(8,128)(2,1)}, bf16[512,1024]{1,0:T(8,128)(2,1)}, u32[]{:S(2)}, u32[]{:S(2)}) collective-permute-start(bf16[512,1024]{1,0:T(8,128)(2,1)} %convolution_convert_fusion.15), channel_id=1, source_target_pairs={{0,1},{1,0},{2,3},{3,2},{4,5},{5,4},{6,7},{7,6},{8,9},{9,8},{10,11... | collective-permute-start | bytes 3145736 | tf_op jit(solution)/shard_map/ppermute | solution.py:235
  99.5 28.1 %collective-permute-start.7 = (bf16[512,1024]{1,0:T(8,128)(2,1)}, bf16[512,1024]{1,0:T(8,128)(2,1)}, u32[]{:S(2)}, u32[]{:S(2)}) collective-permute-start(bf16[512,1024]{1,0:T(8,128)(2,1)} %fusion.64), channel_id=1, source_target_pairs={{0,1},{1,0},{2,3},{3,2},{4,5},{5,4},{6,7},{7,6},{8,9},{9,8},{10,11... | collective-permute-start | bytes 3145736 | tf_op jit(solution)/shard_map/ppermute | solution.py:235
  142.6 27.5 %collective-permute-start.10 = (bf16[512,1024]{1,0:T(8,128)(2,1)}, bf16[512,1024]{1,0:T(8,128)(2,1)}, u32[]{:S(2)}, u32[]{:S(2)}) collective-permute-start(bf16[512,1024]{1,0:T(8,128)(2,1)} %convolution_convert_fusion.14), channel_id=1, source_target_pairs={{0,1},{1,0},{2,3},{3,2},{4,5},{5,4},{6,7},{7,6},{8,9},{9,8},{10,11... | collective-permute-start | bytes 3145736 | tf_op jit(solution)/shard_map/ppermute | solution.py:235
  186.2 21.4 %collective-permute-start.11 = (bf16[512,1024]{1,0:T(8,128)(2,1)S(1)}, bf16[512,1024]{1,0:T(8,128)(2,1)S(1)}, u32[]{:S(2)}, u32[]{:S(2)}) collective-permute-start(bf16[512,1024]{1,0:T(8,128)(2,1)S(1)} %fusion.70), channel_id=1, source_target_pairs={{0,1},{1,0},{2,3},{3,2},{4,5},{5,4},{6,7},{7,6},{8,9},{9,8},{10,11... | collective-permute-start | bytes 3145736 | tf_op jit(solution)/shard_map/ppermute | solution.py:235
  189.7 20.5 %collective-permute-start.12 = (bf16[1024,1024]{1,0:T(8,128)(2,1)S(1)}, bf16[1024,1024]{1,0:T(8,128)(2,1)S(1)}, u32[]{:S(2)}, u32[]{:S(2)}) collective-permute-start(bf16[1024,1024]{1,0:T(8,128)(2,1)S(1)} %broadcast_select_fusion.3), channel_id=1, source_target_pairs={{0,16},{16,0},{1,17},{17,1},{2,18},{18,2},{3,19},{19,3},{4,20},{20... | collective-permute-start | bytes 6291464 | tf_op jit(solution)/shard_map/ppermute | solution.py:231
  196.0 15.9 %collective-permute-start.13 = (bf16[512,2048]{1,0:T(8,128)(2,1)S(1)}, bf16[512,2048]{1,0:T(8,128)(2,1)S(1)}, u32[]{:S(2)}, u32[]{:S(2)}) collective-permute-start(bf16[512,2048]{1,0:T(8,128)(2,1)S(1)} %broadcast_select_fusion.1), channel_id=1, source_target_pairs={{0,16},{16,0},{1,17},{17,1},{2,18},{18,2},{3,19},{19,3},{4,20},{20... | collective-permute-start | bytes 6291464 | tf_op jit(solution)/shard_map/ppermute | solution.py:231
  213.6 369.9 %all-reduce.4.cloned.1.call-start = ((), (), s32[]{:S(2)}) async-start(), calls=%async_computation | async-start | bytes 4194304 | tf_op jit(solution)/shard_map/psum | solution.py:405
  228.2 20.6 %collective-permute-start.14 = (bf16[512,1024]{1,0:T(8,128)(2,1)S(1)}, bf16[512,1024]{1,0:T(8,128)(2,1)S(1)}, u32[]{:S(2)}, u32[]{:S(2)}) collective-permute-start(bf16[512,1024]{1,0:T(8,128)(2,1)S(1)} %add_convert_fusion.6), channel_id=1, source_target_pairs={{0,1},{1,0},{2,3},{3,2},{4,5},{5,4},{6,7},{7,6},{8,9},{9,8},{10,11... | collective-permute-start | bytes 3145736 | tf_op jit(solution)/shard_map/ppermute | solution.py:235
  234.2 44.0 %collective-permute-start.66 = (bf16[2,1024,512]{2,1,0:T(8,128)(2,1)S(1)}, bf16[2,1024,512]{2,1,0:T(8,128)(2,1)S(1)}, u32[]{:S(2)}, u32[]{:S(2)}) collective-permute-start(bf16[2,1024,512]{2,1,0:T(8,128)(2,1)S(1)} %broadcast_select_fusion.4), channel_id=1, source_target_pairs={{0,16},{16,0},{1,17},{17,1},{2,18},{18,2},{3,19},{19,3},{4,20},{20... | collective-permute-start | bytes 6291464 | tf_op jit(solution)/shard_map/ppermute | solution.py:231
  249.9 29.9 %collective-permute-start.18 = (bf16[512,1024]{1,0:T(8,128)(2,1)}, bf16[512,1024]{1,0:T(8,128)(2,1)}, u32[]{:S(2)}, u32[]{:S(2)}) collective-permute-start(bf16[512,1024]{1,0:T(8,128)(2,1)} %convolution_convert_fusion.9), channel_id=1, source_target_pairs={{0,1},{1,0},{2,3},{3,2},{4,5},{5,4},{6,7},{7,6},{8,9},{9,8},{10,11... | collective-permute-start | bytes 3145736 | tf_op jit(solution)/shard_map/ppermute | solution.py:235
  260.9 40.1 %collective-permute-start.17 = (bf16[512,1024]{1,0:T(8,128)(2,1)}, bf16[512,1024]{1,0:T(8,128)(2,1)}, u32[]{:S(2)}, u32[]{:S(2)}) collective-permute-start(bf16[512,1024]{1,0:T(8,128)(2,1)} %fusion.61), channel_id=1, source_target_pairs={{0,1},{1,0},{2,3},{3,2},{4,5},{5,4},{6,7},{7,6},{8,9},{9,8},{10,11... | collective-permute-start | bytes 3145736 | tf_op jit(solution)/shard_map/ppermute | solution.py:235
  266.9 76.6 %collective-permute-start.15 = (bf16[1024,1024]{1,0:T(8,128)(2,1)}, bf16[1024,1024]{1,0:T(8,128)(2,1)}, u32[]{:S(2)}, u32[]{:S(2)}) collective-permute-start(bf16[1024,1024]{1,0:T(8,128)(2,1)} %broadcast_select_fusion.2), channel_id=1, source_target_pairs={{0,16},{16,0},{1,17},{17,1},{2,18},{18,2},{3,19},{19,3},{4,20},{20... | collective-permute-start | bytes 6291464 | tf_op jit(solution)/shard_map/ppermute | solution.py:231
  277.6 61.2 %collective-permute-start.16 = (bf16[512,2048]{1,0:T(8,128)(2,1)}, bf16[512,2048]{1,0:T(8,128)(2,1)}, u32[]{:S(2)}, u32[]{:S(2)}) collective-permute-start(bf16[512,2048]{1,0:T(8,128)(2,1)} %broadcast_select_fusion), channel_id=1, source_target_pairs={{0,16},{16,0},{1,17},{17,1},{2,18},{18,2},{3,19},{19,3},{4,20},{20... | collective-permute-start | bytes 6291464 | tf_op jit(solution)/shard_map/ppermute | solution.py:231
  324.1 26.0 %collective-permute-start.20 = (bf16[1024,512]{1,0:T(8,128)(2,1)}, bf16[1024,512]{1,0:T(8,128)(2,1)}, u32[]{:S(2)}, u32[]{:S(2)}) collective-permute-start(bf16[1024,512]{1,0:T(8,128)(2,1)} %convolution_convert_fusion.7), channel_id=1, source_target_pairs={{0,16},{16,0},{1,17},{17,1},{2,18},{18,2},{3,19},{19,3},{4,20},{20... | collective-permute-start | bytes 3145736 | tf_op jit(solution)/shard_map/ppermute | solution.py:231
  327.8 26.8 %collective-permute-start.19 = (bf16[1024,512]{1,0:T(8,128)(2,1)}, bf16[1024,512]{1,0:T(8,128)(2,1)}, u32[]{:S(2)}, u32[]{:S(2)}) collective-permute-start(bf16[1024,512]{1,0:T(8,128)(2,1)} %convolution_convert_fusion.8), channel_id=1, source_target_pairs={{0,16},{16,0},{1,17},{17,1},{2,18},{18,2},{3,19},{19,3},{4,20},{20... | collective-permute-start | bytes 3145736 | tf_op jit(solution)/shard_map/ppermute | solution.py:231
  329.5 17.4 %collective-permute-start.22 = (bf16[512,1024]{1,0:T(8,128)(2,1)}, bf16[512,1024]{1,0:T(8,128)(2,1)}, u32[]{:S(2)}, u32[]{:S(2)}) collective-permute-start(bf16[512,1024]{1,0:T(8,128)(2,1)} %convolution_convert_fusion.5), channel_id=1, source_target_pairs={{0,16},{16,0},{1,17},{17,1},{2,18},{18,2},{3,19},{19,3},{4,20},{20... | collective-permute-start | bytes 3145736 | tf_op jit(solution)/shard_map/ppermute | solution.py:231
  338.8 19.3 %collective-permute-start.21 = (bf16[1024,512]{1,0:T(8,128)(2,1)}, bf16[1024,512]{1,0:T(8,128)(2,1)S(1)}, u32[]{:S(2)}, u32[]{:S(2)}) collective-permute-start(bf16[1024,512]{1,0:T(8,128)(2,1)} %convolution_convert_fusion.6), channel_id=1, source_target_pairs={{0,16},{16,0},{1,17},{17,1},{2,18},{18,2},{3,19},{19,3},{4,20},{20... | collective-permute-start | bytes 3145736 | tf_op jit(solution)/shard_map/ppermute | solution.py:231
  374.1 84.3 %collective-permute-start.23 = (bf16[3,512,512]{2,1,0:T(8,128)(2,1)}, bf16[3,512,512]{2,1,0:T(8,128)(2,1)}, u32[]{:S(2)}, u32[]{:S(2)}) collective-permute-start(bf16[3,512,512]{2,1,0:T(8,128)(2,1)} %pad_maximum_fusion.7), channel_id=1, source_target_pairs={{0,1},{1,0},{2,3},{3,2},{4,5},{5,4},{6,7},{7,6},{8,9},{9,8},{10,11... | collective-permute-start | bytes 4718600 | tf_op jit(solution)/shard_map/ppermute | solution.py:235
  374.9 82.0 %collective-permute-start.24 = (f32[8,128]{1,0:T(8,128)S(1)}, f32[8,128]{1,0:T(8,128)S(1)}, u32[]{:S(2)}, u32[]{:S(2)}) collective-permute-start(f32[8,128]{1,0:T(8,128)S(1)} %reshape.758), channel_id=1, source_target_pairs={{0,1},{1,0},{2,3},{3,2},{4,5},{5,4},{6,7},{7,6},{8,9},{9,8},{10,11... | collective-permute-start | bytes 12296 | tf_op jit(solution)/shard_map/ppermute | solution.py:235
  421.7 15.2 %collective-permute-start.36 = (bf16[64,2048]{1,0:T(8,128)(2,1)S(1)}, bf16[64,2048]{1,0:T(8,128)(2,1)S(1)}, u32[]{:S(2)}, u32[]{:S(2)}) collective-permute-start(bf16[64,2048]{1,0:T(8,128)(2,1)S(1)} %bitcast_add_fusion.19), channel_id=1, source_target_pairs={{0,2},{4,0},{8,4},{12,8},{14,12},{10,14},{6,10},{2,6},{1,3},{5,1},... | collective-permute-start | bytes 786440 | tf_op jit(solution)/shard_map/ppermute | solution.py:421
  422.9 31.5 %collective-permute-start.56 = (bf16[256,512]{1,0:T(8,128)(2,1)S(1)}, bf16[256,512]{1,0:T(8,128)(2,1)S(1)}, u32[]{:S(2)}, u32[]{:S(2)}) collective-permute-start(bf16[256,512]{1,0:T(8,128)(2,1)S(1)} %bitcast_add_fusion.6), channel_id=1, source_target_pairs={{0,2},{4,0},{8,4},{12,8},{14,12},{10,14},{6,10},{2,6},{1,3},{5,1},... | collective-permute-start | bytes 786440 | tf_op jit(solution)/shard_map/ppermute | solution.py:421
  425.7 30.4 %collective-permute-start.42 = (bf16[256,512]{1,0:T(8,128)(2,1)S(1)}, bf16[256,512]{1,0:T(8,128)(2,1)S(1)}, u32[]{:S(2)}, u32[]{:S(2)}) collective-permute-start(bf16[256,512]{1,0:T(8,128)(2,1)S(1)} %bitcast_add_fusion.13), channel_id=1, source_target_pairs={{0,4},{4,8},{8,12},{12,14},{14,10},{10,6},{6,2},{2,0},{1,5},{5,9},... | collective-permute-start | bytes 786440 | tf_op jit(solution)/shard_map/ppermute | solution.py:421
  436.9 41.5 %collective-permute-start.34 = (bf16[128,1024]{1,0:T(8,128)(2,1)}, bf16[128,1024]{1,0:T(8,128)(2,1)}, u32[]{:S(2)}, u32[]{:S(2)}) collective-permute-start(bf16[128,1024]{1,0:T(8,128)(2,1)} %bitcast_add_fusion.21), channel_id=1, source_target_pairs={{0,4},{4,8},{8,12},{12,14},{14,10},{10,6},{6,2},{2,0},{1,5},{5,9},... | collective-permute-start | bytes 786440 | tf_op jit(solution)/shard_map/ppermute | solution.py:421
  454.5 26.7 %collective-permute-start.37 = (bf16[64,2048]{1,0:T(8,128)(2,1)S(1)}, bf16[64,2048]{1,0:T(8,128)(2,1)}, u32[]{:S(2)}, u32[]{:S(2)}) collective-permute-start(bf16[64,2048]{1,0:T(8,128)(2,1)S(1)} %bitcast_add_fusion.18), channel_id=1, source_target_pairs={{0,2},{4,0},{8,4},{12,8},{14,12},{10,14},{6,10},{2,6},{1,3},{5,1},... | collective-permute-start | bytes 786440 | tf_op jit(solution)/shard_map/ppermute | solution.py:421
  456.2 18.3 %collective-permute-start.57 = (bf16[256,512]{1,0:T(8,128)(2,1)}, bf16[256,512]{1,0:T(8,128)(2,1)}, u32[]{:S(2)}, u32[]{:S(2)}) collective-permute-start(bf16[256,512]{1,0:T(8,128)(2,1)} %bitcast_add_fusion.5), channel_id=1, source_target_pairs={{0,2},{4,0},{8,4},{12,8},{14,12},{10,14},{6,10},{2,6},{1,3},{5,1},... | collective-permute-start | bytes 786440 | tf_op jit(solution)/shard_map/ppermute | solution.py:421
  456.9 18.6 %collective-permute-start.43 = (bf16[256,512]{1,0:T(8,128)(2,1)}, bf16[256,512]{1,0:T(8,128)(2,1)}, u32[]{:S(2)}, u32[]{:S(2)}) collective-permute-start(bf16[256,512]{1,0:T(8,128)(2,1)} %bitcast_add_fusion.12), channel_id=1, source_target_pairs={{0,4},{4,8},{8,12},{12,14},{14,10},{10,6},{6,2},{2,0},{1,5},{5,9},... | collective-permute-start | bytes 786440 | tf_op jit(solution)/shard_map/ppermute | solution.py:421
  466.0 137.3 %collective-permute-start.31 = (f32[2,512,512]{2,1,0:T(8,128)}, f32[2,512,512]{2,1,0:T(8,128)}, u32[]{:S(2)}, u32[]{:S(2)}) collective-permute-start(f32[2,512,512]{2,1,0:T(8,128)} %get-tuple-element.219), channel_id=1, source_target_pairs={{0,16},{16,0},{1,17},{17,1},{2,18},{18,2},{3,19},{19,3},{4,20},{20... | collective-permute-start | bytes 6291464 | tf_op jit(solution)/shard_map/ppermute | solution.py:231
  476.5 16.7 %collective-permute-start.44 = (bf16[256,512]{1,0:T(8,128)(2,1)S(1)}, bf16[256,512]{1,0:T(8,128)(2,1)S(1)}, u32[]{:S(2)}, u32[]{:S(2)}) collective-permute-start(bf16[256,512]{1,0:T(8,128)(2,1)S(1)} %bitcast_add_fusion.11), channel_id=1, source_target_pairs={{0,4},{4,8},{8,12},{12,14},{14,10},{10,6},{6,2},{2,0},{1,5},{5,9},... | collective-permute-start | bytes 786440 | tf_op jit(solution)/shard_map/ppermute | solution.py:421
  479.5 15.3 %collective-permute-start.67 = (bf16[128,1024]{1,0:T(8,128)(2,1)S(1)}, bf16[128,1024]{1,0:T(8,128)(2,1)S(1)}, u32[]{:S(2)}, u32[]{:S(2)}) collective-permute-start(bf16[128,1024]{1,0:T(8,128)(2,1)S(1)} %bitcast_add_fusion.20), channel_id=1, source_target_pairs={{0,4},{4,8},{8,12},{12,14},{14,10},{10,6},{6,2},{2,0},{1,5},{5,9},... | collective-permute-start | bytes 786440 | tf_op jit(solution)/shard_map/ppermute | solution.py:421
  493.1 20.6 %collective-permute-start.59 = (bf16[256,512]{1,0:T(8,128)(2,1)S(1)}, bf16[256,512]{1,0:T(8,128)(2,1)S(1)}, u32[]{:S(2)}, u32[]{:S(2)}) collective-permute-start(bf16[256,512]{1,0:T(8,128)(2,1)S(1)} %bitcast_add_fusion.3), channel_id=1, source_target_pairs={{0,2},{4,0},{8,4},{12,8},{14,12},{10,14},{6,10},{2,6},{1,3},{5,1},... | collective-permute-start | bytes 786440 | tf_op jit(solution)/shard_map/ppermute | solution.py:421
  493.2 21.3 %collective-permute-start.45 = (bf16[256,512]{1,0:T(8,128)(2,1)S(1)}, bf16[256,512]{1,0:T(8,128)(2,1)S(1)}, u32[]{:S(2)}, u32[]{:S(2)}) collective-permute-start(bf16[256,512]{1,0:T(8,128)(2,1)S(1)} %bitcast_add_fusion.10), channel_id=1, source_target_pairs={{0,4},{4,8},{8,12},{12,14},{14,10},{10,6},{6,2},{2,0},{1,5},{5,9},... | collective-permute-start | bytes 786440 | tf_op jit(solution)/shard_map/ppermute | solution.py:421
  494.8 16.9 %collective-permute-start.74 = (bf16[64,2048]{1,0:T(8,128)(2,1)S(1)}, bf16[64,2048]{1,0:T(8,128)(2,1)S(1)}, u32[]{:S(2)}, u32[]{:S(2)}) collective-permute-start(bf16[64,2048]{1,0:T(8,128)(2,1)S(1)} %bitcast_add_fusion.1), channel_id=1, source_target_pairs={{0,2},{4,0},{8,4},{12,8},{14,12},{10,14},{6,10},{2,6},{1,3},{5,1},... | collective-permute-start | bytes 786440 | tf_op jit(solution)/shard_map/ppermute | solution.py:421
  513.7 16.4 %collective-permute-start.75 = (bf16[64,2048]{1,0:T(8,128)(2,1)S(1)}, bf16[64,2048]{1,0:T(8,128)(2,1)S(1)}, u32[]{:S(2)}, u32[]{:S(2)}) collective-permute-start(bf16[64,2048]{1,0:T(8,128)(2,1)S(1)} %collective-permute-done.74), channel_id=1, source_target_pairs={{0,2},{4,0},{8,4},{12,8},{14,12},{10,14},{6,10},{2,6},{1,3},{5,1},... | collective-permute-start | bytes 786440 | tf_op jit(solution)/shard_map/ppermute | solution.py:421
  514.5 31.2 %collective-permute-start.60 = (bf16[256,512]{1,0:T(8,128)(2,1)S(1)}, bf16[256,512]{1,0:T(8,128)(2,1)S(1)}, u32[]{:S(2)}, u32[]{:S(2)}) collective-permute-start(bf16[256,512]{1,0:T(8,128)(2,1)S(1)} %collective-permute-done.59), channel_id=1, source_target_pairs={{0,2},{4,0},{8,4},{12,8},{14,12},{10,14},{6,10},{2,6},{1,3},{5,1},... | collective-permute-start | bytes 786440 | tf_op jit(solution)/shard_map/ppermute | solution.py:421
  516.1 29.7 %collective-permute-start.46 = (bf16[256,512]{1,0:T(8,128)(2,1)S(1)}, bf16[256,512]{1,0:T(8,128)(2,1)S(1)}, u32[]{:S(2)}, u32[]{:S(2)}) collective-permute-start(bf16[256,512]{1,0:T(8,128)(2,1)S(1)} %collective-permute-done.45), channel_id=1, source_target_pairs={{0,4},{4,8},{8,12},{12,14},{14,10},{10,6},{6,2},{2,0},{1,5},{5,9},... | collective-permute-start | bytes 786440 | tf_op jit(solution)/shard_map/ppermute | solution.py:421
  530.2 50.2 %collective-permute-start.88 = (f32[14,128]{1,0:T(8,128)S(1)}, f32[14,128]{1,0:T(8,128)S(1)}, u32[]{:S(2)}, u32[]{:S(2)}) collective-permute-start(f32[14,128]{1,0:T(8,128)S(1)} %fusion.217), channel_id=1, source_target_pairs={{0,8},{4,12},{8,0},{12,4},{1,9},{5,13},{9,1},{13,5},{2,10},{6,14},... | collective-permute-start | bytes 21512 | tf_op jit(solution)/shard_map/ppermute | solution.py:413
  530.2 32.2 %collective-permute-start.76 = (bf16[64,2048]{1,0:T(8,128)(2,1)S(1)}, bf16[64,2048]{1,0:T(8,128)(2,1)S(1)}, u32[]{:S(2)}, u32[]{:S(2)}) collective-permute-start(bf16[64,2048]{1,0:T(8,128)(2,1)S(1)} %collective-permute-done.75), channel_id=1, source_target_pairs={{0,2},{4,0},{8,4},{12,8},{14,12},{10,14},{6,10},{2,6},{1,3},{5,1},... | collective-permute-start | bytes 786440 | tf_op jit(solution)/shard_map/ppermute | solution.py:421
  545.8 16.7 %collective-permute-start.47 = (bf16[256,512]{1,0:T(8,128)(2,1)S(1)}, bf16[256,512]{1,0:T(8,128)(2,1)S(1)}, u32[]{:S(2)}, u32[]{:S(2)}) collective-permute-start(bf16[256,512]{1,0:T(8,128)(2,1)S(1)} %collective-permute-done.46), channel_id=1, source_target_pairs={{0,4},{4,8},{8,12},{12,14},{14,10},{10,6},{6,2},{2,0},{1,5},{5,9},... | collective-permute-start | bytes 786440 | tf_op jit(solution)/shard_map/ppermute | solution.py:421
  597.3 20.2 %collective-permute-start.65 = (bf16[256,512]{1,0:T(8,128)(2,1)S(1)}, bf16[256,512]{1,0:T(8,128)(2,1)S(1)}, u32[]{:S(2)}, u32[]{:S(2)}) collective-permute-start(bf16[256,512]{1,0:T(8,128)(2,1)S(1)} %collective-permute-done.64), channel_id=1, source_target_pairs={{0,2},{4,0},{8,4},{12,8},{14,12},{10,14},{6,10},{2,6},{1,3},{5,1},... | collective-permute-start | bytes 786440 | tf_op jit(solution)/shard_map/ppermute | solution.py:421
  600.0 19.3 %collective-permute-start.51 = (bf16[256,512]{1,0:T(8,128)(2,1)S(1)}, bf16[256,512]{1,0:T(8,128)(2,1)S(1)}, u32[]{:S(2)}, u32[]{:S(2)}) collective-permute-start(bf16[256,512]{1,0:T(8,128)(2,1)S(1)} %collective-permute-done.50), channel_id=1, source_target_pairs={{0,4},{4,8},{8,12},{12,14},{14,10},{10,6},{6,2},{2,0},{1,5},{5,9},... | collective-permute-start | bytes 786440 | tf_op jit(solution)/shard_map/ppermute | solution.py:421
  (199 other events, 1725.9 us)
Sparse Core Ops, SparseCore 0:
  9.6 19.2 all-gather.10
  30.4 11.7 all-gather.12
  43.7 21.0 all-gather.14
  66.1 21.0 all-gather.16
  89.2 14.8 all-gather.18
  213.7 161.0 all-reduce.5
  414.2 138.9 all-reduce.3
